TPU v7x, 128 devices: a whole 4x4x4 slice. The times are simulated.
128 devices in a mesh: rep: 4 (over y_lo, core), fsdp: 32 (over y_hi, x, z).
Axes of the slice: x: 4, y: 4 (y_hi: 2, y_lo: 2; y = y_hi * 2 + y_lo), z: 4, core: 2. Of those that a mesh axis runs over, the one named last changes fastest.
Arguments:
- tokens: bfloat16 [2, 128, 128, 1024], P(None, ('rep', 'fsdp')), may hold values from -6 to 6
- segments: int32 [2, 128, 128], P(None, ('rep', 'fsdp')), may hold values from 0 to 31, never falling along the last dimension, each value on 1 to 64 neighbouring positions
- routes: int32 [2, 128, 128, 8], P(None, ('rep', 'fsdp')), may hold values from 0 to 31, all different within a row; in each aligned block of 128 rows (0 to 127, 128 to 255, ..., all dimensions but the last counted through in order) at most 48 rows name the same one
- cotangent: bfloat16 [2, 128, 128, 1024], P(None, ('rep', 'fsdp')), may hold values from -6 to 6
- attn_gain: bfloat16 [1024], P('fsdp'), may hold values from 0.5 to 1.5
- moe_gain: bfloat16 [1024], P('fsdp'), may hold values from 0.5 to 1.5
- w_query: bfloat16 [1024, 1024], P('fsdp'), may hold values from -0.75 to 0.75
- w_key: bfloat16 [1024, 512], P('fsdp'), may hold values from -0.75 to 0.75
- w_value: bfloat16 [1024, 512], P('fsdp'), may hold values from -0.1875 to 0.1875
- w_output: bfloat16 [1024, 1024], P('fsdp'), may hold values from -1.5 to 1.5
- w_router: bfloat16 [1024, 32], P('fsdp'), may hold values from -0.09375 to 0.09375
- w_gate: bfloat16 [32, 1024, 512], P('fsdp'), may hold values from -0.1875 to 0.1875
- w_up: bfloat16 [32, 1024, 512], P('fsdp'), may hold values from -0.1875 to 0.1875
- w_down: bfloat16 [32, 512, 1024], P('fsdp'), may hold values from -6 to 6
Outputs:
- output: bfloat16 [2, 128, 128, 1024], P(None, ('rep', 'fsdp'))
- grad_tokens: float32 [2, 128, 128, 1024], P(None, ('rep', 'fsdp'))
- grad_attn_gain: float32 [1024], P('fsdp')
- grad_moe_gain: float32 [1024], P('fsdp')
- grad_query: float32 [1024, 1024], P('fsdp')
- grad_key: float32 [1024, 512], P('fsdp')
- grad_value: float32 [1024, 512], P('fsdp')
- grad_w_output: float32 [1024, 1024], P('fsdp')
- grad_router: float32 [1024, 32], P('fsdp')
- grad_gate: float32 [32, 1024, 512], P('fsdp')
- grad_up: float32 [32, 1024, 512], P('fsdp')
- grad_down: float32 [32, 512, 1024], P('fsdp')
Inputs may be any that keep to these rules, and one draw needn't show every extreme that they name: `segments`: within a sequence segment numbers never fall; every segment has 1 to 64 tokens and some segment has exactly 64. `routes`: A token's 8 experts differ. Within one sequence no expert is named by more than 48 tokens, and in every draw some sequence names some expert exactly 48 times.
All inputs are finite; a program needn't handle non-finite values.
Results may differ from a plain program's by a relative error of at most 0.018.
Values may be sent and summed in bfloat16 or wider, within the bound.
A program may use at most 192 MiB of HBM per device.

v0:
```python
import math

import jax
import jax.numpy as jnp
from jax import lax
from jax.sharding import PartitionSpec as P

D = 1024
HEADS = 16
KV_HEADS = 8
HEAD_DIM = 64
EXPERTS = 32
TOPK = 8
CAP = 48


EPS = 1e-06
RESIDUAL = 0.22
ATT_SCALE = 0.015625
ROPE_BASE = 10000.0
NEG = -1000000000.0


def phases(segment):
    length = segment.shape[0]
    places = jnp.arange(length, dtype=jnp.int32)
    starts = jnp.concatenate([jnp.ones((1,), dtype=bool), segment[1:] != segment[:-1]])
    opening = lax.cummax(jnp.where(starts, places, 0), axis=0)
    offset = (places - opening).astype(jnp.float32)
    halves = HEAD_DIM // 2
    frequency = jnp.exp(
        -math.log(ROPE_BASE) * 2.0 * jnp.arange(halves).astype(jnp.float32) / HEAD_DIM
    )
    angles = offset[:, None] * frequency[None, :]
    angles = jnp.concatenate([angles, angles], axis=1)[:, None, :]
    visible = (places[None, :] <= places[:, None]) & (segment[:, None] == segment[None, :])
    return (jnp.cos(angles), jnp.sin(angles), visible)


def rotate(values, cos_table, sin_table):
    height = values.shape[0]
    per_head = values.reshape(height, -1, HEAD_DIM)
    halves = HEAD_DIM // 2
    turned = jnp.concatenate([-per_head[..., halves:], per_head[..., :halves]], axis=-1)
    return (per_head * cos_table + turned * sin_table).reshape(height, -1)


def slot_index(route_ids):
    flat_routes = route_ids.reshape(-1)
    choose = (flat_routes[:, None] == jnp.arange(EXPERTS, dtype=jnp.int32)[None, :]).astype(
        jnp.int32
    )
    before = jnp.cumsum(choose, axis=0) - choose
    slots = jnp.sum(before * choose, axis=1)
    return flat_routes * CAP + slots


def normalize(values, gain):
    scale = lax.rsqrt(jnp.mean(values * values, axis=-1, keepdims=True) + EPS)
    normed = values * scale
    return (normed, scale, normed * gain)


def normalize_back(grad_out, normed, scale, gain):
    grad_norm = grad_out * gain
    grad_in = scale * (grad_norm - normed * jnp.mean(grad_norm * normed, axis=-1, keepdims=True))
    return (grad_in, jnp.sum(grad_out * normed, axis=0))


def scores_of(query_low, key_low, visible):
    height = query_low.shape[0]
    query_four = query_low.reshape(height, KV_HEADS, HEADS // KV_HEADS, HEAD_DIM)
    key_three = key_low.reshape(height, KV_HEADS, HEAD_DIM)
    scores = (
        jnp.einsum("qkgd,skd->kgqs", query_four, key_three, preferred_element_type=jnp.float32)
        * ATT_SCALE
    )
    return jnp.where(visible[None, None], scores, NEG)


def attend(query_low, key_low, value_low, visible):
    height = query_low.shape[0]
    scores = scores_of(query_low, key_low, visible)
    highest = jnp.max(scores, axis=-1, keepdims=True)
    log_total = highest + jnp.log(jnp.sum(jnp.exp(scores - highest), axis=-1, keepdims=True))
    attention = jnp.exp(scores - log_total).astype(jnp.bfloat16)
    value_three = value_low.reshape(height, KV_HEADS, HEAD_DIM)
    attended = jnp.einsum(
        "kgqs,skd->qkgd", attention, value_three, preferred_element_type=jnp.float32
    )
    return (attended.reshape(height, -1).astype(jnp.bfloat16), log_total)


def attend_back(query_low, key_low, value_low, visible, log_total, grad_mixed):
    height = query_low.shape[0]
    query_four = query_low.reshape(height, KV_HEADS, HEADS // KV_HEADS, HEAD_DIM)
    key_three = key_low.reshape(height, KV_HEADS, HEAD_DIM)
    value_three = value_low.reshape(height, KV_HEADS, HEAD_DIM)
    attention = jnp.exp(scores_of(query_low, key_low, visible) - log_total)
    attention_low = attention.astype(jnp.bfloat16)
    grad_four = grad_mixed.reshape(height, KV_HEADS, HEADS // KV_HEADS, HEAD_DIM)
    value_grad = jnp.einsum(
        "kgqs,qkgd->skd", attention_low, grad_four, preferred_element_type=jnp.float32
    )
    prob_grad = jnp.einsum(
        "qkgd,skd->kgqs", grad_four, value_three, preferred_element_type=jnp.float32
    )
    inner_prod = jnp.sum(attention * prob_grad, axis=-1, keepdims=True)
    score_grad = (attention * (prob_grad - inner_prod)).astype(jnp.bfloat16)
    query_grad = (
        jnp.einsum("kgqs,skd->qkgd", score_grad, key_three, preferred_element_type=jnp.float32)
        * ATT_SCALE
    )
    key_grad = (
        jnp.einsum("kgqs,qkgd->skd", score_grad, query_four, preferred_element_type=jnp.float32)
        * ATT_SCALE
    )
    return (
        query_grad.reshape(height, -1),
        key_grad.reshape(height, -1),
        value_grad.reshape(height, -1),
    )


def fetch_dense(attn_gain, moe_gain, w_query, w_key, w_value, w_output, w_router):
    return (
        lax.all_gather(attn_gain, "fsdp", axis=0, tiled=True),
        lax.all_gather(moe_gain, "fsdp", axis=0, tiled=True),
        lax.all_gather(w_query, "fsdp", axis=0, tiled=True),
        lax.all_gather(w_key, "fsdp", axis=0, tiled=True),
        lax.all_gather(w_value, "fsdp", axis=0, tiled=True),
        lax.all_gather(w_output, "fsdp", axis=0, tiled=True),
        lax.all_gather(w_router, "fsdp", axis=0, tiled=True),
    )


def reduce_dense(grads):
    return (
        lax.psum_scatter(grads[0], "fsdp", scatter_dimension=0, tiled=True),
        lax.psum_scatter(grads[1], "fsdp", scatter_dimension=0, tiled=True),
        lax.psum_scatter(grads[2], "fsdp", scatter_dimension=0, tiled=True),
        lax.psum_scatter(grads[3], "fsdp", scatter_dimension=0, tiled=True),
        lax.psum_scatter(grads[4], "fsdp", scatter_dimension=0, tiled=True),
        lax.psum_scatter(grads[5], "fsdp", scatter_dimension=0, tiled=True),
        lax.psum_scatter(grads[6], "fsdp", scatter_dimension=0, tiled=True),
    )


def combine_sum(current, update):
    return current + update


def on_device(
    tokens,
    segments,
    routes,
    cotangent,
    attn_gain,
    moe_gain,
    w_query,
    w_key,
    w_value,
    w_output,
    w_router,
    w_gate,
    w_up,
    w_down,
):
    micro = tokens.shape[0]
    length = tokens.shape[2]
    groups = lax.axis_size("fsdp")
    local_experts = w_gate.shape[0]
    shards = (attn_gain, moe_gain, w_query, w_key, w_value, w_output, w_router)
    totals = tuple((jnp.zeros(member.shape, jnp.float32) for member in shards))
    grad_gate = jnp.zeros(w_gate.shape, jnp.float32)
    grad_up = jnp.zeros(w_up.shape, jnp.float32)
    grad_down = jnp.zeros(w_down.shape, jnp.float32)
    outputs = []
    grads_in = []
    expert_ids = jnp.arange(EXPERTS, dtype=jnp.int32)
    for number in range(micro):
        dense_set = fetch_dense(attn_gain, moe_gain, w_query, w_key, w_value, w_output, w_router)
        gain_one = dense_set[0].astype(jnp.float32)
        gain_two = dense_set[1].astype(jnp.float32)
        inputs = tokens[number, 0].astype(jnp.float32)
        segment = segments[number, 0]
        route_ids = routes[number, 0]
        cos_table, sin_table, visible = phases(segment)
        normed_one, scale_one, hidden_one = normalize(inputs, gain_one)
        hidden_low = hidden_one.astype(jnp.bfloat16)
        query_raw = jnp.dot(hidden_low, dense_set[2], preferred_element_type=jnp.float32)
        key_raw = jnp.dot(hidden_low, dense_set[3], preferred_element_type=jnp.float32)
        value_low = jnp.dot(hidden_low, dense_set[4], preferred_element_type=jnp.float32).astype(
            jnp.bfloat16
        )
        query_low = rotate(query_raw, cos_table, sin_table).astype(jnp.bfloat16)
        key_low = rotate(key_raw, cos_table, sin_table).astype(jnp.bfloat16)
        mixed_low, log_total = attend(query_low, key_low, value_low, visible)
        branch = jnp.dot(mixed_low, dense_set[5], preferred_element_type=jnp.float32)
        middle = inputs + RESIDUAL * branch
        normed_two, scale_two, hidden_two = normalize(middle, gain_two)
        routed_low = hidden_two.astype(jnp.bfloat16)
        logits = jnp.dot(routed_low, dense_set[6], preferred_element_type=jnp.float32)
        choose = (route_ids[:, :, None] == expert_ids[None, None, :]).astype(jnp.float32)
        chosen = jnp.einsum("tke,te->tk", choose, logits)
        gate_weights = jax.nn.softmax(chosen, axis=-1)
        places = slot_index(route_ids)
        copies = jnp.repeat(routed_low, TOPK, axis=0)
        outgoing = (
            jnp.zeros((EXPERTS * CAP, D), jnp.bfloat16)
            .at[places]
            .set(copies)
            .reshape(EXPERTS, CAP, D)
        )
        arrived = lax.all_to_all(outgoing, "fsdp", split_axis=0, concat_axis=0, tiled=True).reshape(
            groups, local_experts, CAP, D
        )
        gate_act = jnp.einsum("secd,edf->secf", arrived, w_gate, preferred_element_type=jnp.float32)
        up_act = jnp.einsum("secd,edf->secf", arrived, w_up, preferred_element_type=jnp.float32)
        sigmoid_act = jax.nn.sigmoid(gate_act)
        swish_act = gate_act * sigmoid_act
        inner_low = (swish_act * up_act).astype(jnp.bfloat16)
        expert_out = jnp.einsum(
            "secf,efd->secd", inner_low, w_down, preferred_element_type=jnp.float32
        ).astype(jnp.bfloat16)
        returned = lax.all_to_all(
            expert_out.reshape(groups * local_experts, CAP, D),
            "fsdp",
            split_axis=0,
            concat_axis=0,
            tiled=True,
        ).reshape(EXPERTS * CAP, D)
        picked = returned[places].reshape(length, TOPK, D)
        mixture = jnp.sum(gate_weights[:, :, None] * picked, axis=1)
        result = middle + RESIDUAL * mixture
        outputs.append(result.astype(jnp.bfloat16))
        dense_set = fetch_dense(attn_gain, moe_gain, w_query, w_key, w_value, w_output, w_router)
        upstream = cotangent[number, 0].astype(jnp.float32)
        grad_mix = RESIDUAL * upstream
        gate_grad = jnp.sum(picked * grad_mix[:, None, :], axis=-1)
        slot_grad = (
            (gate_weights[:, :, None] * grad_mix[:, None, :])
            .astype(jnp.bfloat16)
            .reshape(length * TOPK, D)
        )
        sending = (
            jnp.zeros((EXPERTS * CAP, D), jnp.bfloat16)
            .at[places]
            .set(slot_grad)
            .reshape(EXPERTS, CAP, D)
        )
        arrived_grad = lax.all_to_all(
            sending, "fsdp", split_axis=0, concat_axis=0, tiled=True
        ).reshape(groups, local_experts, CAP, D)
        inner_grad = jnp.einsum(
            "secd,efd->secf", arrived_grad, w_down, preferred_element_type=jnp.float32
        )
        grad_down = grad_down + jnp.einsum(
            "secf,secd->efd", inner_low, arrived_grad, preferred_element_type=jnp.float32
        )
        gate_pre = (
            inner_grad * up_act * sigmoid_act * (1.0 + gate_act * (1.0 - sigmoid_act))
        ).astype(jnp.bfloat16)
        up_pre = (inner_grad * swish_act).astype(jnp.bfloat16)
        grad_gate = grad_gate + jnp.einsum(
            "secd,secf->edf", arrived, gate_pre, preferred_element_type=jnp.float32
        )
        grad_up = grad_up + jnp.einsum(
            "secd,secf->edf", arrived, up_pre, preferred_element_type=jnp.float32
        )
        feature_grad = jnp.einsum(
            "secf,edf->secd", gate_pre, w_gate, preferred_element_type=jnp.float32
        )
        feature_grad = feature_grad + jnp.einsum(
            "secf,edf->secd", up_pre, w_up, preferred_element_type=jnp.float32
        )
        back_rows = lax.all_to_all(
            feature_grad.astype(jnp.bfloat16).reshape(groups * local_experts, CAP, D),
            "fsdp",
            split_axis=0,
            concat_axis=0,
            tiled=True,
        ).reshape(EXPERTS * CAP, D)
        routed_grad = jnp.sum(
            back_rows[places].reshape(length, TOPK, D).astype(jnp.float32), axis=1
        )
        choice_grad = gate_weights * (
            gate_grad - jnp.sum(gate_weights * gate_grad, axis=-1, keepdims=True)
        )
        logit_grad = jnp.einsum("tke,tk->te", choose, choice_grad).astype(jnp.bfloat16)
        router_grad = jnp.einsum(
            "td,te->de", routed_low, logit_grad, preferred_element_type=jnp.float32
        )
        routed_grad = routed_grad + jnp.einsum(
            "te,de->td", logit_grad, dense_set[6], preferred_element_type=jnp.float32
        )
        middle_grad, gain_two_grad = normalize_back(routed_grad, normed_two, scale_two, gain_two)
        middle_grad = middle_grad + upstream
        branch_low = (RESIDUAL * middle_grad).astype(jnp.bfloat16)
        output_grad = jnp.einsum(
            "tf,td->fd", mixed_low, branch_low, preferred_element_type=jnp.float32
        )
        mixed_grad = jnp.einsum(
            "td,fd->tf", branch_low, dense_set[5], preferred_element_type=jnp.float32
        ).astype(jnp.bfloat16)
        query_grad, key_grad, value_grad = attend_back(
            query_low, key_low, value_low, visible, log_total, mixed_grad
        )
        query_low_grad = rotate(query_grad, cos_table, -sin_table).astype(jnp.bfloat16)
        key_low_grad = rotate(key_grad, cos_table, -sin_table).astype(jnp.bfloat16)
        value_low_grad = value_grad.astype(jnp.bfloat16)
        wq_grad = jnp.einsum(
            "td,tf->df", hidden_low, query_low_grad, preferred_element_type=jnp.float32
        )
        wk_grad = jnp.einsum(
            "td,tf->df", hidden_low, key_low_grad, preferred_element_type=jnp.float32
        )
        wv_grad = jnp.einsum(
            "td,tf->df", hidden_low, value_low_grad, preferred_element_type=jnp.float32
        )
        hidden_grad = jnp.einsum(
            "tf,df->td", query_low_grad, dense_set[2], preferred_element_type=jnp.float32
        )
        hidden_grad = hidden_grad + jnp.einsum(
            "tf,df->td", key_low_grad, dense_set[3], preferred_element_type=jnp.float32
        )
        hidden_grad = hidden_grad + jnp.einsum(
            "tf,df->td", value_low_grad, dense_set[4], preferred_element_type=jnp.float32
        )
        normed_grad, gain_one_grad = normalize_back(hidden_grad, normed_one, scale_one, gain_one)
        grads_in.append(middle_grad + normed_grad)
        dense_grads = (
            gain_one_grad,
            gain_two_grad,
            wq_grad,
            wk_grad,
            wv_grad,
            output_grad,
            router_grad,
        )
        reduced = reduce_dense(dense_grads)
        totals = tuple((combine_sum(current, update) for current, update in zip(totals, reduced)))
    summed = lax.psum(
        (
            totals[0],
            totals[1],
            totals[2],
            totals[3],
            totals[4],
            totals[5],
            totals[6],
            grad_gate,
            grad_up,
            grad_down,
        ),
        "rep",
    )
    return (
        jnp.stack(outputs)[:, None],
        jnp.stack(grads_in)[:, None],
        summed[0],
        summed[1],
        summed[2],
        summed[3],
        summed[4],
        summed[5],
        summed[6],
        summed[7],
        summed[8],
        summed[9],
    )


def solution(mesh):
    placed = (
        P(None, ("rep", "fsdp"), None, None),
        P(None, ("rep", "fsdp"), None),
        P(None, ("rep", "fsdp"), None, None),
        P(None, ("rep", "fsdp"), None, None),
        P("fsdp"),
        P("fsdp"),
        P("fsdp", None),
        P("fsdp", None),
        P("fsdp", None),
        P("fsdp", None),
        P("fsdp", None),
        P("fsdp", None, None),
        P("fsdp", None, None),
        P("fsdp", None, None),
    )
    return jax.shard_map(
        on_device,
        mesh=mesh,
        in_specs=placed,
        out_specs=(
            P(None, ("rep", "fsdp"), None, None),
            P(None, ("rep", "fsdp"), None, None),
            P("fsdp"),
            P("fsdp"),
            P("fsdp", None),
            P("fsdp", None),
            P("fsdp", None),
            P("fsdp", None),
            P("fsdp", None),
            P("fsdp", None, None),
            P("fsdp", None, None),
            P("fsdp", None, None),
        ),
        check_vma=False,
    )
```

profile of v0, /device:TPU:1, one launch (start us, length us, event | category | flops | bytes accessed | tf_op | source)
XLA Modules:
  0.0 1932.4 jit_solution(3319828074950691068)
XLA Ops:
  16.1 84.6 %all-reduce.7 = (bf16[1024]{0:T(1024)(128)(2,1)S(1)}, bf16[1024]{0:T(1024)(128)(2,1)S(1)}) all-reduce(bf16[1024]{0:T(1024)(128)(2,1)S(1)} %dynamic-update-slice, bf16[1024]{0:T(1024)(128)(2,1)S(1)} %dynamic-update-slice.1), channel_id=1, replica_groups=mesh['rep'=4,'fsdp'=32] {'fsdp'}, use_global_device_ids=true, to_apply=%add | all-reduce | flops 2048 | bytes 8192
  103.2 9.0 reduce-window.37
  117.0 28.5 %all-gather.7.cloned.1.call-done = bf16[1024,512]{1,0:T(8,128)(2,1)} async-done(((bf16[32,512]{1,0:T(8,128)(2,1)}), bf16[1024,512]{1,0:T(8,128)(2,1)}) %all-gather.7.cloned.1.call-update) | async-done | bytes 1048592 | tf_op jit(solution)/shard_map/all_gather | solution.py:130
  147.6 69.3 %all-gather.9.cloned.1.call-done = bf16[1024,1024]{1,0:T(8,128)(2,1)} async-done(((bf16[32,1024]{1,0:T(8,128)(2,1)}), bf16[1024,1024]{1,0:T(8,128)(2,1)}) %all-gather.9.cloned.1.call-update) | async-done | bytes 2097168 | tf_op jit(solution)/shard_map/all_gather | solution.py:129
  225.7 61.9 %all-gather.11.cloned.1.call-done = bf16[1024,1024]{1,0:T(8,128)(2,1)} async-done(((bf16[32,1024]{1,0:T(8,128)(2,1)}), bf16[1024,1024]{1,0:T(8,128)(2,1)}) %all-gather.11.cloned.1.call-update) | async-done | bytes 2097168 | tf_op jit(solution)/shard_map/all_gather | solution.py:132
  290.6 7.3 scatter_custom_fusion
  298.0 4.9 all-to-all-start
  303.7 107.3 %all_gather.20 = bf16[1024,32]{1,0:T(8,128)(2,1)S(1)} all-gather(bf16[32,32]{1,0:T(8,128)(2,1)S(1)} %copy-done.108), channel_id=1, replica_groups=mesh['rep'=4,'fsdp'=32] {'fsdp'}, dimensions={0}, use_global_device_ids=true | all-gather | bytes 67584 | tf_op jit(solution)/shard_map/all_gather | solution.py:133
  418.4 7.9 scatter_custom_fusion.2
  426.3 4.8 all-to-all-start.4
  432.0 5.6 fusion.72
  437.6 23.1 %all-to-all-done.4 = bf16[32,48,1024]{2,1,0:T(8,128)(2,1)} async-done(((bf16[32,48,1024]{2,1,0:T(8,128)(2,1)}), bf16[32,48,1024]{2,1,0:T(8,128)(2,1)}, u32[]{:S(2)}, u32[]{:S(2)}) %all-to-all-start.4) | async-done | bytes 3145760 | tf_op jit(solution)/shard_map/all_to_all | solution.py:252
  464.9 6.4 fusion.40
  476.0 13.0 all-to-all-start.1
  489.3 9.0 reduce-window.40
  510.8 13.0 all-to-all-done.1
  523.8 22.2 %all-to-all-start.5 = ((bf16[32,48,1024]{2,1,0:T(8,128)(2,1)}), bf16[32,48,1024]{2,1,0:T(8,128)(2,1)}, u32[]{:S(2)}, u32[]{:S(2)}) async-start(bf16[32,48,1024]{2,1,0:T(8,128)(2,1)} %add_convert_fusion.1), calls=%async_computation.5 | async-start | bytes 6291456 | tf_op jit(solution)/shard_map/all_to_all | solution.py:277
  552.4 7.3 gather_fusion
  563.9 18.4 all-to-all-done.5
  582.3 7.7 gather_fusion.2
  594.3 7.5 scatter_custom_fusion.1
  601.8 13.1 all-to-all-start.2
  616.5 7.9 scatter_custom_fusion.3
  624.4 30.1 %all-to-all-done.2 = bf16[32,48,1024]{2,1,0:T(8,128)(2,1)} async-done(((bf16[32,48,1024]{2,1,0:T(8,128)(2,1)}), bf16[32,48,1024]{2,1,0:T(8,128)(2,1)}, u32[]{:S(2)}, u32[]{:S(2)}) %all-to-all-start.2) | async-done | bytes 3145760 | tf_op jit(solution)/shard_map/all_to_all | solution.py:215
  654.5 10.5 all-to-all-start.6
  665.1 5.4 fusion.70
  670.5 34.6 %all-to-all-done.6 = bf16[32,48,1024]{2,1,0:T(8,128)(2,1)} async-done(((bf16[32,48,1024]{2,1,0:T(8,128)(2,1)}), bf16[32,48,1024]{2,1,0:T(8,128)(2,1)}, u32[]{:S(2)}, u32[]{:S(2)}) %all-to-all-start.6) | async-done | bytes 3145760 | tf_op jit(solution)/shard_map/all_to_all | solution.py:252
  709.0 6.3 fusion.42
  720.0 10.4 all-to-all-start.3
  737.3 33.3 %all-to-all-done.3 = bf16[32,48,1024]{2,1,0:T(8,128)(2,1)} async-done(((bf16[32,48,1024]{2,1,0:T(8,128)(2,1)}), bf16[32,48,1024]{2,1,0:T(8,128)(2,1)}, u32[]{:S(2)}, u32[]{:S(2)}) %all-to-all-start.3) | async-done | bytes 3145760 | tf_op jit(solution)/shard_map/all_to_all | solution.py:226
  770.7 10.6 all-to-all-start.7
  782.0 8.3 gather_fusion.1
  790.3 4.2 fusion.3
  795.2 27.0 %all-to-all-done.7 = bf16[32,48,1024]{2,1,0:T(8,128)(2,1)S(1)} async-done(((bf16[32,48,1024]{2,1,0:T(8,128)(2,1)}), bf16[32,48,1024]{2,1,0:T(8,128)(2,1)S(1)}, u32[]{:S(2)}, u32[]{:S(2)}) %all-to-all-start.7) | async-done | bytes 3145760 | tf_op jit(solution)/shard_map/all_to_all | solution.py:277
  822.2 5.6 gather_fusion.3
  863.9 4.3 fusion.225
  872.1 5.2 fusion.46
  877.6 5.2 fusion.28
  882.8 5.1 fusion.29
  889.2 6.2 fusion.30
  895.4 114.7 %reduce-scatter.10.cloned.1.call-done = f32[32,512]{1,0:T(8,128)} async-done(((f32[1024,512]{1,0:T(8,128)}), f32[32,512]{1,0:T(8,128)}) %reduce-scatter.10.cloned.1.call-update) | async-done | bytes 65552 | tf_op jit(solution)/shard_map/reduce_scatter | solution.py:143
  1010.2 184.8 %reduce-scatter.8.cloned.1.call-done = f32[32,512]{1,0:T(8,128)} async-done(((f32[1024,512]{1,0:T(8,128)}), f32[32,512]{1,0:T(8,128)}) %reduce-scatter.8.cloned.1.call-update) | async-done | bytes 65552 | tf_op jit(solution)/shard_map/reduce_scatter | solution.py:142
  1195.0 191.4 %reduce-scatter.12.cloned.1.call-done = f32[32,1024]{1,0:T(8,128)} async-done(((f32[1024,1024]{1,0:T(8,128)}), f32[32,1024]{1,0:T(8,128)}) %reduce-scatter.12.cloned.1.call-update) | async-done | bytes 131088 | tf_op jit(solution)/shard_map/reduce_scatter | solution.py:144
  1386.4 189.5 %reduce-scatter.6.cloned.1.call-done = f32[32,1024]{1,0:T(8,128)} async-done(((f32[1024,1024]{1,0:T(8,128)}), f32[32,1024]{1,0:T(8,128)}) %reduce-scatter.6.cloned.1.call-update) | async-done | bytes 131088 | tf_op jit(solution)/shard_map/reduce_scatter | solution.py:141
  1584.7 77.8 %all-reduce.4 = (f32[1024]{0:T(1024)S(1)}, f32[1024]{0:T(1024)S(1)}) all-reduce(f32[1024]{0:T(1024)S(1)} %add.332, f32[1024]{0:T(1024)S(1)} %copy-done.96), channel_id=9, replica_groups=mesh['rep'=4,'fsdp'=32] {'fsdp'}, use_global_device_ids=true, to_apply=%region_39.40.clone | all-reduce | flops 2048 | bytes 16384
  1665.9 89.4 %reduce-scatter.14.cloned.1.call-done = f32[32,32]{1,0:T(8,128)} async-done(((f32[1024,32]{1,0:T(8,128)}), f32[32,32]{1,0:T(8,128)}) %reduce-scatter.14.cloned.1.call-update) | async-done | bytes 4112 | tf_op jit(solution)/shard_map/reduce_scatter | solution.py:145
  1755.2 36.6 %all-reduce.5 = (f32[32]{0:T(128)}, f32[32]{0:T(128)}, f32[32,32]{1,0:T(8,128)}) all-reduce(f32[32]{0:T(128)S(1)} %dynamic-slice.3, f32[32]{0:T(128)S(1)} %dynamic-slice.5, f32[32,32]{1,0:T(8,128)} %reduce-scatter.14.cloned.1.call-done), channel_id=1, replica_groups=mesh['rep'=4,'fsdp'=32] {'rep'}, use_global_device_ids=true, to_apply=%region_42.43 | all-reduce | flops 1088 | bytes 8704 | tf_op jit(solution)/shard_map/psum | solution.py:343
  1791.8 120.3 %all-reduce.10.cloned.1.call-done = (f32[32,1024]{1,0:T(8,128)}, f32[32,512]{1,0:T(8,128)}, f32[32,512]{1,0:T(8,128)}, f32[32,1024]{1,0:T(8,128)}, f32[1,1024,51...) async-done(((f32[32,1024]{1,0:T(8,128)}, f32[32,512]{1,0:T(8,128)}, f32[32,512]{1,0:T(8,128)}, f32[32,1024]{1,0:T(8,128)}, f32[1,1024,512]{2,1,0:T(8,128)}, ...) | async-done | bytes 6684688 | tf_op jit(solution)/shard_map/psum | solution.py:343
  (453 shorter events, 157.9 us)
Async XLA Ops:
  7.2 457.7 %copy-start = (bf16[1,1024,512]{2,1,0:T(8,128)(2,1)S(1)}, bf16[1,1024,512]{2,1,0:T(8,128)(2,1)}, u32[]{:S(2)}) copy-start(bf16[1,1024,512]{2,1,0:T(8,128)(2,1)} %param.25) | copy-start | bytes 3145732
  7.2 106.8 %copy-start.103 = (s32[2,1,128]{2,1,0:T(1,128)S(1)}, s32[2,1,128]{2,1,0:T(1,128)}, u32[]{:S(2)}) copy-start(s32[2,1,128]{2,1,0:T(1,128)} %param.15) | copy-start | bytes 3076
  7.2 108.0 %copy-start.2 = (bf16[2,1,128,1024]{3,2,1,0:T(8,128)(2,1)S(1)}, bf16[2,1,128,1024]{3,2,1,0:T(8,128)(2,1)}, u32[]{:S(2)}) copy-start(bf16[2,1,128,1024]{3,2,1,0:T(8,128)(2,1)} %param.14) | copy-start | bytes 1572868
  7.2 108.0 %all-gather.5.cloned.1.call-start = ((), (), s32[]{:S(2)}) async-start(), calls=%async_computation.13 | async-start | bytes 1081344 | tf_op jit(solution)/shard_map/all_gather | solution.py:131
  8.0 137.5 %all-gather.7.cloned.1.call-start = ((), (), s32[]{:S(2)}) async-start(), calls=%async_computation.14 | async-start | bytes 1081344 | tf_op jit(solution)/shard_map/all_gather | solution.py:130
  8.7 208.1 %all-gather.9.cloned.1.call-start = ((), (), s32[]{:S(2)}) async-start(), calls=%async_computation.15 | async-start | bytes 2162688 | tf_op jit(solution)/shard_map/all_gather | solution.py:129
  9.4 278.1 %all-gather.11.cloned.1.call-start = ((), (), s32[]{:S(2)}) async-start(), calls=%async_computation.16 | async-start | bytes 2162688 | tf_op jit(solution)/shard_map/all_gather | solution.py:132
  103.2 120.0 %copy-start.68 = (f32[128,64]{0,1:T(8,128)}, f32[128,64]{0,1:T(8,128)S(1)}, u32[]{:S(2)}) copy-start(f32[128,64]{0,1:T(8,128)S(1)} %get-tuple-element.115) | copy-start | bytes 98308
  114.5 106.3 %copy-start.89 = (f32[128]{0:T(128)}, f32[128]{0:T(128)S(1)}, u32[]{:S(2)}) copy-start(f32[128]{0:T(128)S(1)} %get-tuple-element.159) | copy-start | bytes 1540
  114.5 176.1 %copy-start.94 = (s32[1024,1]{0,1:T(1,128)}, s32[1024,1]{0,1:T(1,128)S(1)}, u32[]{:S(2)}) copy-start(s32[1024,1]{0,1:T(1,128)S(1)} %compare_select_fusion.1) | copy-start | bytes 12292
  116.9 107.6 %copy-start.50 = (bf16[128,512]{0,1:T(8,128)(2,1)}, bf16[128,512]{0,1:T(8,128)(2,1)S(1)}, u32[]{:S(2)}) copy-start(bf16[128,512]{0,1:T(8,128)(2,1)S(1)} %copy.80) | copy-start | bytes 393220
  147.6 75.7 %copy-start.53 = (bf16[128,8,64,1]{0,2,3,1:T(8,128)(2,1)}, bf16[128,8,64,1]{0,2,3,1:T(8,128)(2,1)S(1)}, u32[]{:S(2)}) copy-start(bf16[128,8,64,1]{0,2,3,1:T(8,128)(2,1)S(1)} %fusion.168) | copy-start | bytes 393220
  225.7 64.1 %copy-start.36 = (bf16[8,64,2,128]{3,1,2,0:T(8,128)(2,1)}, bf16[8,64,2,128]{3,1,2,0:T(8,128)(2,1)S(1)}, u32[]{:S(2)}) copy-start(bf16[8,64,2,128]{3,1,2,0:T(8,128)(2,1)S(1)} %convolution_convert_fusion.5) | copy-start | bytes 786436
  298.0 128.3 %all-to-all-start = ((bf16[32,48,1024]{2,1,0:T(8,128)(2,1)}), bf16[32,48,1024]{2,1,0:T(8,128)(2,1)}, u32[]{:S(2)}, u32[]{:S(2)}) async-start(bf16[32,48,1024]{2,1,0:T(8,128)(2,1)} %bitcast.622), calls=%async_computation | async-start | bytes 6291456 | tf_op jit(solution)/shard_map/all_to_all | solution.py:215
  413.0 13.3 copy-start.19
  426.3 34.4 %all-to-all-start.4 = ((bf16[32,48,1024]{2,1,0:T(8,128)(2,1)}), bf16[32,48,1024]{2,1,0:T(8,128)(2,1)}, u32[]{:S(2)}, u32[]{:S(2)}) async-start(bf16[32,48,1024]{2,1,0:T(8,128)(2,1)} %bitcast.624), calls=%async_computation.4 | async-start | bytes 6291456 | tf_op jit(solution)/shard_map/all_to_all | solution.py:252
  476.0 22.7 %copy-start.80 = (f32[128,32]{0,1:T(8,128)S(1)}, f32[128,32]{0,1:T(8,128)}, u32[]{:S(2)}) copy-start(f32[128,32]{0,1:T(8,128)} %get-tuple-element.134) | copy-start | bytes 49156
  476.0 23.6 %copy-start.95 = (s32[1024,1]{0,1:T(1,128)S(1)}, s32[1024,1]{0,1:T(1,128)}, u32[]{:S(2)}) copy-start(s32[1024,1]{0,1:T(1,128)} %copy-done.94) | copy-start | bytes 12292
  476.0 24.8 %copy-start.86 = (f32[128]{0:T(128)S(1)}, f32[128]{0:T(128)}, u32[]{:S(2)}) copy-start(f32[128]{0:T(128)} %get-tuple-element.158) | copy-start | bytes 1540
  476.0 47.8 %all-to-all-start.1 = ((bf16[32,48,1024]{2,1,0:T(8,128)(2,1)}), bf16[32,48,1024]{2,1,0:T(8,128)(2,1)}, u32[]{:S(2)}, u32[]{:S(2)}) async-start(bf16[32,48,1024]{2,1,0:T(8,128)(2,1)} %convolution_convert_fusion.1), calls=%async_computation.1 | async-start | bytes 6291456 | tf_op jit(solution)/shard_map/all_to_all | solution.py:226
  499.4 49.1 %copy-start.69 = (f32[128,64]{0,1:T(8,128)}, f32[128,64]{0,1:T(8,128)S(1)}, u32[]{:S(2)}) copy-start(f32[128,64]{0,1:T(8,128)S(1)} %get-tuple-element.119) | copy-start | bytes 98308
  502.5 46.8 %copy-start.52 = (bf16[128,512]{0,1:T(8,128)(2,1)}, bf16[128,512]{0,1:T(8,128)(2,1)S(1)}, u32[]{:S(2)}) copy-start(bf16[128,512]{0,1:T(8,128)(2,1)S(1)} %copy.91) | copy-start | bytes 393220
  503.8 44.9 %copy-start.55 = (bf16[128,8,64,1]{0,2,3,1:T(8,128)(2,1)}, bf16[128,8,64,1]{0,2,3,1:T(8,128)(2,1)S(1)}, u32[]{:S(2)}) copy-start(bf16[128,8,64,1]{0,2,3,1:T(8,128)(2,1)S(1)} %fusion.167) | copy-start | bytes 393220
  510.8 35.2 %copy-start.87 = (f32[128]{0:T(128)S(1)}, f32[128]{0:T(128)}, u32[]{:S(2)}) copy-start(f32[128]{0:T(128)} %get-tuple-element.158) | copy-start | bytes 1540
  523.8 58.5 %all-to-all-start.5 = ((bf16[32,48,1024]{2,1,0:T(8,128)(2,1)}), bf16[32,48,1024]{2,1,0:T(8,128)(2,1)}, u32[]{:S(2)}, u32[]{:S(2)}) async-start(bf16[32,48,1024]{2,1,0:T(8,128)(2,1)} %add_convert_fusion.1), calls=%async_computation.5 | async-start | bytes 6291456 | tf_op jit(solution)/shard_map/all_to_all | solution.py:277
  563.9 27.5 %copy-start.74 = (f32[128,1,32]{2,1,0:T(1,128)}, f32[128,1,32]{2,1,0:T(1,128)S(1)}, u32[]{:S(2)}) copy-start(f32[128,1,32]{2,1,0:T(1,128)S(1)} %fusion.124) | copy-start | bytes 49156
  594.3 20.7 %copy-start.30 = (bf16[128,1024]{1,0:T(8,128)(2,1)}, bf16[128,1024]{1,0:T(8,128)(2,1)S(1)}, u32[]{:S(2)}) copy-start(bf16[128,1024]{1,0:T(8,128)(2,1)S(1)} %get-tuple-element.126) | copy-start | bytes 786436
  601.8 14.7 copy-start.18
  601.8 52.7 %all-to-all-start.2 = ((bf16[32,48,1024]{2,1,0:T(8,128)(2,1)}), bf16[32,48,1024]{2,1,0:T(8,128)(2,1)}, u32[]{:S(2)}, u32[]{:S(2)}) async-start(bf16[32,48,1024]{2,1,0:T(8,128)(2,1)} %bitcast.623), calls=%async_computation.2 | async-start | bytes 6291456 | tf_op jit(solution)/shard_map/all_to_all | solution.py:215
  615.0 39.5 %copy-start.82 = (s32[128,8]{1,0:T(8,128)}, s32[128,8]{1,0:T(8,128)S(1)}, u32[]{:S(2)}) copy-start(s32[128,8]{1,0:T(8,128)S(1)} %copy.94) | copy-start | bytes 12292
  616.2 38.3 %copy-start.106 = (f32[128]{0:T(128)}, f32[128]{0:T(128)S(1)}, u32[]{:S(2)}) copy-start(f32[128]{0:T(128)S(1)} %fusion.185) | copy-start | bytes 1540
  616.4 38.2 %copy-start.62 = (f32[128,8]{1,0:T(8,128)}, f32[128,8]{1,0:T(8,128)S(1)}, u32[]{:S(2)}) copy-start(f32[128,8]{1,0:T(8,128)S(1)} %fusion.184) | copy-start | bytes 12292
  654.5 50.6 %all-to-all-start.6 = ((bf16[32,48,1024]{2,1,0:T(8,128)(2,1)}), bf16[32,48,1024]{2,1,0:T(8,128)(2,1)}, u32[]{:S(2)}, u32[]{:S(2)}) async-start(bf16[32,48,1024]{2,1,0:T(8,128)(2,1)} %bitcast.625), calls=%async_computation.6 | async-start | bytes 6291456 | tf_op jit(solution)/shard_map/all_to_all | solution.py:252
  665.1 40.1 %copy-start.117 = (bf16[1,512,1024]{2,1,0:T(8,128)(2,1)S(1)}, bf16[1,512,1024]{2,1,0:T(8,128)(2,1)}, u32[]{:S(2)}) copy-start(bf16[1,512,1024]{2,1,0:T(8,128)(2,1)} %param.27) | copy-start | bytes 3145732
  720.0 50.7 %all-to-all-start.3 = ((bf16[32,48,1024]{2,1,0:T(8,128)(2,1)}), bf16[32,48,1024]{2,1,0:T(8,128)(2,1)}, u32[]{:S(2)}, u32[]{:S(2)}) async-start(bf16[32,48,1024]{2,1,0:T(8,128)(2,1)} %convolution_convert_fusion), calls=%async_computation.3 | async-start | bytes 6291456 | tf_op jit(solution)/shard_map/all_to_all | solution.py:226
  737.3 44.0 %copy-start.93 = (s32[1024,1]{0,1:T(1,128)S(1)}, s32[1024,1]{0,1:T(1,128)}, u32[]{:S(2)}) copy-start(s32[1024,1]{0,1:T(1,128)} %compare_select_fusion) | copy-start | bytes 12292
  737.3 44.0 %copy-start.115 = (f32[128]{0:T(128)S(1)}, f32[128]{0:T(128)}, u32[]{:S(2)}) copy-start(f32[128]{0:T(128)} %get-tuple-element.55) | copy-start | bytes 1540
  770.7 51.5 %all-to-all-start.7 = ((bf16[32,48,1024]{2,1,0:T(8,128)(2,1)}), bf16[32,48,1024]{2,1,0:T(8,128)(2,1)S(1)}, u32[]{:S(2)}, u32[]{:S(2)}) async-start(bf16[32,48,1024]{2,1,0:T(8,128)(2,1)} %add_convert_fusion), calls=%async_computation.7 | async-start | bytes 6291456 | tf_op jit(solution)/shard_map/all_to_all | solution.py:277
  781.3 228.8 %reduce-scatter.10.cloned.1.call-start = ((), (), s32[]{:S(2)}) async-start(), calls=%async_computation.19 | async-start | bytes 2162688 | tf_op jit(solution)/shard_map/reduce_scatter | solution.py:143
  795.2 35.8 %copy-start.76 = (f32[128,1,32]{2,1,0:T(1,128)}, f32[128,1,32]{2,1,0:T(1,128)S(1)}, u32[]{:S(2)}) copy-start(f32[128,1,32]{2,1,0:T(1,128)S(1)} %fusion.122) | copy-start | bytes 49156
  846.1 348.9 %reduce-scatter.8.cloned.1.call-start = ((), (), s32[]{:S(2)}) async-start(), calls=%async_computation.18 | async-start | bytes 2162688 | tf_op jit(solution)/shard_map/reduce_scatter | solution.py:142
  852.7 533.7 %reduce-scatter.12.cloned.1.call-start = ((), (), s32[]{:S(2)}) async-start(), calls=%async_computation.20 | async-start | bytes 4325376 | tf_op jit(solution)/shard_map/reduce_scatter | solution.py:144
  856.5 719.4 %reduce-scatter.6.cloned.1.call-start = ((), (), s32[]{:S(2)}) async-start(), calls=%async_computation.17 | async-start | bytes 4325376 | tf_op jit(solution)/shard_map/reduce_scatter | solution.py:141
  863.9 891.3 %reduce-scatter.14.cloned.1.call-start = ((), (), s32[]{:S(2)}) async-start(), calls=%async_computation.21 | async-start | bytes 540672 | tf_op jit(solution)/shard_map/reduce_scatter | solution.py:145
  888.9 1023.2 %all-reduce.10.cloned.1.call-start = ((), (), s32[]{:S(2)}) async-start(), calls=%async_computation.22 | async-start | bytes 13369344 | tf_op jit(solution)/shard_map/psum | solution.py:343
  1583.4 79.2 %copy-start.59 = (bf16[1,128,1024]{2,1,0:T(8,128)(2,1)S(1)}, bf16[1,128,1024]{2,1,0:T(8,128)(2,1)}, u32[]{:S(2)}) copy-start(bf16[1,128,1024]{2,1,0:T(8,128)(2,1)} %get-tuple-element.88) | copy-start | bytes 786436
  1583.4 79.2 %copy-start.60 = (bf16[1,128,1024]{2,1,0:T(8,128)(2,1)S(1)}, bf16[1,128,1024]{2,1,0:T(8,128)(2,1)}, u32[]{:S(2)}) copy-start(bf16[1,128,1024]{2,1,0:T(8,128)(2,1)} %get-tuple-element.95) | copy-start | bytes 786436
  1583.5 80.0 %copy-start.14 = (f32[128,1024]{1,0:T(8,128)S(1)}, f32[128,1024]{1,0:T(8,128)}, u32[]{:S(2)}) copy-start(f32[128,1024]{1,0:T(8,128)} %copy-done.12) | copy-start | bytes 1572868
  (94 other events, 355.4 us)
Sparse Core Ops, SparseCore 0:
  11.0 67.9 all-gather.4
  82.0 63.4 all-gather.6
  148.6 68.2 all-gather.8
  219.8 67.6 all-gather.10
  846.2 163.9 reduce-scatter.9
  1013.1 181.8 reduce-scatter.7
  1197.3 188.9 reduce-scatter.11
  1388.8 187.0 reduce-scatter.5
  1578.2 176.9 reduce-scatter.13
  1759.0 153.0 all-reduce.9
where the time goes:
time: 1940 us; the launch traced here: 1930 us
  waiting for transfers between devices  1230 us (63%)
  blocking collectives  306 us (16%)
  matrix products  132 us (7%)
  starting transfers between devices  90.4 us (5%)
  local copies, waits for them, and re-layouts  81.1 us (4%)
  other arithmetic  72.8 us (4%)
    reduce_scatter x1, waiting for transfers between devices, reduce_dense(): lax.psum_scatter(grads[5], 'fsdp', scatter_dimension=0, tiled=True)  191 us
    reduce_scatter x1, waiting for transfers between devices, reduce_dense(): lax.psum_scatter(grads[2], 'fsdp', scatter_dimension=0, tiled=True)  189 us
    reduce_scatter x1, waiting for transfers between devices, reduce_dense(): lax.psum_scatter(grads[3], 'fsdp', scatter_dimension=0, tiled=True)  185 us
    unnamed x2, blocking collectives  162 us
    psum x1, waiting for transfers between devices, on_device(): lax.psum((totals[0], totals[1], totals[2], totals[3], totals[4], totals[5...  120 us
    reduce_scatter x1, waiting for transfers between devices, reduce_dense(): lax.psum_scatter(grads[4], 'fsdp', scatter_dimension=0, tiled=True)  115 us
    all_gather x1, blocking collectives, fetch_dense(): lax.all_gather(w_router, 'fsdp', axis=0, tiled=True)  107 us
    reduce_scatter x1, waiting for transfers between devices, reduce_dense(): lax.psum_scatter(grads[6], 'fsdp', scatter_dimension=0, tiled=True)  89.4 us
  transfers between devices with their start and end apart: 18, of which 16 were waited for; matrix products, arithmetic and copies ran while one was open for 9% of the time, Pallas kernels for 0%

commit v1 on v0

v1 whole, which is shorter than its diff:
```python
import functools
import math

import jax
import jax.numpy as jnp
from jax import lax
from jax.experimental import pallas as pl
from jax.experimental.pallas import tpu as pltpu
from jax.sharding import PartitionSpec as P

D = 1024
HEADS = 16
KV_HEADS = 8
HEAD_DIM = 64
EXPERTS = 32
FE = 512
TOPK = 8
CAP = 48
LENGTH = 128

EPS = 1e-06
RESIDUAL = 0.22
ATT_SCALE = 0.015625
ROPE_BASE = 10000.0
NEG = -1000000000.0

MESH = pl.DeviceIdType.MESH
F32 = jnp.float32
BF16 = jnp.bfloat16
WIDE = 3200
CUT = 1664
HERE = 4


class Place:
    def __init__(self):
        rep = lax.axis_index("rep")
        flat = lax.axis_index("fsdp")
        self.core = lax.rem(rep, 2)
        self.low = lax.div(rep, 2)
        self.high = lax.div(flat, 16)
        self.x = lax.rem(lax.div(flat, 4), 4)
        self.z = lax.rem(flat, 4)

    def at(self, low=None, core=None, high=None, x=None, z=None):
        low = self.low if low is None else low
        core = self.core if core is None else core
        high = self.high if high is None else high
        x = self.x if x is None else x
        z = self.z if z is None else z
        return (low * 2 + core, high * 16 + x * 4 + z)

    def right(self):
        return self.at(x=lax.rem(self.x + 1, 4))

    def left(self):
        return self.at(x=lax.rem(self.x + 3, 4))

    def above(self):
        return self.at(z=lax.rem(self.z + 1, 4))

    def below(self):
        return self.at(z=lax.rem(self.z + 3, 4))

    def cross(self):
        return self.at(low=1 - self.low, high=1 - self.high)

    def twin(self):
        return self.at(low=1 - self.low)

    def sibling(self):
        return self.at(core=1 - self.core)


class Lines:
    def __init__(self, send_sems, recv_sems):
        self.send_sems, self.recv_sems, self.copies = send_sems, recv_sems, []

    def send(self, src, dst, device):
        i = len(self.copies)
        assert i < self.send_sems.shape[0]
        copy = pltpu.make_async_remote_copy(
            src_ref=src,
            dst_ref=dst,
            send_sem=self.send_sems.at[i],
            recv_sem=self.recv_sems.at[i],
            device_id=device,
            device_id_type=MESH,
        )
        copy.start()
        self.copies.append(copy)
        return copy

    def drain(self):
        for copy in self.copies:
            copy.wait_send()


def greet(partners):
    barrier = pltpu.get_barrier_semaphore()
    for partner in partners:
        pl.semaphore_signal(barrier, inc=1, device_id=partner, device_id_type=MESH)
    pl.semaphore_wait(barrier, len(partners))


def drive(*chains):
    live = list(chains)
    while live:
        for chain in list(live):
            try:
                next(chain)
            except StopIteration:
                live.remove(chain)


def ring_gather(lines, source, slot, half, pos, right, left, spread=None):
    ahead, behind, far = lax.rem(pos + 1, 4), lax.rem(pos + 3, 4), lax.rem(pos + 2, 4)
    spread = spread or (lambda p: None)
    a = lines.send(source, slot(pos), right)
    b = lines.send(source, slot(pos), left)
    yield
    a.wait_recv()
    c = lines.send(half(behind, 0), half(behind, 0), right)
    b.wait_recv()
    d = lines.send(half(ahead, 1), half(ahead, 1), left)
    spread(behind)
    spread(ahead)
    yield
    c.wait_recv()
    d.wait_recv()
    spread(far)


def group_gather(lines, me, source, buf):
    rows = buf.shape[1]
    ahead, behind, far = lax.rem(me.x + 1, 4), lax.rem(me.x + 3, 4), lax.rem(me.x + 2, 4)
    right, left, cross = me.right(), me.left(), me.cross()
    base, other = me.high * 4, (1 - me.high) * 4

    def half(k, h):
        return buf.at[k, pl.ds(h * rows // 2, rows // 2)]

    a = lines.send(source, buf.at[base + me.x], right)
    b = lines.send(source, buf.at[base + me.x], left)
    e = lines.send(source, buf.at[base + me.x], cross)
    yield
    a.wait_recv()
    c = lines.send(half(base + behind, 0), half(base + behind, 0), right)
    b.wait_recv()
    d = lines.send(half(base + ahead, 1), half(base + ahead, 1), left)
    e.wait_recv()
    f = lines.send(buf.at[other + me.x], buf.at[other + me.x], right)
    g = lines.send(buf.at[other + me.x], buf.at[other + me.x], left)
    yield
    c.wait_recv()
    d.wait_recv()
    h = lines.send(buf.at[base + far], buf.at[base + far], cross)
    yield
    f.wait_recv()
    g.wait_recv()
    h.wait_recv()


def tiles(rows, step, body):
    @pl.loop(0, rows // step)
    def _(i):
        body(pl.ds(pl.multiple_of(i * step, step), step))


def group_scatter(lines, me, q, out, by, sf, tl, tr, t, hl, hr, nl, nr, fl, fr, fy):
    rows = q.shape[1]
    mid = rows // 2
    step = min(32, mid)
    ahead, behind, far = lax.rem(me.x + 1, 4), lax.rem(me.x + 3, 4), lax.rem(me.x + 2, 4)
    right, left, cross = me.right(), me.left(), me.cross()
    base, other = me.high * 4, (1 - me.high) * 4
    first, second = pl.ds(0, mid), pl.ds(mid, mid)

    def wide(ref, sl):
        return ref[sl].astype(F32)

    e = lines.send(q.at[other + far], by, cross)
    g1 = lines.send(q.at[other + ahead], tl, right)
    g2 = lines.send(q.at[other + behind], tr, left)
    i1 = lines.send(q.at[base + ahead, second], fl.at[second], right)
    i2 = lines.send(q.at[base + behind, first], fr.at[first], left)
    yield
    e.wait_recv()

    def far_sum(sl):
        sf[sl] = (q[base + far, sl].astype(F32) + wide(by, sl)).astype(sf.dtype)

    tiles(rows, step, far_sum)
    j1 = lines.send(sf.at[first], hl, right)
    j2 = lines.send(sf.at[second], hr, left)
    yield
    g1.wait_recv()
    g2.wait_recv()

    def partner_sum(sl):
        t[sl] = (q[other + me.x, sl].astype(F32) + wide(tl, sl) + wide(tr, sl)).astype(t.dtype)

    tiles(rows, step, partner_sum)
    k = lines.send(t, fy, cross)
    yield
    j1.wait_recv()

    def right_sum(sl):
        nl[sl] = (q[base + ahead, sl].astype(F32) + wide(hl, sl)).astype(nl.dtype)

    tiles(mid, step, right_sum)
    l1 = lines.send(nl, fl.at[first], right)
    j2.wait_recv()

    @pl.loop(0, mid // step)
    def _(i):
        here = pl.ds(pl.multiple_of(i * step, step), step)
        there = pl.ds(pl.multiple_of(mid + i * step, step), step)
        nr[here] = (q[base + behind, there].astype(F32) + wide(hr, here)).astype(nr.dtype)

    l2 = lines.send(nr, fr.at[second], left)
    yield
    for copy in (i1, i2, l1, l2, k):
        copy.wait_recv()

    def total(sl):
        out[sl] = q[base + me.x, sl].astype(F32) + wide(fl, sl) + wide(fr, sl) + wide(fy, sl)

    tiles(rows, step, total)


def ring_scatter(lines, arr, pos, right, left, hl, hr, fl, fr, store):
    n = arr.shape[2]
    ahead, behind, far = lax.rem(pos + 1, 4), lax.rem(pos + 3, 4), lax.rem(pos + 2, 4)
    a = lines.send(arr.at[far, 0], hl, right)
    b = lines.send(arr.at[far, 1], hr, left)
    c = lines.send(arr.at[ahead, 1], fl.at[1], right)
    d = lines.send(arr.at[behind, 0], fr.at[0], left)
    yield
    a.wait_recv()

    @pl.loop(0, n)
    def _(j):
        arr[ahead, 0, j] = (arr[ahead, 0, j].astype(F32) + hl[j].astype(F32)).astype(arr.dtype)

    e = lines.send(arr.at[ahead, 0], fl.at[0], right)
    b.wait_recv()

    @pl.loop(0, n)
    def _(j):
        arr[behind, 1, j] = (arr[behind, 1, j].astype(F32) + hr[j].astype(F32)).astype(arr.dtype)

    f = lines.send(arr.at[behind, 1], fr.at[1], left)
    yield
    for copy in (c, d, e, f):
        copy.wait_recv()
    for half in range(2):

        @pl.loop(0, n)
        def _(j, half=half):
            store(
                half,
                j,
                arr[pos, half, j].astype(F32) + fl[half, j].astype(F32) + fr[half, j].astype(F32),
            )


def early_kernel(
    pack, g, slots, wg, wu, wd, dense, gbuf, sbuf, wgb, wub, wdb, send_sems, recv_sems, local_sems
):
    me = Place()
    right, left, above, below = me.right(), me.left(), me.above(), me.below()
    cross, sibling = me.cross(), me.sibling()
    rows = pl.ds(pl.multiple_of(me.core * 16, 16), 16)
    own = me.high * 4 + me.x
    local = [
        pltpu.make_async_copy(pack.at[rows], dense.at[me.high, me.x, me.z, rows], local_sems.at[0]),
        pltpu.make_async_copy(g, gbuf.at[own], local_sems.at[1]),
        pltpu.make_async_copy(slots, sbuf.at[own], local_sems.at[2]),
        pltpu.make_async_copy(wg, wgb.at[me.z], local_sems.at[3]),
        pltpu.make_async_copy(wu, wub.at[me.z], local_sems.at[4]),
        pltpu.make_async_copy(wd, wdb.at[me.z], local_sems.at[5]),
    ]
    for copy in local:
        copy.start()
    greet((right, left, above, below, cross, sibling))
    lines = Lines(send_sems, recv_sems)
    shared = []

    def dense_chain(columns, x_first):
        def on_z(p, k=None):
            if x_first:
                return dense.at[slice(None) if k is None else k, :, p, rows, columns]
            return dense.at[slice(None) if k is None else k, me.x, p, rows, columns]

        def on_x(p, k=None):
            if x_first:
                return dense.at[slice(None) if k is None else k, p, me.z, rows, columns]
            return dense.at[slice(None) if k is None else k, p, :, rows, columns]

        if x_first:
            first = (on_x(me.x), on_x, on_x, me.x, right, left)
            last = (on_z(me.z), on_z, on_z, me.z, above, below)
        else:
            first = (on_z(me.z), on_z, on_z, me.z, above, below)
            last = (on_x(me.x), on_x, on_x, me.x, right, left)
        yield from ring_gather(lines, *first)

        def spread(p):
            shared.append(lines.send(last[1](p), last[1](p), sibling))

        spread(last[3])
        yield from ring_gather(lines, *last, spread=spread)

    def weight_chain(source, buf):
        half_rows = source.shape[0] // 2
        quarter = half_rows // 2
        start = me.core * half_rows

        def slot(p):
            return buf.at[p, pl.ds(pl.multiple_of(start, half_rows), half_rows)]

        def half(p, k):
            return buf.at[p, pl.ds(pl.multiple_of(start + k * quarter, quarter), quarter)]

        def spread(p):
            shared.append(lines.send(slot(p), slot(p), sibling))

        yield from ring_gather(
            lines,
            source.at[pl.ds(pl.multiple_of(start, half_rows), half_rows)],
            slot,
            half,
            me.z,
            above,
            below,
            spread=spread,
        )

    swap = lines.send(pack.at[rows], dense.at[me.high, me.x, me.z, rows], cross)
    local[0].wait()
    swap.wait_recv()
    drive(
        dense_chain(pl.ds(0, CUT), False),
        dense_chain(pl.ds(CUT, WIDE - CUT), True),
        group_gather(lines, me, g, gbuf),
        group_gather(lines, me, slots, sbuf),
        weight_chain(wg, wgb),
        weight_chain(wu, wub),
        weight_chain(wd, wdb),
    )
    for copy in shared:
        copy.wait_recv()
    for copy in local[1:]:
        copy.wait()
    lines.drain()


def anywhere(n):
    return [pl.BlockSpec(memory_space=pl.ANY)] * n


def vmem(n):
    return [pl.BlockSpec(memory_space=pltpu.VMEM)] * n


def sems(n):
    return [pltpu.SemaphoreType.DMA((n,)), pltpu.SemaphoreType.DMA((n,))]


def params(number=None, limit=56):
    if number is None:
        return pltpu.CompilerParams(vmem_limit_bytes=limit << 20)
    return pltpu.CompilerParams(
        collective_id=number, has_side_effects=True, vmem_limit_bytes=limit << 20
    )


def early(pack, g, slots, wg, wu, wd):
    shape = jax.ShapeDtypeStruct
    return pl.pallas_call(
        early_kernel,
        name="early",
        out_shape=(
            shape((2, 4, 4, 32, WIDE), BF16),
            shape((8,) + g.shape, BF16),
            shape((8,) + slots.shape, BF16),
            shape((4,) + wg.shape, BF16),
            shape((4,) + wu.shape, BF16),
            shape((4,) + wd.shape, BF16),
        ),
        in_specs=anywhere(6),
        out_specs=anywhere(6),
        scratch_shapes=sems(72) + [pltpu.SemaphoreType.DMA((6,))],
        compiler_params=params(0),
    )(pack, g, slots, wg, wu, wd)


def route_kernel(h, gates, hbuf, gbuf, send_sems, recv_sems, local_sems):
    me = Place()
    own = me.high * 4 + me.x
    local = [
        pltpu.make_async_copy(h, hbuf.at[own], local_sems.at[0]),
        pltpu.make_async_copy(gates, gbuf.at[own], local_sems.at[1]),
    ]
    for copy in local:
        copy.start()
    greet((me.right(), me.left(), me.cross()))
    lines = Lines(send_sems, recv_sems)
    drive(group_gather(lines, me, h, hbuf), group_gather(lines, me, gates, gbuf))
    for copy in local:
        copy.wait()
    lines.drain()


def route(h, gates):
    shape = jax.ShapeDtypeStruct
    return pl.pallas_call(
        route_kernel,
        name="route",
        out_shape=(shape((8,) + h.shape, h.dtype), shape((8,) + gates.shape, gates.dtype)),
        in_specs=anywhere(2),
        out_specs=anywhere(2),
        scratch_shapes=sems(24) + [pltpu.SemaphoreType.DMA((2,))],
        compiler_params=params(1),
    )(h, gates)


def scatter_scratch(rows, columns, dtype):
    full = pltpu.VMEM((rows, columns), dtype)
    half = pltpu.VMEM((rows // 2, columns), dtype)
    return [full] * 5 + [half] * 4 + [full] * 3


def back_kernel(qy, qh, qg, y, dh, dg, *scratch):
    me = Place()
    send_sems, recv_sems = scratch[:2]
    greet((me.right(), me.left(), me.cross()))
    lines = Lines(send_sems, recv_sems)
    drive(
        group_scatter(lines, me, qg, dg, *scratch[2:14]),
        group_scatter(lines, me, qh, dh, *scratch[14:26]),
        group_scatter(lines, me, qy, y, *scratch[26:38]),
    )
    lines.drain()


def send_back(qy, qh, qg):
    shape = jax.ShapeDtypeStruct
    rows = qy.shape[1]
    return pl.pallas_call(
        back_kernel,
        name="send_back",
        out_shape=(shape((rows, D), F32), shape((rows, D), F32), shape(qg.shape[1:], F32)),
        in_specs=vmem(3),
        out_specs=vmem(3),
        scratch_shapes=sems(36)
        + scatter_scratch(qg.shape[1], qg.shape[2], F32)
        + scatter_scratch(rows, D, BF16)
        + scatter_scratch(rows, D, BF16),
        compiler_params=params(2),
    )(qy, qh, qg)


def expert_sum_kernel(gg, gu, gd, og, ou, od, *scratch):
    me = Place()
    send_sems, recv_sems = scratch[:2]
    above, below, twin, sibling = me.above(), me.below(), me.twin(), me.sibling()
    greet((above, below, twin, sibling))
    lines = Lines(send_sems, recv_sems)

    def chain(grad, out, rc, acc, hl, hr, fl, fr, tot, yb):
        first = lines.send(grad.at[:, 1 - me.core], rc, sibling)
        yield
        first.wait_recv()

        @pl.loop(0, 32)
        def _(i):
            p, k, j = lax.div(i, 8), lax.rem(lax.div(i, 4), 2), lax.rem(i, 4)
            acc[p, k, j] = (
                grad[p, me.core, k, j].astype(F32) + rc[p, k, j].astype(F32)
            ).astype(BF16)

        def store(k, j, value):
            tot[k, j] = value.astype(BF16)

        yield from ring_scatter(lines, acc, me.z, above, below, hl, hr, fl, fr, store)
        second = lines.send(tot, yb, twin)
        yield
        second.wait_recv()
        for k in range(2):

            @pl.loop(0, 4)
            def _(j, k=k):
                out[me.core, k, j] = tot[k, j].astype(F32) + yb[k, j].astype(F32)

        last = lines.send(out.at[me.core], out.at[me.core], sibling)
        yield
        last.wait_recv()

    drive(
        chain(gg, og, *scratch[2:10]),
        chain(gu, ou, *scratch[10:18]),
        chain(gd, od, *scratch[18:26]),
    )
    lines.drain()


def expert_sum(gg, gu, gd):
    def scratch(r, w):
        shapes = [(4, 2, 4, r, w)] * 2 + [(4, r, w)] * 2 + [(2, 4, r, w)] * 4
        return [pltpu.VMEM(s, BF16) for s in shapes]

    shape = jax.ShapeDtypeStruct
    outs = pl.pallas_call(
        expert_sum_kernel,
        name="expert_sum",
        out_shape=(
            shape((2, 2, 4, 64, 512), F32),
            shape((2, 2, 4, 64, 512), F32),
            shape((2, 2, 4, 32, 1024), F32),
        ),
        in_specs=vmem(3),
        out_specs=vmem(3),
        scratch_shapes=sems(30) + scratch(64, 512) + scratch(64, 512) + scratch(32, 1024),
        compiler_params=params(3, 58),
    )(
        gg.reshape(4, 2, 2, 4, 64, 512),
        gu.reshape(4, 2, 2, 4, 64, 512),
        gd.reshape(4, 2, 2, 4, 32, 1024),
    )
    return outs[0].reshape(1, D, FE), outs[1].reshape(1, D, FE), outs[2].reshape(1, FE, D)


def dense_sum_kernel(grads, out, rc, *scratch):
    me = Place()
    send_sems, recv_sems = scratch[:2]
    right, left, above, below = me.right(), me.left(), me.above(), me.below()
    cross, twin, sibling = me.cross(), me.twin(), me.sibling()
    greet((right, left, above, below, cross, twin, sibling))
    lines = Lines(send_sems, recv_sems)
    mine = pl.ds(pl.multiple_of(me.core * 16, 16), 16)
    theirs = pl.ds(pl.multiple_of((1 - me.core) * 16, 16), 16)
    swap = lines.send(grads.at[:, :, :, theirs], rc, sibling)
    swap.wait_recv()

    def chain(columns, x_first, acc, second, hl, hr, fl, fr, hl2, hr2, fl2, fr2, r2, ry, r3, yb):
        @pl.loop(0, 32)
        def _(i):
            k, x, z = lax.div(i, 16), lax.rem(lax.div(i, 4), 4), lax.rem(i, 4)
            value = grads[k, x, z, mine, columns].astype(F32) + rc[k, x, z, :, columns].astype(F32)
            if x_first:
                acc[x, k, z] = value.astype(BF16)
            else:
                acc[z, k, x] = value.astype(BF16)

        yield

        def store(k, j, value):
            second[j, k, 0] = value.astype(BF16)

        def store_last(k, j, value):
            r2[k] = value.astype(BF16)

        on_x, on_z = (me.x, right, left), (me.z, above, below)
        one, two = (on_x, on_z) if x_first else (on_z, on_x)
        yield from ring_scatter(lines, acc, *one, hl, hr, fl, fr, store)
        yield from ring_scatter(lines, second, *two, hl2, hr2, fl2, fr2, store_last)
        a = lines.send(r2.at[1 - me.high], ry, cross)
        yield
        a.wait_recv()
        r3[...] = (r2[me.high].astype(F32) + ry[...].astype(F32)).astype(BF16)
        b = lines.send(r3, yb, twin)
        yield
        b.wait_recv()
        out[mine, columns] = r3[...].astype(F32) + yb[...].astype(F32)
        c = lines.send(out.at[mine, columns], out.at[mine, columns], sibling)
        yield
        c.wait_recv()

    drive(
        chain(pl.ds(0, CUT), True, *scratch[2:16]),
        chain(pl.ds(CUT, WIDE - CUT), False, *scratch[16:30]),
    )
    lines.drain()


def dense_sum(grads):
    def scratch(w):
        shapes = [
            (4, 2, 4, 16, w),
            (4, 2, 1, 16, w),
            (4, 16, w),
            (4, 16, w),
            (2, 4, 16, w),
            (2, 4, 16, w),
            (1, 16, w),
            (1, 16, w),
            (2, 1, 16, w),
            (2, 1, 16, w),
            (2, 16, w),
            (16, w),
            (16, w),
            (16, w),
        ]
        return [pltpu.VMEM(s, BF16) for s in shapes]

    return pl.pallas_call(
        dense_sum_kernel,
        name="dense_sum",
        out_shape=jax.ShapeDtypeStruct((32, WIDE), F32),
        in_specs=vmem(1),
        out_specs=pl.BlockSpec(memory_space=pltpu.VMEM),
        scratch_shapes=[pltpu.VMEM((2, 4, 4, 16, WIDE), BF16)]
        + sems(40)
        + scratch(CUT)
        + scratch(WIDE - CUT),
        compiler_params=params(4),
    )(grads.reshape(2, 4, 4, 32, WIDE))


def dot(a, b, dims=((1,), (0,))):
    return lax.dot_general(a, b, (dims, ((), ())), preferred_element_type=F32)


def experts_kernel(
    h, g, pos, gates, wg, wu, wd, qy, qh, dg, gg, gu, gd, xs, gs, dys, gys, dhs, ms, das, dbs, gcol, dcol
):
    e = pl.program_id(0)
    n_seqs = h.shape[0]
    rows = n_seqs * CAP
    places = lax.broadcasted_iota(jnp.int32, (CAP, LENGTH), 0).astype(F32)

    def slots_of(s, k):
        return pl.ds(pl.multiple_of(s * CAP, CAP), CAP)

    @pl.loop(0, n_seqs)
    def _(s):
        here = slots_of(s, e)
        chosen = places == pos[e, pl.ds(s, 1), :]
        pick = chosen.astype(F32).astype(BF16)
        xs[here] = dot(pick, h[s]).astype(BF16)
        got = dot(pick, g[s])
        weight = jnp.sum(jnp.where(chosen, gates[e, pl.ds(s, 1), :], 0.0), axis=1, keepdims=True)
        gs[here] = got.astype(BF16)
        dys[here] = (weight * (RESIDUAL * got)).astype(BF16)
        gcol[here] = jnp.broadcast_to(weight, (CAP, LENGTH))

    @pl.loop(0, rows // 256)
    def _(r):
        here = pl.ds(pl.multiple_of(r * 256, 256), 256)
        x = xs[here]
        a = dot(x, wg[0])
        b = dot(x, wu[0])
        sig = jax.nn.sigmoid(a)
        swish = a * sig
        m = (swish * b).astype(BF16)
        ms[here] = m
        y = dot(m, wd[0]).astype(BF16).astype(F32)
        inner = RESIDUAL * jnp.sum(gs[here].astype(F32) * y, axis=1, keepdims=True)
        dcol[here] = jnp.broadcast_to(inner, (256, LENGTH))
        gys[e, here] = (gcol[here][:, :1] * y).astype(BF16)
        dm = dot(dys[here], wd[0], ((1,), (1,)))
        da = (dm * b * sig * (1.0 + a * (1.0 - sig))).astype(BF16)
        db = (dm * swish).astype(BF16)
        das[here] = da
        dbs[here] = db
        dh = dot(da, wg[0], ((1,), (1,))) + dot(db, wu[0], ((1,), (1,)))
        dhs[e, here] = dh.astype(BF16)

    @pl.loop(0, n_seqs)
    def _(s):
        chosen = places == pos[e, pl.ds(s, 1), :]
        part = jnp.sum(jnp.where(chosen, dcol[slots_of(s, e)], 0.0), axis=0, keepdims=True)
        dg[e, pl.ds(s, 1), :] = part

    @pl.loop(0, D // 256)
    def _(r):
        here = pl.ds(pl.multiple_of(r * 256, 256), 256)
        x = xs[:, here]
        gg[0, here] = dot(x, das[...], ((0,), (0,))).astype(BF16)
        gu[0, here] = dot(x, dbs[...], ((0,), (0,))).astype(BF16)

    @pl.loop(0, FE // 256)
    def _(r):
        here = pl.ds(pl.multiple_of(r * 256, 256), 256)
        gd[0, here] = dot(ms[:, here], dys[...], ((0,), (0,))).astype(BF16)

    @pl.when(e == HERE - 1)
    def _():
        @pl.loop(0, n_seqs)
        def _(s):
            here = slots_of(s, e)
            pick = jnp.concatenate(
                [(places == pos[k, pl.ds(s, 1), :]).astype(F32).astype(BF16) for k in range(HERE)]
            )
            qy[s] = dot(
                pick, jnp.concatenate([gys[k, here] for k in range(HERE)]), ((0,), (0,))
            ).astype(BF16)
            qh[s] = dot(
                pick, jnp.concatenate([dhs[k, here] for k in range(HERE)]), ((0,), (0,))
            ).astype(BF16)


def experts(h, g, pos, gates, wg, wu, wd):
    n_seqs = h.shape[0]
    rows = n_seqs * CAP
    shape = jax.ShapeDtypeStruct
    whole = pl.BlockSpec(memory_space=pltpu.VMEM)

    def per_expert(a, b):
        return pl.BlockSpec((1, a, b), lambda e: (e, 0, 0))

    return pl.pallas_call(
        experts_kernel,
        name="experts",
        grid=(HERE,),
        out_shape=(
            shape((n_seqs, LENGTH, D), BF16),
            shape((n_seqs, LENGTH, D), BF16),
            shape((HERE, n_seqs, LENGTH), F32),
            shape((HERE, D, FE), BF16),
            shape((HERE, D, FE), BF16),
            shape((HERE, FE, D), BF16),
        ),
        in_specs=[whole] * 4 + [per_expert(D, FE), per_expert(D, FE), per_expert(FE, D)],
        out_specs=(whole, whole, whole, per_expert(D, FE), per_expert(D, FE), per_expert(FE, D)),
        scratch_shapes=[pltpu.VMEM((rows, D), BF16)] * 3
        + [pltpu.VMEM((HERE, rows, D), BF16)] * 2
        + [pltpu.VMEM((rows, FE), BF16)] * 3
        + [pltpu.VMEM((rows, LENGTH), F32)] * 2,
        compiler_params=params(limit=60),
    )(h, g, pos, gates, wg, wu, wd)


def phases(segment):
    length = segment.shape[0]
    places = jnp.arange(length, dtype=jnp.int32)
    same = segment[:, None] == segment[None, :]
    visible = (places[None, :] <= places[:, None]) & same
    offset = jnp.sum(visible.astype(F32), axis=1) - 1.0
    halves = HEAD_DIM // 2
    frequency = jnp.exp(-math.log(ROPE_BASE) * 2.0 * jnp.arange(halves).astype(F32) / HEAD_DIM)
    angles = offset[:, None] * frequency[None, :]
    angles = jnp.concatenate([angles, angles], axis=1)[:, None, :]
    return (jnp.cos(angles), jnp.sin(angles), visible)


def rotate(values, cos_table, sin_table):
    height = values.shape[0]
    per_head = values.reshape(height, -1, HEAD_DIM)
    halves = HEAD_DIM // 2
    turned = jnp.concatenate([-per_head[..., halves:], per_head[..., :halves]], axis=-1)
    return (per_head * cos_table + turned * sin_table).reshape(height, -1)


def slot_table(route_ids):
    length = route_ids.shape[0]
    ids = jnp.arange(EXPERTS, dtype=jnp.int32)
    named = jnp.any(route_ids[None, :, :] == ids[:, None, None], axis=2)
    before = jnp.arange(length)[:, None] < jnp.arange(length)[None, :]
    count = jnp.dot(named.astype(BF16), before.astype(BF16), preferred_element_type=F32)
    return jnp.where(named, count, -1.0)


def normalize(values, gain):
    scale = lax.rsqrt(jnp.mean(values * values, axis=-1, keepdims=True) + EPS)
    normed = values * scale
    return (normed, scale, normed * gain)


def normalize_back(grad_out, normed, scale, gain):
    grad_norm = grad_out * gain
    grad_in = scale * (grad_norm - normed * jnp.mean(grad_norm * normed, axis=-1, keepdims=True))
    return (grad_in, jnp.sum(grad_out * normed, axis=0))


def scores_of(query_low, key_low, visible):
    height = query_low.shape[0]
    query_four = query_low.reshape(height, KV_HEADS, HEADS // KV_HEADS, HEAD_DIM)
    key_three = key_low.reshape(height, KV_HEADS, HEAD_DIM)
    scores = jnp.einsum("qkgd,skd->kgqs", query_four, key_three, preferred_element_type=F32) * ATT_SCALE
    return jnp.where(visible[None, None], scores, NEG)


def attend(query_low, key_low, value_low, visible):
    height = query_low.shape[0]
    scores = scores_of(query_low, key_low, visible)
    highest = jnp.max(scores, axis=-1, keepdims=True)
    log_total = highest + jnp.log(jnp.sum(jnp.exp(scores - highest), axis=-1, keepdims=True))
    attention = jnp.exp(scores - log_total).astype(BF16)
    value_three = value_low.reshape(height, KV_HEADS, HEAD_DIM)
    attended = jnp.einsum("kgqs,skd->qkgd", attention, value_three, preferred_element_type=F32)
    return (attended.reshape(height, -1).astype(BF16), log_total)


def attend_back(query_low, key_low, value_low, visible, log_total, grad_mixed):
    height = query_low.shape[0]
    query_four = query_low.reshape(height, KV_HEADS, HEADS // KV_HEADS, HEAD_DIM)
    key_three = key_low.reshape(height, KV_HEADS, HEAD_DIM)
    value_three = value_low.reshape(height, KV_HEADS, HEAD_DIM)
    attention = jnp.exp(scores_of(query_low, key_low, visible) - log_total)
    attention_low = attention.astype(BF16)
    grad_four = grad_mixed.reshape(height, KV_HEADS, HEADS // KV_HEADS, HEAD_DIM)
    value_grad = jnp.einsum("kgqs,qkgd->skd", attention_low, grad_four, preferred_element_type=F32)
    prob_grad = jnp.einsum("qkgd,skd->kgqs", grad_four, value_three, preferred_element_type=F32)
    inner_prod = jnp.sum(attention * prob_grad, axis=-1, keepdims=True)
    score_grad = (attention * (prob_grad - inner_prod)).astype(BF16)
    query_grad = jnp.einsum("kgqs,skd->qkgd", score_grad, key_three, preferred_element_type=F32) * ATT_SCALE
    key_grad = jnp.einsum("kgqs,qkgd->skd", score_grad, query_four, preferred_element_type=F32) * ATT_SCALE
    return (
        query_grad.reshape(height, -1),
        key_grad.reshape(height, -1),
        value_grad.reshape(height, -1),
    )


def on_device(
    tokens,
    segments,
    routes,
    cotangent,
    attn_gain,
    moe_gain,
    w_query,
    w_key,
    w_value,
    w_output,
    w_router,
    w_gate,
    w_up,
    w_down,
):
    micro = tokens.shape[0]
    rows = micro * LENGTH
    flat = lax.axis_index("fsdp")
    first_expert = (flat // 4) * 4
    segments = segments[:, 0]
    routes = routes[:, 0]
    slots = jax.vmap(slot_table)(routes)
    small = jnp.concatenate(
        [w_router, attn_gain[:, None], moe_gain[:, None], jnp.zeros((32, 94), BF16)], axis=1
    )
    pack = jnp.concatenate([w_query, w_key, w_value, w_output, small], axis=1)
    upstream = cotangent.reshape(rows, D)
    dense, gbuf, sbuf, wgb, wub, wdb = early(
        pack,
        upstream,
        slots.reshape(micro * EXPERTS, LENGTH).astype(BF16),
        w_gate[0],
        w_up[0],
        w_down[0],
    )
    dense = dense.reshape(D, WIDE)
    wq, wk, wv, wo = dense[:, :1024], dense[:, 1024:1536], dense[:, 1536:2048], dense[:, 2048:3072]
    wr = dense[:, 3072:3104]
    gain_one = dense[:, 3104].astype(F32)
    gain_two = dense[:, 3105].astype(F32)

    inputs = tokens.reshape(rows, D).astype(F32)
    cos_table, sin_table, visible = jax.vmap(phases)(segments)

    def split(a):
        return a.reshape((micro, LENGTH) + a.shape[1:])

    def join(a):
        return a.reshape((rows,) + a.shape[2:])

    normed_one, scale_one, hidden_one = normalize(inputs, gain_one)
    hidden_low = hidden_one.astype(BF16)
    query_raw = jnp.dot(hidden_low, wq, preferred_element_type=F32)
    key_raw = jnp.dot(hidden_low, wk, preferred_element_type=F32)
    value_low = jnp.dot(hidden_low, wv, preferred_element_type=F32).astype(BF16)
    query_low = jax.vmap(rotate)(split(query_raw), cos_table, sin_table).astype(BF16)
    key_low = jax.vmap(rotate)(split(key_raw), cos_table, sin_table).astype(BF16)
    mixed, log_total = jax.vmap(attend)(query_low, key_low, split(value_low), visible)
    mixed_low = join(mixed)
    middle = inputs + RESIDUAL * jnp.dot(mixed_low, wo, preferred_element_type=F32)
    normed_two, scale_two, hidden_two = normalize(middle, gain_two)
    routed_low = hidden_two.astype(BF16)
    logits = jnp.dot(routed_low, wr, preferred_element_type=F32)
    by_expert = jnp.swapaxes(split(logits), 1, 2)
    named = slots >= 0
    shifted = jnp.where(named, by_expert, -jnp.inf)
    top = jnp.max(shifted, axis=1, keepdims=True)
    raised = jnp.exp(shifted - top)
    gates = raised / jnp.sum(raised, axis=1, keepdims=True)

    hbuf, gatebuf = route(routed_low, gates.reshape(micro * EXPERTS, LENGTH))

    def mine(buf):
        by_seq = buf.reshape(8 * micro, EXPERTS, LENGTH)
        part = lax.dynamic_slice_in_dim(by_seq, first_expert, HERE, axis=1)
        return jnp.swapaxes(part, 0, 1).astype(F32)

    qy, qh, dg, gg, gu, gd = experts(
        hbuf.reshape(8 * micro, LENGTH, D),
        gbuf.reshape(8 * micro, LENGTH, D),
        mine(sbuf),
        mine(gatebuf),
        wgb,
        wub,
        wdb,
    )
    qg = lax.dynamic_update_slice_in_dim(
        jnp.zeros((8 * micro, EXPERTS, LENGTH), F32), jnp.swapaxes(dg, 0, 1), first_expert, axis=1
    )
    mixture, routed_grad, gate_grad = send_back(
        qy.reshape(8, rows, D), qh.reshape(8, rows, D), qg.reshape(8, micro * EXPERTS, LENGTH)
    )
    grad_gate, grad_up, grad_down = expert_sum(gg, gu, gd)

    result = (middle + RESIDUAL * mixture).astype(BF16)
    gate_grad = gate_grad.reshape(micro, EXPERTS, LENGTH)
    choice = gates * (gate_grad - jnp.sum(gates * gate_grad, axis=1, keepdims=True))
    logit_grad = join(jnp.swapaxes(choice, 1, 2)).astype(BF16)
    router_grad = dot(routed_low, logit_grad, ((0,), (0,)))
    routed_grad = routed_grad + dot(logit_grad, wr, ((1,), (1,)))
    middle_grad, gain_two_grad = normalize_back(routed_grad, normed_two, scale_two, gain_two)
    middle_grad = middle_grad + upstream.astype(F32)
    branch_low = (RESIDUAL * middle_grad).astype(BF16)
    output_grad = dot(mixed_low, branch_low, ((0,), (0,)))
    mixed_grad = dot(branch_low, wo, ((1,), (1,))).astype(BF16)
    query_grad, key_grad, value_grad = jax.vmap(attend_back)(
        query_low, key_low, split(value_low), visible, log_total, split(mixed_grad)
    )
    query_low_grad = join(jax.vmap(rotate)(query_grad, cos_table, -sin_table)).astype(BF16)
    key_low_grad = join(jax.vmap(rotate)(key_grad, cos_table, -sin_table)).astype(BF16)
    value_low_grad = join(value_grad).astype(BF16)
    wq_grad = dot(hidden_low, query_low_grad, ((0,), (0,)))
    wk_grad = dot(hidden_low, key_low_grad, ((0,), (0,)))
    wv_grad = dot(hidden_low, value_low_grad, ((0,), (0,)))
    hidden_grad = (
        dot(query_low_grad, wq, ((1,), (1,)))
        + dot(key_low_grad, wk, ((1,), (1,)))
        + dot(value_low_grad, wv, ((1,), (1,)))
    )
    normed_grad, gain_one_grad = normalize_back(hidden_grad, normed_one, scale_one, gain_one)
    grad_tokens = middle_grad + normed_grad
    grads = jnp.concatenate(
        [
            wq_grad.astype(BF16),
            wk_grad.astype(BF16),
            wv_grad.astype(BF16),
            output_grad.astype(BF16),
            router_grad.astype(BF16),
            gain_one_grad[:, None].astype(BF16),
            gain_two_grad[:, None].astype(BF16),
            jnp.zeros((D, 94), BF16),
        ],
        axis=1,
    )
    summed = dense_sum(grads)
    return (
        result.reshape(micro, 1, LENGTH, D),
        grad_tokens.reshape(micro, 1, LENGTH, D),
        summed[:, 3104],
        summed[:, 3105],
        summed[:, :1024],
        summed[:, 1024:1536],
        summed[:, 1536:2048],
        summed[:, 2048:3072],
        summed[:, 3072:3104],
        grad_gate,
        grad_up,
        grad_down,
    )


def solution(mesh):
    sequences = P(None, ("rep", "fsdp"), None, None)
    placed = (
        sequences,
        P(None, ("rep", "fsdp"), None),
        sequences,
        sequences,
        P("fsdp"),
        P("fsdp"),
        P("fsdp", None),
        P("fsdp", None),
        P("fsdp", None),
        P("fsdp", None),
        P("fsdp", None),
        P("fsdp", None, None),
        P("fsdp", None, None),
        P("fsdp", None, None),
    )
    return jax.shard_map(
        on_device,
        mesh=mesh,
        in_specs=placed,
        out_specs=(sequences, sequences) + placed[4:],
        check_vma=False,
    )
```

time: 1940 us -> 544 us (0.28)
  waiting for transfers between devices: 1230 us -> 0 us
  Pallas kernels: 0 us -> 437 us
  blocking collectives: 306 us -> 0 us
  matrix products: 132 us -> 31.5 us
  starting transfers between devices: 90.4 us -> 0 us
  other arithmetic: 72.8 us -> 14.7 us
  local copies, waits for them, and re-layouts: 81.1 us -> 57.8 us
    reduce_scatter x5 -> x0, waiting for transfers between devices: 770 us -> none  [the longest x1 191 us: reduce_dense(): lax.psum_scatter(grads[5], 'fsdp', scatter_dimension=0, tiled=True)]
    pallas_call x0 -> x6, Pallas kernels: none -> 437 us  [the longest x1 117 us: early(): pl.pallas_call(early_kernel, name='early', out_shape=(shape((2, 4, 4, 32,...]
    all_to_all x8 -> x0, waiting for transfers between devices: 180 us -> none  [the longest x2 57.7 us: on_device(): lax.all_to_all(sending, 'fsdp', split_axis=0, concat_axis=0, tiled=True)]
    unnamed x2 -> x0, blocking collectives: 162 us -> none
    all_gather x4 -> x0, waiting for transfers between devices: 160 us -> none  [the longest x1 69.3 us: fetch_dense(): lax.all_gather(w_query, 'fsdp', axis=0, tiled=True)]
    psum x1 -> x0, waiting for transfers between devices: 120 us -> none  [on_device(): lax.psum((totals[0], totals[1], totals[2], totals[3], totals[4], totals[5...]
    all_gather x1 -> x0, blocking collectives: 107 us -> none  [fetch_dense(): lax.all_gather(w_router, 'fsdp', axis=0, tiled=True)]
    dot_general x52 -> x16, matrix products: 126 us -> 25.9 us  [the longest x10 16.9 us: dot(): return lax.dot_general(a, b, (dims, ((), ())), preferred_element_type=F32)]
  transfers between devices with their start and end apart: 18 -> 0, of which waited for: 16 -> 0; matrix products, arithmetic and copies ran while one was open for 9% -> 0% of each run, Pallas kernels for 0% -> 0%
where the time goes in v1:
time: 544 us; the launch traced here: 543 us
  Pallas kernels  437 us (80%)
  local copies, waits for them, and re-layouts  57.8 us (11%)
  matrix products  31.5 us (6%)
  other arithmetic  14.7 us (3%)
    pallas_call x1, Pallas kernels, early(): pl.pallas_call(early_kernel, name='early', out_shape=(shape((2, 4, 4, 32,...  117 us
    pallas_call x1, Pallas kernels, expert_sum(): pl.pallas_call(expert_sum_kernel, name='expert_sum', out_shape=(shape((2,...  97.3 us
    pallas_call x1, Pallas kernels, experts(): pl.pallas_call(experts_kernel, name='experts', grid=(HERE,), out_shape=(s...  69.8 us
    pallas_call x1, Pallas kernels, send_back(): pl.pallas_call(back_kernel, name='send_back', out_shape=(shape((rows, D),...  67 us
    pallas_call x1, Pallas kernels, dense_sum(): pl.pallas_call(dense_sum_kernel, name='dense_sum', out_shape=jax.ShapeDty...  47.7 us
    pallas_call x1, Pallas kernels, route(): pl.pallas_call(route_kernel, name='route', out_shape=(shape((8,) + h.shap...  38.2 us
    dot_general x10, matrix products, dot(): return lax.dot_general(a, b, (dims, ((), ())), preferred_element_type=F32)  16.9 us
    unnamed x82, local copies, waits for them, and re-layouts  13 us

profile of v1, /device:TPU:1, one launch (start us, length us, event | category | flops | bytes accessed | tf_op | source)
XLA Modules:
  0.0 542.6 jit_solution(8046326050894887821)
XLA Ops:
  3.7 1.7 concatenate.45.pack
  5.4 117.3 %early.1 = (bf16[2,4,4,32,3200]{4,3,2,1,0:T(8,128)(2,1)}, bf16[8,256,1024]{2,1,0:T(8,128)(2,1)}, bf16[8,64,128]{2,1,0:T(8,128)(2,1)}, bf16[4,1024,512]{2,1,0:T(8...) custom-call(bf16[32,3200]{1,0:T(8,128)(2,1)} %concatenate.45.pack, bf16[256,1024]{1,0:T(8,128)(2,1)} %bitcast.288, ...), custom_call_target="tpu_custom_call" | custom-call | tf_op jit(solution)/shard_map/early/pallas_call | solution.py:381
  122.7 2.1 slice_convert_fusion
  125.3 3.1 slice_bitcast_fusion
  128.4 2.9 copy.85
  132.9 0.9 broadcast_multiply_fusion.3
  133.8 1.0 fusion.34
  134.8 1.3 slice_bitcast_fusion.1
  138.8 1.7 convolution_convert_fusion.5
  140.5 0.8 copy.83
  141.3 1.0 reshape_reshape.4
  143.4 3.5 multiply_reduce_fusion.4
  147.6 1.8 copy.150
  149.4 1.4 multiply_convert_fusion.1.h
  151.6 1.8 convolution_bitcast_fusion.3
  153.4 1.6 fusion.26
  155.0 38.2 %route.1 = (bf16[8,256,1024]{2,1,0:T(8,128)(2,1)}, f32[8,64,128]{2,1,0:T(8,128)}) custom-call(bf16[256,1024]{1,0:T(8,128)(2,1)} %copy-done.5, f32[64,128]{1,0:T(8,128)} %bitcast.304), custom_call_target="tpu_custom_call" | custom-call | tf_op jit(solution)/shard_map/route/pallas_call | solution.py:418
  193.2 0.9 constant_dynamic-slice_fusion
  196.0 69.8 %experts.1 = (bf16[16,128,1024]{2,1,0:T(8,128)(2,1)}, bf16[16,128,1024]{2,1,0:T(8,128)(2,1)}, f32[4,16,128]{2,1,0:T(8,128)}, bf16[4,1024,512]{2,1,0:T(8,128)(2,1...) custom-call(bf16[16,128,1024]{2,1,0:T(8,128)(2,1)} %bitcast.266, bf16[16,128,1024]{2,1,0:T(8,128)(2,1)} %bitcast.265, ...), custom_call_target="tpu_custom_call" | custom-call | tf_op jit(solution)/shard_map/experts/pallas_call | solution.py:714
  265.9 97.3 %expert_sum.1 = (f32[2,2,4,64,512]{4,3,2,1,0:T(8,128)}, f32[2,2,4,64,512]{4,3,2,1,0:T(8,128)}, f32[2,2,4,32,1024]{4,3,2,1,0:T(8,128)}) custom-call(bf16[4,2,2,4,64,512]{5,4,3,2,1,0:T(8,128)(2,1)} %bitcast.267, bf16[4,2,2,4,64,512]{5,4,3,2,1,0:T(8,128)(2,1)} %bitcast.268, bf16[4,2,2,4,32,1024]{5,4,3,2,1,0:T(8,128)(2,1)} %bitcast.269), custom_call_target="tpu_custom_call" | custom-call | tf_op jit(solution)/shard_map/expert_sum/pallas_call | solution.py:515
  363.9 67.0 %send_back.1 = (f32[256,1024]{1,0:T(8,128)}, f32[256,1024]{1,0:T(8,128)}, f32[64,128]{1,0:T(8,128)}) custom-call(bf16[8,256,1024]{2,1,0:T(8,128)(2,1)} %bitcast.270, bf16[8,256,1024]{2,1,0:T(8,128)(2,1)} %bitcast.271, f32[8,64,128]{2,1,0:T(8,128)} %bitcast.292), custom_call_target="tpu_custom_call" | custom-call | tf_op jit(solution)/shard_map/send_back/pallas_call | solution.py:451
  431.0 0.9 fusion.31
  432.4 0.8 convolution_convert_fusion.6
  433.3 1.7 copy.111
  435.0 2.9 multiply_reduce_fusion
  437.9 1.2 convert_add_fusion
  439.1 2.0 convolution_convert_fusion
  441.2 3.2 fusion.19
  444.4 3.4 reshape.397
  447.8 3.5 copy.97
  451.4 1.6 fusion.24
  453.2 1.5 convolution_convert_fusion.2
  457.6 1.5 convolution_convert_fusion.3
  460.4 1.2 pad_maximum_fusion
  462.5 2.1 convolution_convert_fusion.1
  467.4 1.6 multiply_reduce_fusion.1
  470.7 10.7 %concatenate.57.grads = bf16[2,4,4,32,3200]{4,3,2,1,0:T(8,128)(2,1)} concatenate(bf16[2,4,4,32,1024]{4,3,2,1,0:T(8,128)(2,1)} %bitcast.248, bf16[2,4,4,32,512]{4,3,2,1,0:T(8,128)(2,1)} %bitcast.277, bf16[2,4,4,32,512]{4,3,2,1,0:T(8,128)(2,1)} %bitcast.276, bf16[2,4,4,32,1024]{4,3,2,1,0:T(8,128)(2,1)S(1)} %bitcast.246, bf16[2,4,4,32,32]{4,3,2,1,0:T(8,128)(2,1)S(1)} %bitcast.289, ...), dimensions={4} | concatenate | bytes 13107200 | tf_op jit(solution)/shard_map/concatenate | solution.py:940
  481.4 47.7 %dense_sum.1 = f32[32,3200]{1,0:T(8,128)} custom-call(bf16[2,4,4,32,3200]{4,3,2,1,0:T(8,128)(2,1)} %concatenate.57.grads), custom_call_target="tpu_custom_call" | custom-call | tf_op jit(solution)/shard_map/dense_sum/pallas_call | solution.py:608
  529.1 1.7 fusion.104
  530.8 1.7 fusion.105
  532.5 1.3 slice.87
  533.8 1.5 slice_reduce_fusion
  535.3 1.3 multiply_add_fusion
  536.6 1.3 copy.220
  537.9 1.0 copy-done.15
  539.0 1.3 copy.221
  540.3 1.0 copy-done.14
  541.3 1.3 copy.222
  (131 shorter events, 23.3 us)
Async XLA Ops:
  1.4 0.8 copy-start.33
  5.4 119.6 %copy-start.4 = (bf16[2,1,128,1024]{3,2,1,0:T(8,128)(2,1)S(1)}, bf16[2,1,128,1024]{3,2,1,0:T(8,128)(2,1)}, u32[]{:S(2)}) copy-start(bf16[2,1,128,1024]{3,2,1,0:T(8,128)(2,1)} %param.14) | copy-start | bytes 1572868
  124.9 13.7 %copy-start.25 = (f32[1024,1]{0,1:T(1,128)}, f32[1024,1]{0,1:T(1,128)S(1)}, u32[]{:S(2)}) copy-start(f32[1024,1]{0,1:T(1,128)S(1)} %copy.149) | copy-start | bytes 12292
  125.1 13.5 %copy-start.31 = (f32[256]{0:T(256)}, f32[256]{0:T(256)S(1)}, u32[]{:S(2)}) copy-start(f32[256]{0:T(256)S(1)} %get-tuple-element.116) | copy-start | bytes 3076
  132.0 0.7 copy-start.29
  136.6 1.0 copy-start.8
  137.3 0.9 copy-start.10
  143.4 3.5 copy-start.12
  150.8 0.8 copy-start.5
  265.9 97.3 %copy-start.28 = (f32[4,16,128]{2,1,0:T(8,128)S(1)}, f32[4,16,128]{2,1,0:T(8,128)}, u32[]{:S(2)}) copy-start(f32[4,16,128]{2,1,0:T(8,128)} %get-tuple-element.42) | copy-start | bytes 98308
  363.2 0.7 copy-start.19
  363.9 67.0 %copy-start.24 = (f32[2,32,128]{2,1,0:T(8,128)S(1)}, f32[2,32,128]{2,1,0:T(8,128)}, u32[]{:S(2)}) copy-start(f32[2,32,128]{2,1,0:T(8,128)} %fusion.26) | copy-start | bytes 98308
  363.9 68.5 %copy-start.6 = (bf16[256,1024]{1,0:T(8,128)(2,1)S(1)}, bf16[256,1024]{1,0:T(8,128)(2,1)}, u32[]{:S(2)}) copy-start(bf16[256,1024]{1,0:T(8,128)(2,1)} %copy-done.5) | copy-start | bytes 1572868
  431.8 0.6 copy-start.23
  434.9 2.9 copy-start.2
  434.9 2.9 copy-start.17
  435.0 2.9 copy-start.21
  435.0 2.9 copy-start.27
  435.0 2.9 copy-start.30
  437.9 1.2 copy-start.13
  439.1 2.0 copy-start
  451.4 3.4 copy-start.7
  455.4 1.0 copy-start.9
  456.4 0.8 copy-start.22
  456.9 2.2 copy-start.11
  460.4 5.5 %slice-start = ((s8[6553600]{0:T(1024)(128)(4,1)}), s8[4194304]{0:T(1024)(128)(4,1)S(1)}, s32[]{:S(2)}) async-start(s8[6553600]{0:T(1024)(128)(4,1)} %bitcast.257), calls=%async_computation | async-start | bytes 8388608
  461.8 4.2 slice-start.1
  466.7 0.7 copy-start.26
  466.7 0.7 copy-start.32
  467.4 2.1 copy-start.34
  467.4 3.3 copy-start.3
  467.4 3.3 copy-start.18
  481.4 53.9 %copy-start.1 = (f32[256,1024]{1,0:T(8,128)S(1)}, f32[256,1024]{1,0:T(8,128)}, u32[]{:S(2)}) copy-start(f32[256,1024]{1,0:T(8,128)} %copy-done) | copy-start | bytes 3145732
  481.4 53.9 %copy-start.20 = (f32[256,1024]{1,0:T(8,128)S(1)}, f32[256,1024]{1,0:T(8,128)}, u32[]{:S(2)}) copy-start(f32[256,1024]{1,0:T(8,128)} %get-tuple-element.129) | copy-start | bytes 3145732
  530.8 5.8 %copy-start.16 = (f32[2,2,4,64,512]{4,3,2,1,0:T(8,128)S(1)}, f32[2,2,4,64,512]{4,3,2,1,0:T(8,128)}, u32[]{:S(2)}) copy-start(f32[2,2,4,64,512]{4,3,2,1,0:T(8,128)} %get-tuple-element.49) | copy-start | bytes 6291460
  536.6 2.3 copy-start.15
  539.0 2.3 copy-start.14

commit v2 on v1

--- a/solution.py
+++ b/solution.py
@@ -94,6 +94,11 @@
     def drain(self):
         for copy in self.copies:
             copy.wait_send()
+
+
+def step(*chains):
+    for chain in chains:
+        next(chain, None)
 
 
 def greet(partners):
@@ -241,14 +246,14 @@
 
     @pl.loop(0, n)
     def _(j):
-        arr[ahead, 0, j] = (arr[ahead, 0, j].astype(F32) + hl[j].astype(F32)).astype(arr.dtype)
+        arr[ahead, 0, j] = arr[ahead, 0, j] + hl[j]
 
     e = lines.send(arr.at[ahead, 0], fl.at[0], right)
     b.wait_recv()
 
     @pl.loop(0, n)
     def _(j):
-        arr[behind, 1, j] = (arr[behind, 1, j].astype(F32) + hr[j].astype(F32)).astype(arr.dtype)
+        arr[behind, 1, j] = arr[behind, 1, j] + hr[j]
 
     f = lines.send(arr.at[behind, 1], fr.at[1], left)
     yield
@@ -265,8 +270,87 @@
             )
 
 
-def early_kernel(
-    pack, g, slots, wg, wu, wd, dense, gbuf, sbuf, wgb, wub, wdb, send_sems, recv_sems, local_sems
+def dot(a, b, dims=((1,), (0,))):
+    return lax.dot_general(a, b, (dims, ((), ())), preferred_element_type=F32)
+
+
+def lanes():
+    return lax.broadcasted_iota(jnp.int32, (1, 128), 1)
+
+
+def swap_halves(u):
+    return jnp.where(
+        lax.rem(lanes(), 64) < 32, pltpu.roll(u, 96, axis=1), pltpu.roll(u, 32, axis=1)
+    )
+
+
+def doubled(tile, odd):
+    wide = tile.astype(F32)
+    turned = pltpu.roll(wide, 64, axis=1)
+    low = lanes() < 64
+    return jnp.where(low, turned if odd else wide, wide if odd else turned).astype(BF16)
+
+
+def stacked(pair):
+    wide = pair.astype(F32)
+    low = lanes() < 64
+    return jnp.concatenate([jnp.where(low, wide, 0.0), jnp.where(low, 0.0, wide)]).astype(BF16)
+
+
+def side_by_side(both):
+    return jnp.where(lanes() < 64, both[:128], both[128:])
+
+
+def folded(even, odd):
+    even = even + pltpu.roll(even, 64, axis=1)
+    odd = odd + pltpu.roll(odd, 64, axis=1)
+    return jnp.where(lanes() < 64, even, odd)
+
+
+def norm_scale(values):
+    return lax.rsqrt(jnp.mean(values * values, axis=1, keepdims=True) + EPS)
+
+
+def gain_rows(small):
+    row = lax.broadcasted_iota(jnp.int32, (8, 128), 0)
+    lane = lax.broadcasted_iota(jnp.int32, (8, 128), 1)
+    pick = (lane == row + EXPERTS).astype(F32).astype(BF16)
+    rows = dot(pick, small, ((1,), (1,)))
+    return rows[0:1], rows[1:2]
+
+
+def column_sums(values, column):
+    rows = values.shape[0]
+    pick = (lax.broadcasted_iota(jnp.int32, (rows, 128), 1) == column).astype(F32).astype(BF16)
+    upper = values.astype(BF16)
+    lower = (values - upper.astype(F32)).astype(BF16)
+    return dot(upper, pick, ((0,), (0,))) + dot(lower, pick, ((0,), (0,)))
+
+
+def anywhere(n):
+    return [pl.BlockSpec(memory_space=pl.ANY)] * n
+
+
+def vmem(n):
+    return [pl.BlockSpec(memory_space=pltpu.VMEM)] * n
+
+
+def sems(n):
+    return [pltpu.SemaphoreType.DMA((n,)), pltpu.SemaphoreType.DMA((n,))]
+
+
+def params(number=None, limit=56):
+    if number is None:
+        return pltpu.CompilerParams(vmem_limit_bytes=limit << 20)
+    return pltpu.CompilerParams(
+        collective_id=number, has_side_effects=True, vmem_limit_bytes=limit << 20
+    )
+
+
+def front_kernel(
+    tokens, cos, sin, keep, slots, pack, g, wg, wu, wd,
+    dense, gbuf, sbuf, wgb, wub, wdb, hbuf, gatebuf, q, k, v, p, o, y1, gates,
+    dn, h, send_sems, recv_sems, local_sems,
 ):
     me = Place()
     right, left, above, below = me.right(), me.left(), me.above(), me.below()
@@ -274,7 +358,7 @@
     rows = pl.ds(pl.multiple_of(me.core * 16, 16), 16)
     own = me.high * 4 + me.x
     local = [
-        pltpu.make_async_copy(pack.at[rows], dense.at[me.high, me.x, me.z, rows], local_sems.at[0]),
+        pltpu.make_async_copy(pack.at[rows], dn.at[me.high, me.x, me.z, rows], local_sems.at[0]),
         pltpu.make_async_copy(g, gbuf.at[own], local_sems.at[1]),
         pltpu.make_async_copy(slots, sbuf.at[own], local_sems.at[2]),
         pltpu.make_async_copy(wg, wgb.at[me.z], local_sems.at[3]),
@@ -290,13 +374,13 @@
     def dense_chain(columns, x_first):
         def on_z(p, k=None):
             if x_first:
-                return dense.at[slice(None) if k is None else k, :, p, rows, columns]
-            return dense.at[slice(None) if k is None else k, me.x, p, rows, columns]
+                return dn.at[slice(None) if k is None else k, :, p, rows, columns]
+            return dn.at[slice(None) if k is None else k, me.x, p, rows, columns]
 
         def on_x(p, k=None):
             if x_first:
-                return dense.at[slice(None) if k is None else k, p, me.z, rows, columns]
-            return dense.at[slice(None) if k is None else k, p, :, rows, columns]
+                return dn.at[slice(None) if k is None else k, p, me.z, rows, columns]
+            return dn.at[slice(None) if k is None else k, p, :, rows, columns]
 
         if x_first:
             first = (on_x(me.x), on_x, on_x, me.x, right, left)
@@ -337,93 +421,135 @@
             spread=spread,
         )
 
-    swap = lines.send(pack.at[rows], dense.at[me.high, me.x, me.z, rows], cross)
+    swap = lines.send(pack.at[rows], dn.at[me.high, me.x, me.z, rows], cross)
     local[0].wait()
     swap.wait_recv()
-    drive(
-        dense_chain(pl.ds(0, CUT), False),
-        dense_chain(pl.ds(CUT, WIDE - CUT), True),
-        group_gather(lines, me, g, gbuf),
-        group_gather(lines, me, slots, sbuf),
-        weight_chain(wg, wgb),
-        weight_chain(wu, wub),
-        weight_chain(wd, wdb),
-    )
+    gs = group_gather(lines, me, g, gbuf)
+    ss = group_gather(lines, me, slots, sbuf)
+    w1, w2, w3 = weight_chain(wg, wgb), weight_chain(wu, wub), weight_chain(wd, wdb)
+    drive(dense_chain(pl.ds(0, CUT), False), dense_chain(pl.ds(CUT, WIDE - CUT), True))
     for copy in shared:
         copy.wait_recv()
-    for copy in local[1:]:
+    del shared[:]
+    step(gs, ss, w1)
+    keeping = pltpu.make_async_copy(dn, dense, local_sems.at[6])
+    keeping.start()
+
+    def weight(start, size):
+        return dn[:, :, :, :, start : start + size].reshape(D, size)
+
+    small = weight(3072, 128)
+    gain_one, gain_two = gain_rows(small)
+    x = tokens[...].astype(F32)
+    h[...] = (x * norm_scale(x) * gain_one).astype(BF16)
+    for piece in range(4):
+        raw = dot(h[...], weight(piece * 256, 256))
+        for t in range(2):
+            u = raw[:, t * 128 : t * 128 + 128]
+            q[:, piece * 256 + t * 128 : piece * 256 + t * 128 + 128] = (
+                u * cos[...] + swap_halves(u) * sin[...]
+            ).astype(BF16)
+    for piece in range(2):
+        raw = dot(h[...], weight(1024 + piece * 256, 256))
+        for t in range(2):
+            u = raw[:, t * 128 : t * 128 + 128]
+            k[:, piece * 256 + t * 128 : piece * 256 + t * 128 + 128] = (
+                u * cos[...] + swap_halves(u) * sin[...]
+            ).astype(BF16)
+    v[...] = dot(h[...], weight(1536, 512)).astype(BF16)
+    step(w2)
+
+    def attend(i):
+        s, m = lax.div(i, 4), lax.rem(i, 4)
+        here = pl.ds(pl.multiple_of(s * 128, 128), 128)
+        column = pl.ds(pl.multiple_of(m * 128, 128), 128)
+        seen = keep[s]
+        seen = jnp.concatenate([seen, seen]) > 0.0
+        k_tile, v_tile = k[here, column], v[here, column]
+        for odd in range(2):
+            q_column = pl.ds(pl.multiple_of(m * 256 + odd * 128, 128), 128)
+            scores = dot(stacked(q[here, q_column]), doubled(k_tile, odd), ((1,), (1,))) * ATT_SCALE
+            scores = jnp.where(seen, scores, NEG)
+            raised = jnp.exp(scores - jnp.max(scores, axis=1, keepdims=True))
+            probs = raised / jnp.sum(raised, axis=1, keepdims=True)
+            p[i, odd] = probs
+            both = dot(probs.astype(BF16), doubled(v_tile, odd))
+            o[here, q_column] = side_by_side(both).astype(BF16)
+
+    for part in range(4):
+
+        @pl.loop(part * 2, part * 2 + 2)
+        def _(i):
+            attend(i)
+
+        if part == 1:
+            step(w1)
+        if part == 2:
+            step(gs, ss)
+        if part == 3:
+            step(w3)
+
+    middle = tokens[...].astype(F32) + RESIDUAL * dot(o[...], weight(2048, 1024))
+    y1[...] = middle
+    h[...] = (middle * norm_scale(middle) * gain_two).astype(BF16)
+    logits = dot(small, h[...], ((0,), (1,)))[:EXPERTS]
+    named = slots[...] >= 0.0
+    top = jnp.max(jnp.where(named, logits, -jnp.inf), axis=0, keepdims=True)
+    raised = jnp.where(named, jnp.exp(jnp.where(named, logits - top, 0.0)), 0.0)
+    gates[...] = raised / jnp.sum(raised, axis=0, keepdims=True)
+
+    late = [
+        pltpu.make_async_copy(h, hbuf.at[own], local_sems.at[7]),
+        pltpu.make_async_copy(gates, gatebuf.at[own], local_sems.at[8]),
+    ]
+    for copy in late:
+        copy.start()
+    drive(
+        group_gather(lines, me, h, hbuf),
+        group_gather(lines, me, gates, gatebuf),
+        gs,
+        ss,
+        w1,
+        w2,
+        w3,
+    )
+    for copy in shared:
+        copy.wait_recv()
+    for copy in local[1:] + [keeping] + late:
         copy.wait()
     lines.drain()
 
 
-def anywhere(n):
-    return [pl.BlockSpec(memory_space=pl.ANY)] * n
-
-
-def vmem(n):
-    return [pl.BlockSpec(memory_space=pltpu.VMEM)] * n
-
-
-def sems(n):
-    return [pltpu.SemaphoreType.DMA((n,)), pltpu.SemaphoreType.DMA((n,))]
-
-
-def params(number=None, limit=56):
-    if number is None:
-        return pltpu.CompilerParams(vmem_limit_bytes=limit << 20)
-    return pltpu.CompilerParams(
-        collective_id=number, has_side_effects=True, vmem_limit_bytes=limit << 20
-    )
-
-
-def early(pack, g, slots, wg, wu, wd):
+def front(tokens, cos, sin, keep, slots, pack, g, wg, wu, wd):
     shape = jax.ShapeDtypeStruct
+    rows = tokens.shape[0]
     return pl.pallas_call(
-        early_kernel,
-        name="early",
+        front_kernel,
+        name="front",
         out_shape=(
             shape((2, 4, 4, 32, WIDE), BF16),
             shape((8,) + g.shape, BF16),
-            shape((8,) + slots.shape, BF16),
+            shape((8,) + slots.shape, F32),
             shape((4,) + wg.shape, BF16),
             shape((4,) + wu.shape, BF16),
             shape((4,) + wd.shape, BF16),
+            shape((8, rows, D), BF16),
+            shape((8, EXPERTS, rows), F32),
+            shape((rows, 1024), BF16),
+            shape((rows, 512), BF16),
+            shape((rows, 512), BF16),
+            shape((8, 2, 256, 128), F32),
+            shape((rows, 1024), BF16),
+            shape((rows, D), F32),
+            shape((EXPERTS, rows), F32),
         ),
-        in_specs=anywhere(6),
-        out_specs=anywhere(6),
-        scratch_shapes=sems(72) + [pltpu.SemaphoreType.DMA((6,))],
+        in_specs=vmem(6) + anywhere(4),
+        out_specs=anywhere(8) + vmem(7),
+        scratch_shapes=[pltpu.VMEM((2, 4, 4, 32, WIDE), BF16), pltpu.VMEM((rows, D), BF16)]
+        + sems(88)
+        + [pltpu.SemaphoreType.DMA((9,))],
         compiler_params=params(0),
-    )(pack, g, slots, wg, wu, wd)
-
-
-def route_kernel(h, gates, hbuf, gbuf, send_sems, recv_sems, local_sems):
-    me = Place()
-    own = me.high * 4 + me.x
-    local = [
-        pltpu.make_async_copy(h, hbuf.at[own], local_sems.at[0]),
-        pltpu.make_async_copy(gates, gbuf.at[own], local_sems.at[1]),
-    ]
-    for copy in local:
-        copy.start()
-    greet((me.right(), me.left(), me.cross()))
-    lines = Lines(send_sems, recv_sems)
-    drive(group_gather(lines, me, h, hbuf), group_gather(lines, me, gates, gbuf))
-    for copy in local:
-        copy.wait()
-    lines.drain()
-
-
-def route(h, gates):
-    shape = jax.ShapeDtypeStruct
-    return pl.pallas_call(
-        route_kernel,
-        name="route",
-        out_shape=(shape((8,) + h.shape, h.dtype), shape((8,) + gates.shape, gates.dtype)),
-        in_specs=anywhere(2),
-        out_specs=anywhere(2),
-        scratch_shapes=sems(24) + [pltpu.SemaphoreType.DMA((2,))],
-        compiler_params=params(1),
-    )(h, gates)
+    )(tokens, cos, sin, keep, slots, pack, g, wg, wu, wd)
 
 
 def scatter_scratch(rows, columns, dtype):
@@ -432,7 +558,7 @@
     return [full] * 5 + [half] * 4 + [full] * 3
 
 
-def back_kernel(qy, qh, qg, y, dh, dg, *scratch):
+def back_kernel(qh, qg, dh, dg, *scratch):
     me = Place()
     send_sems, recv_sems = scratch[:2]
     greet((me.right(), me.left(), me.cross()))
@@ -440,99 +566,188 @@
     drive(
         group_scatter(lines, me, qg, dg, *scratch[2:14]),
         group_scatter(lines, me, qh, dh, *scratch[14:26]),
-        group_scatter(lines, me, qy, y, *scratch[26:38]),
     )
     lines.drain()
 
 
-def send_back(qy, qh, qg):
+def send_back(qh, qg):
     shape = jax.ShapeDtypeStruct
-    rows = qy.shape[1]
+    rows = qh.shape[1]
     return pl.pallas_call(
         back_kernel,
         name="send_back",
-        out_shape=(shape((rows, D), F32), shape((rows, D), F32), shape(qg.shape[1:], F32)),
-        in_specs=vmem(3),
-        out_specs=vmem(3),
+        out_shape=(shape((rows, D), F32), shape(qg.shape[1:], F32)),
+        in_specs=vmem(2),
+        out_specs=vmem(2),
         scratch_shapes=sems(36)
         + scatter_scratch(qg.shape[1], qg.shape[2], F32)
-        + scatter_scratch(rows, D, BF16)
         + scatter_scratch(rows, D, BF16),
-        compiler_params=params(2),
-    )(qy, qh, qg)
-
-
-def expert_sum_kernel(gg, gu, gd, og, ou, od, *scratch):
+        compiler_params=params(1),
+    )(qh, qg)
+
+
+def retreat_kernel(
+    tokens, cos, sin, gates, dense, g, y1, q, k, v, p, o, dh, dg, qy, gg, gu, gd,
+    grads, grad_tokens, result, tg, tu, td,
+    h, do, dq, dk, dv, small_grad, mixture, *scratch,
+):
     me = Place()
-    send_sems, recv_sems = scratch[:2]
-    above, below, twin, sibling = me.above(), me.below(), me.twin(), me.sibling()
-    greet((above, below, twin, sibling))
+    send_sems, recv_sems, local_sems = scratch[:3]
+    above, below, sibling = me.above(), me.below(), me.sibling()
+    local = []
+    for i, (grad, acc) in enumerate(((gg, scratch[4]), (gu, scratch[10]), (gd, scratch[16]))):
+        local.append(pltpu.make_async_copy(grad.at[:, me.core], acc, local_sems.at[i]))
+        local[-1].start()
+    greet((me.right(), me.left(), me.cross(), above, below, sibling))
     lines = Lines(send_sems, recv_sems)
 
-    def chain(grad, out, rc, acc, hl, hr, fl, fr, tot, yb):
+    def chain(grad, tot, mine, rc, acc, hl, hr, fl, fr):
         first = lines.send(grad.at[:, 1 - me.core], rc, sibling)
         yield
+        mine.wait()
         first.wait_recv()
 
         @pl.loop(0, 32)
         def _(i):
-            p, k, j = lax.div(i, 8), lax.rem(lax.div(i, 4), 2), lax.rem(i, 4)
-            acc[p, k, j] = (
-                grad[p, me.core, k, j].astype(F32) + rc[p, k, j].astype(F32)
-            ).astype(BF16)
-
-        def store(k, j, value):
-            tot[k, j] = value.astype(BF16)
+            a, b, j = lax.div(i, 8), lax.rem(lax.div(i, 4), 2), lax.rem(i, 4)
+            acc[a, b, j] = acc[a, b, j] + rc[a, b, j]
+
+        def store(b, j, value):
+            tot[b, j] = value.astype(BF16)
 
         yield from ring_scatter(lines, acc, me.z, above, below, hl, hr, fl, fr, store)
-        second = lines.send(tot, yb, twin)
-        yield
-        second.wait_recv()
-        for k in range(2):
-
-            @pl.loop(0, 4)
-            def _(j, k=k):
-                out[me.core, k, j] = tot[k, j].astype(F32) + yb[k, j].astype(F32)
-
-        last = lines.send(out.at[me.core], out.at[me.core], sibling)
-        yield
-        last.wait_recv()
-
-    drive(
-        chain(gg, og, *scratch[2:10]),
-        chain(gu, ou, *scratch[10:18]),
-        chain(gd, od, *scratch[18:26]),
-    )
+
+    e1 = chain(gg, tg, local[0], *scratch[3:9])
+    e2 = chain(gu, tu, local[1], *scratch[9:15])
+    e3 = chain(gd, td, local[2], *scratch[15:21])
+    ys = group_scatter(lines, me, qy, mixture, *scratch[21:33])
+    step(e1, e2, e3, ys)
+
+    small = dense[:, 3072:3200]
+    gain_one, gain_two = gain_rows(small)
+    x = tokens[...].astype(F32)
+    h[...] = (x * norm_scale(x) * gain_one).astype(BF16)
+    middle = y1[...]
+    scale = norm_scale(middle)
+    normed = middle * scale
+    routed = (normed * gain_two).astype(BF16)
+    inner = jnp.sum(gates[...] * dg[...], axis=0, keepdims=True)
+    choice = gates[...] * (dg[...] - inner)
+    by_token = jnp.transpose(
+        jnp.concatenate([choice, jnp.zeros((128 - EXPERTS, choice.shape[1]), F32)])
+    ).astype(BF16)
+    dh2 = dh[...] + dot(by_token, small, ((1,), (1,)))
+    small_grad[...] = dot(routed, by_token, ((0,), (0,))) + column_sums(dh2 * normed, EXPERTS + 1)
+    dn = dh2 * gain_two
+    dy = g[...].astype(F32) + scale * (dn - normed * jnp.mean(dn * normed, axis=1, keepdims=True))
+    grad_tokens[...] = dy
+    dz = (RESIDUAL * dy).astype(BF16)
+    step(e1)
+    for t in range(4):
+        here = slice(t * 256, t * 256 + 256)
+        grads[here, 2048:3072] = dot(o[:, here], dz, ((0,), (0,))).astype(BF16)
+    do[...] = dot(dz, dense[:, 2048:3072], ((1,), (1,))).astype(BF16)
+    step(e2)
+
+    def attend_back(i):
+        s, m = lax.div(i, 4), lax.rem(i, 4)
+        here = pl.ds(pl.multiple_of(s * 128, 128), 128)
+        column = pl.ds(pl.multiple_of(m * 128, 128), 128)
+        cos_s, sin_s = cos[here], sin[here]
+        k_tile, v_tile = k[here, column], v[here, column]
+        dk_both, dv_both = [], []
+        for odd in range(2):
+            q_column = pl.ds(pl.multiple_of(m * 256 + odd * 128, 128), 128)
+            q_two, do_two = stacked(q[here, q_column]), stacked(do[here, q_column])
+            probs = p[i, odd]
+            dp = dot(do_two, doubled(v_tile, odd), ((1,), (1,)))
+            inner = jnp.sum(probs * dp, axis=1, keepdims=True)
+            ds = (probs * (dp - inner)).astype(BF16)
+            dv_both.append(dot(probs.astype(BF16), do_two, ((0,), (0,))))
+            dk_both.append(dot(ds, q_two, ((0,), (0,))) * ATT_SCALE)
+            u = side_by_side(dot(ds, doubled(k_tile, odd))) * ATT_SCALE
+            dq[here, q_column] = (u * cos_s - swap_halves(u) * sin_s).astype(BF16)
+        u = folded(*dk_both)
+        dk[here, column] = (u * cos_s - swap_halves(u) * sin_s).astype(BF16)
+        dv[here, column] = folded(*dv_both).astype(BF16)
+
+    for part in range(4):
+
+        @pl.loop(part * 2, part * 2 + 2)
+        def _(i):
+            attend_back(i)
+
+        step((e3, ys, e1, e2)[part])
+
+    for t in range(4):
+        here = slice(t * 256, t * 256 + 256)
+        grads[here, 0:1024] = dot(h[:, here], dq[...], ((0,), (0,))).astype(BF16)
+        grads[here, 1024:1536] = dot(h[:, here], dk[...], ((0,), (0,))).astype(BF16)
+        grads[here, 1536:2048] = dot(h[:, here], dv[...], ((0,), (0,))).astype(BF16)
+    dh1 = (
+        dot(dq[...], dense[:, 0:1024], ((1,), (1,)))
+        + dot(dk[...], dense[:, 1024:1536], ((1,), (1,)))
+        + dot(dv[...], dense[:, 1536:2048], ((1,), (1,)))
+    )
+    step(e3, ys)
+    x = tokens[...].astype(F32)
+    scale = norm_scale(x)
+    normed = x * scale
+    grads[:, 3072:3200] = (small_grad[...] + column_sums(dh1 * normed, EXPERTS)).astype(BF16)
+    dn = dh1 * gain_one
+    grad_tokens[...] += scale * (dn - normed * jnp.mean(dn * normed, axis=1, keepdims=True))
+    drive(ys, e1, e2, e3)
+    result[...] = (y1[...] + RESIDUAL * mixture[...]).astype(BF16)
     lines.drain()
 
 
-def expert_sum(gg, gu, gd):
+def halves(r, w):
+    return (4, 2, 2, 4, r, w)
+
+
+def retreat(tokens, cos, sin, gates, dense, g, y1, q, k, v, p, o, dh, dg, qy, gg, gu, gd):
     def scratch(r, w):
-        shapes = [(4, 2, 4, r, w)] * 2 + [(4, r, w)] * 2 + [(2, 4, r, w)] * 4
+        shapes = [(4, 2, 4, r, w)] * 2 + [(4, r, w)] * 2 + [(2, 4, r, w)] * 2
         return [pltpu.VMEM(s, BF16) for s in shapes]
 
     shape = jax.ShapeDtypeStruct
-    outs = pl.pallas_call(
-        expert_sum_kernel,
-        name="expert_sum",
+    rows = tokens.shape[0]
+    return pl.pallas_call(
+        retreat_kernel,
+        name="retreat",
         out_shape=(
-            shape((2, 2, 4, 64, 512), F32),
-            shape((2, 2, 4, 64, 512), F32),
-            shape((2, 2, 4, 32, 1024), F32),
+            shape((D, WIDE), BF16),
+            shape((rows, D), F32),
+            shape((rows, D), BF16),
+            shape((2, 4, 64, 512), BF16),
+            shape((2, 4, 64, 512), BF16),
+            shape((2, 4, 32, 1024), BF16),
         ),
-        in_specs=vmem(3),
-        out_specs=vmem(3),
-        scratch_shapes=sems(30) + scratch(64, 512) + scratch(64, 512) + scratch(32, 1024),
-        compiler_params=params(3, 58),
+        in_specs=vmem(15) + anywhere(3),
+        out_specs=vmem(6),
+        scratch_shapes=[
+            pltpu.VMEM((rows, D), BF16),
+            pltpu.VMEM((rows, 1024), BF16),
+            pltpu.VMEM((rows, 1024), BF16),
+            pltpu.VMEM((rows, 512), BF16),
+            pltpu.VMEM((rows, 512), BF16),
+            pltpu.VMEM((D, 128), F32),
+            pltpu.VMEM((rows, D), F32),
+        ]
+        + sems(40)
+        + [pltpu.SemaphoreType.DMA((3,))]
+        + scratch(64, 512)
+        + scratch(64, 512)
+        + scratch(32, 1024)
+        + scatter_scratch(rows, D, BF16),
+        compiler_params=params(2, 60),
     )(
-        gg.reshape(4, 2, 2, 4, 64, 512),
-        gu.reshape(4, 2, 2, 4, 64, 512),
-        gd.reshape(4, 2, 2, 4, 32, 1024),
-    )
-    return outs[0].reshape(1, D, FE), outs[1].reshape(1, D, FE), outs[2].reshape(1, FE, D)
-
-
-def dense_sum_kernel(grads, out, rc, *scratch):
+        tokens, cos, sin, gates, dense, g, y1, q, k, v, p, o, dh, dg, qy,
+        gg.reshape(halves(64, 512)), gu.reshape(halves(64, 512)), gd.reshape(halves(32, 1024)),
+    )
+
+
+def settle_kernel(grads, tg, tu, td, out, og, ou, od, rc, *scratch):
     me = Place()
     send_sems, recv_sems = scratch[:2]
     right, left, above, below = me.right(), me.left(), me.above(), me.below()
@@ -542,7 +757,6 @@
     mine = pl.ds(pl.multiple_of(me.core * 16, 16), 16)
     theirs = pl.ds(pl.multiple_of((1 - me.core) * 16, 16), 16)
     swap = lines.send(grads.at[:, :, :, theirs], rc, sibling)
-    swap.wait_recv()
 
     def chain(columns, x_first, acc, second, hl, hr, fl, fr, hl2, hr2, fl2, fr2, r2, ry, r3, yb):
         @pl.loop(0, 32)
@@ -578,14 +792,32 @@
         yield
         c.wait_recv()
 
+    def swapped(tot, whole, other):
+        a = lines.send(tot, other, twin)
+        yield
+        a.wait_recv()
+        for k in range(2):
+
+            @pl.loop(0, 4)
+            def _(j, k=k):
+                whole[me.core, k, j] = tot[k, j].astype(F32) + other[k, j].astype(F32)
+
+        b = lines.send(whole.at[me.core], whole.at[me.core], sibling)
+        yield
+        b.wait_recv()
+
+    others = [swapped(t, w, s) for t, w, s in zip((tg, tu, td), (og, ou, od), scratch[30:33])]
+    step(*others)
+    swap.wait_recv()
     drive(
         chain(pl.ds(0, CUT), True, *scratch[2:16]),
         chain(pl.ds(CUT, WIDE - CUT), False, *scratch[16:30]),
     )
+    drive(*others)
     lines.drain()
 
 
-def dense_sum(grads):
+def settle(grads, tg, tu, td):
     def scratch(w):
         shapes = [
             (4, 2, 4, 16, w),
@@ -605,22 +837,25 @@
         ]
         return [pltpu.VMEM(s, BF16) for s in shapes]
 
+    shape = jax.ShapeDtypeStruct
     return pl.pallas_call(
-        dense_sum_kernel,
-        name="dense_sum",
-        out_shape=jax.ShapeDtypeStruct((32, WIDE), F32),
-        in_specs=vmem(1),
-        out_specs=pl.BlockSpec(memory_space=pltpu.VMEM),
+        settle_kernel,
+        name="settle",
+        out_shape=(
+            shape((32, WIDE), F32),
+            shape((2, 2, 4, 64, 512), F32),
+            shape((2, 2, 4, 64, 512), F32),
+            shape((2, 2, 4, 32, 1024), F32),
+        ),
+        in_specs=vmem(4),
+        out_specs=vmem(4),
         scratch_shapes=[pltpu.VMEM((2, 4, 4, 16, WIDE), BF16)]
-        + sems(40)
+        + sems(48)
         + scratch(CUT)
-        + scratch(WIDE - CUT),
-        compiler_params=params(4),
-    )(grads.reshape(2, 4, 4, 32, WIDE))
-
-
-def dot(a, b, dims=((1,), (0,))):
-    return lax.dot_general(a, b, (dims, ((), ())), preferred_element_type=F32)
+        + scratch(WIDE - CUT)
+        + [pltpu.VMEM(t.shape, BF16) for t in (tg, tu, td)],
+        compiler_params=params(3),
+    )(grads.reshape(2, 4, 4, 32, WIDE), tg, tu, td)
 
 
 def experts_kernel(
@@ -742,16 +977,12 @@
     halves = HEAD_DIM // 2
     frequency = jnp.exp(-math.log(ROPE_BASE) * 2.0 * jnp.arange(halves).astype(F32) / HEAD_DIM)
     angles = offset[:, None] * frequency[None, :]
-    angles = jnp.concatenate([angles, angles], axis=1)[:, None, :]
-    return (jnp.cos(angles), jnp.sin(angles), visible)
-
-
-def rotate(values, cos_table, sin_table):
-    height = values.shape[0]
-    per_head = values.reshape(height, -1, HEAD_DIM)
-    halves = HEAD_DIM // 2
-    turned = jnp.concatenate([-per_head[..., halves:], per_head[..., :halves]], axis=-1)
-    return (per_head * cos_table + turned * sin_table).reshape(height, -1)
+    cos, sin = jnp.cos(angles), jnp.sin(angles)
+    return (
+        jnp.concatenate([cos] * 4, axis=1),
+        jnp.concatenate([-sin, sin] * 2, axis=1),
+        visible.astype(F32),
+    )
 
 
 def slot_table(route_ids):
@@ -761,58 +992,6 @@
     before = jnp.arange(length)[:, None] < jnp.arange(length)[None, :]
     count = jnp.dot(named.astype(BF16), before.astype(BF16), preferred_element_type=F32)
     return jnp.where(named, count, -1.0)
-
-
-def normalize(values, gain):
-    scale = lax.rsqrt(jnp.mean(values * values, axis=-1, keepdims=True) + EPS)
-    normed = values * scale
-    return (normed, scale, normed * gain)
-
-
-def normalize_back(grad_out, normed, scale, gain):
-    grad_norm = grad_out * gain
-    grad_in = scale * (grad_norm - normed * jnp.mean(grad_norm * normed, axis=-1, keepdims=True))
-    return (grad_in, jnp.sum(grad_out * normed, axis=0))
-
-
-def scores_of(query_low, key_low, visible):
-    height = query_low.shape[0]
-    query_four = query_low.reshape(height, KV_HEADS, HEADS // KV_HEADS, HEAD_DIM)
-    key_three = key_low.reshape(height, KV_HEADS, HEAD_DIM)
-    scores = jnp.einsum("qkgd,skd->kgqs", query_four, key_three, preferred_element_type=F32) * ATT_SCALE
-    return jnp.where(visible[None, None], scores, NEG)
-
-
-def attend(query_low, key_low, value_low, visible):
-    height = query_low.shape[0]
-    scores = scores_of(query_low, key_low, visible)
-    highest = jnp.max(scores, axis=-1, keepdims=True)
-    log_total = highest + jnp.log(jnp.sum(jnp.exp(scores - highest), axis=-1, keepdims=True))
-    attention = jnp.exp(scores - log_total).astype(BF16)
-    value_three = value_low.reshape(height, KV_HEADS, HEAD_DIM)
-    attended = jnp.einsum("kgqs,skd->qkgd", attention, value_three, preferred_element_type=F32)
-    return (attended.reshape(height, -1).astype(BF16), log_total)
-
-
-def attend_back(query_low, key_low, value_low, visible, log_total, grad_mixed):
-    height = query_low.shape[0]
-    query_four = query_low.reshape(height, KV_HEADS, HEADS // KV_HEADS, HEAD_DIM)
-    key_three = key_low.reshape(height, KV_HEADS, HEAD_DIM)
-    value_three = value_low.reshape(height, KV_HEADS, HEAD_DIM)
-    attention = jnp.exp(scores_of(query_low, key_low, visible) - log_total)
-    attention_low = attention.astype(BF16)
-    grad_four = grad_mixed.reshape(height, KV_HEADS, HEADS // KV_HEADS, HEAD_DIM)
-    value_grad = jnp.einsum("kgqs,qkgd->skd", attention_low, grad_four, preferred_element_type=F32)
-    prob_grad = jnp.einsum("qkgd,skd->kgqs", grad_four, value_three, preferred_element_type=F32)
-    inner_prod = jnp.sum(attention * prob_grad, axis=-1, keepdims=True)
-    score_grad = (attention * (prob_grad - inner_prod)).astype(BF16)
-    query_grad = jnp.einsum("kgqs,skd->qkgd", score_grad, key_three, preferred_element_type=F32) * ATT_SCALE
-    key_grad = jnp.einsum("kgqs,qkgd->skd", score_grad, query_four, preferred_element_type=F32) * ATT_SCALE
-    return (
-        query_grad.reshape(height, -1),
-        key_grad.reshape(height, -1),
-        value_grad.reshape(height, -1),
-    )
 
 
 def on_device(
@@ -833,65 +1012,23 @@
 ):
     micro = tokens.shape[0]
     rows = micro * LENGTH
-    flat = lax.axis_index("fsdp")
-    first_expert = (flat // 4) * 4
-    segments = segments[:, 0]
-    routes = routes[:, 0]
-    slots = jax.vmap(slot_table)(routes)
+    first_expert = (lax.axis_index("fsdp") // 4) * 4
+    cos, sin, keep = jax.vmap(phases)(segments[:, 0])
+    cos, sin = cos.reshape(rows, 128), sin.reshape(rows, 128)
+    slots = jnp.swapaxes(jax.vmap(slot_table)(routes[:, 0]), 0, 1).reshape(EXPERTS, rows)
     small = jnp.concatenate(
         [w_router, attn_gain[:, None], moe_gain[:, None], jnp.zeros((32, 94), BF16)], axis=1
     )
     pack = jnp.concatenate([w_query, w_key, w_value, w_output, small], axis=1)
+    inputs = tokens.reshape(rows, D)
     upstream = cotangent.reshape(rows, D)
-    dense, gbuf, sbuf, wgb, wub, wdb = early(
-        pack,
-        upstream,
-        slots.reshape(micro * EXPERTS, LENGTH).astype(BF16),
-        w_gate[0],
-        w_up[0],
-        w_down[0],
-    )
-    dense = dense.reshape(D, WIDE)
-    wq, wk, wv, wo = dense[:, :1024], dense[:, 1024:1536], dense[:, 1536:2048], dense[:, 2048:3072]
-    wr = dense[:, 3072:3104]
-    gain_one = dense[:, 3104].astype(F32)
-    gain_two = dense[:, 3105].astype(F32)
-
-    inputs = tokens.reshape(rows, D).astype(F32)
-    cos_table, sin_table, visible = jax.vmap(phases)(segments)
-
-    def split(a):
-        return a.reshape((micro, LENGTH) + a.shape[1:])
-
-    def join(a):
-        return a.reshape((rows,) + a.shape[2:])
-
-    normed_one, scale_one, hidden_one = normalize(inputs, gain_one)
-    hidden_low = hidden_one.astype(BF16)
-    query_raw = jnp.dot(hidden_low, wq, preferred_element_type=F32)
-    key_raw = jnp.dot(hidden_low, wk, preferred_element_type=F32)
-    value_low = jnp.dot(hidden_low, wv, preferred_element_type=F32).astype(BF16)
-    query_low = jax.vmap(rotate)(split(query_raw), cos_table, sin_table).astype(BF16)
-    key_low = jax.vmap(rotate)(split(key_raw), cos_table, sin_table).astype(BF16)
-    mixed, log_total = jax.vmap(attend)(query_low, key_low, split(value_low), visible)
-    mixed_low = join(mixed)
-    middle = inputs + RESIDUAL * jnp.dot(mixed_low, wo, preferred_element_type=F32)
-    normed_two, scale_two, hidden_two = normalize(middle, gain_two)
-    routed_low = hidden_two.astype(BF16)
-    logits = jnp.dot(routed_low, wr, preferred_element_type=F32)
-    by_expert = jnp.swapaxes(split(logits), 1, 2)
-    named = slots >= 0
-    shifted = jnp.where(named, by_expert, -jnp.inf)
-    top = jnp.max(shifted, axis=1, keepdims=True)
-    raised = jnp.exp(shifted - top)
-    gates = raised / jnp.sum(raised, axis=1, keepdims=True)
-
-    hbuf, gatebuf = route(routed_low, gates.reshape(micro * EXPERTS, LENGTH))
+    dense, gbuf, sbuf, wgb, wub, wdb, hbuf, gatebuf, q, k, v, p, o, y1, gates = front(
+        inputs, cos, sin, keep, slots, pack, upstream, w_gate[0], w_up[0], w_down[0]
+    )
 
     def mine(buf):
-        by_seq = buf.reshape(8 * micro, EXPERTS, LENGTH)
-        part = lax.dynamic_slice_in_dim(by_seq, first_expert, HERE, axis=1)
-        return jnp.swapaxes(part, 0, 1).astype(F32)
+        part = lax.dynamic_slice_in_dim(buf, first_expert, HERE, axis=1)
+        return jnp.swapaxes(part, 0, 1).reshape(HERE, 8 * micro, LENGTH)
 
     qy, qh, dg, gg, gu, gd = experts(
         hbuf.reshape(8 * micro, LENGTH, D),
@@ -903,54 +1040,17 @@
         wdb,
     )
     qg = lax.dynamic_update_slice_in_dim(
-        jnp.zeros((8 * micro, EXPERTS, LENGTH), F32), jnp.swapaxes(dg, 0, 1), first_expert, axis=1
-    )
-    mixture, routed_grad, gate_grad = send_back(
-        qy.reshape(8, rows, D), qh.reshape(8, rows, D), qg.reshape(8, micro * EXPERTS, LENGTH)
-    )
-    grad_gate, grad_up, grad_down = expert_sum(gg, gu, gd)
-
-    result = (middle + RESIDUAL * mixture).astype(BF16)
-    gate_grad = gate_grad.reshape(micro, EXPERTS, LENGTH)
-    choice = gates * (gate_grad - jnp.sum(gates * gate_grad, axis=1, keepdims=True))
-    logit_grad = join(jnp.swapaxes(choice, 1, 2)).astype(BF16)
-    router_grad = dot(routed_low, logit_grad, ((0,), (0,)))
-    routed_grad = routed_grad + dot(logit_grad, wr, ((1,), (1,)))
-    middle_grad, gain_two_grad = normalize_back(routed_grad, normed_two, scale_two, gain_two)
-    middle_grad = middle_grad + upstream.astype(F32)
-    branch_low = (RESIDUAL * middle_grad).astype(BF16)
-    output_grad = dot(mixed_low, branch_low, ((0,), (0,)))
-    mixed_grad = dot(branch_low, wo, ((1,), (1,))).astype(BF16)
-    query_grad, key_grad, value_grad = jax.vmap(attend_back)(
-        query_low, key_low, split(value_low), visible, log_total, split(mixed_grad)
-    )
-    query_low_grad = join(jax.vmap(rotate)(query_grad, cos_table, -sin_table)).astype(BF16)
-    key_low_grad = join(jax.vmap(rotate)(key_grad, cos_table, -sin_table)).astype(BF16)
-    value_low_grad = join(value_grad).astype(BF16)
-    wq_grad = dot(hidden_low, query_low_grad, ((0,), (0,)))
-    wk_grad = dot(hidden_low, key_low_grad, ((0,), (0,)))
-    wv_grad = dot(hidden_low, value_low_grad, ((0,), (0,)))
-    hidden_grad = (
-        dot(query_low_grad, wq, ((1,), (1,)))
-        + dot(key_low_grad, wk, ((1,), (1,)))
-        + dot(value_low_grad, wv, ((1,), (1,)))
-    )
-    normed_grad, gain_one_grad = normalize_back(hidden_grad, normed_one, scale_one, gain_one)
-    grad_tokens = middle_grad + normed_grad
-    grads = jnp.concatenate(
-        [
-            wq_grad.astype(BF16),
-            wk_grad.astype(BF16),
-            wv_grad.astype(BF16),
-            output_grad.astype(BF16),
-            router_grad.astype(BF16),
-            gain_one_grad[:, None].astype(BF16),
-            gain_two_grad[:, None].astype(BF16),
-            jnp.zeros((D, 94), BF16),
-        ],
+        jnp.zeros((8, EXPERTS, rows), F32),
+        jnp.swapaxes(dg.reshape(HERE, 8, rows), 0, 1),
+        first_expert,
         axis=1,
     )
-    summed = dense_sum(grads)
+    dh, gate_grad = send_back(qh.reshape(8, rows, D), qg)
+    grads, grad_tokens, result, tg, tu, td = retreat(
+        inputs, cos, sin, gates, dense.reshape(D, WIDE), upstream, y1, q, k, v, p, o, dh, gate_grad,
+        qy.reshape(8, rows, D), gg, gu, gd,
+    )
+    summed, grad_gate, grad_up, grad_down = settle(grads, tg, tu, td)
     return (
         result.reshape(micro, 1, LENGTH, D),
         grad_tokens.reshape(micro, 1, LENGTH, D),
@@ -961,9 +1061,9 @@
         summed[:, 1536:2048],
         summed[:, 2048:3072],
         summed[:, 3072:3104],
-        grad_gate,
-        grad_up,
-        grad_down,
+        grad_gate.reshape(1, D, FE),
+        grad_up.reshape(1, D, FE),
+        grad_down.reshape(1, FE, D),
     )
 
 

time: 544 us -> 383 us (0.70)
  Pallas kernels: 437 us -> 355 us
  local copies, waits for them, and re-layouts: 57.8 us -> 22 us
  matrix products: 31.5 us -> 0.14 us
  other arithmetic: 14.7 us -> 4.77 us
    pallas_call x4 -> x3, Pallas kernels: 301 us -> 245 us  [the longest x1 118 us: front(): pl.pallas_call(front_kernel, name='front', out_shape=(shape((2, 4, 4, 32,...]
    dot_general x21 -> x0, matrix products: 29.2 us -> none  [the longest x10 16.9 us: dot(): return lax.dot_general(a, b, (dims, ((), ())), preferred_element_type=F32)]
    pallas_call x1, Pallas kernels: 67 us -> 39.7 us  [send_back(): pl.pallas_call(back_kernel, name='send_back', out_shape=(shape((rows, D),...]
    concatenate x2 -> x0, local copies, waits for them, and re-layouts: 10.8 us -> none  [the longest x1 10.7 us: on_device(): jnp.concatenate([wq_grad.astype(BF16), wk_grad.astype(BF16), wv_grad.asty...]
    another operation x3 -> x0, local copies, waits for them, and re-layouts: 8.01 us -> none  [the longest x2 6.99 us: attend_back(): grad_mixed.reshape(height, KV_HEADS, HEADS // KV_HEADS, HEAD_DIM)]
    dot_general x4 -> x0, local copies, waits for them, and re-layouts: 7.76 us -> none  [the longest x2 5.93 us: on_device(): query_raw = jnp.dot(hidden_low, wq, preferred_element_type=F32)]
    unnamed x82 -> x15, local copies, waits for them, and re-layouts: 13 us -> 8.34 us
where the time goes in v2:
time: 383 us; the launch traced here: 382 us
  Pallas kernels  355 us (93%)
  local copies, waits for them, and re-layouts  22 us (6%)
  other arithmetic  4.77 us (1%)
    pallas_call x1, Pallas kernels, front(): pl.pallas_call(front_kernel, name='front', out_shape=(shape((2, 4, 4, 32,...  118 us
    pallas_call x1, Pallas kernels, retreat(): pl.pallas_call(retreat_kernel, name='retreat', out_shape=(shape((D, WIDE)...  74.1 us
    pallas_call x1, Pallas kernels, experts(): pl.pallas_call(experts_kernel, name='experts', grid=(HERE,), out_shape=(s...  70.1 us
    pallas_call x1, Pallas kernels, settle(): pl.pallas_call(settle_kernel, name='settle', out_shape=(shape((32, WIDE),...  53 us
    pallas_call x1, Pallas kernels, send_back(): pl.pallas_call(back_kernel, name='send_back', out_shape=(shape((rows, D),...  39.7 us
    unnamed x15, local copies, waits for them, and re-layouts  8.34 us

profile of v2, /device:TPU:1, one launch (start us, length us, event | category | flops | bytes accessed | tf_op | source)
XLA Modules:
  0.0 382.3 jit_solution(15891788309202077408)
XLA Ops:
  0.7 0.9 fusion.5
  1.6 0.5 fusion.4
  2.2 1.0 pad_maximum_fusion
  3.1 1.5 and_convert_fusion.keep
  4.7 0.8 fusion.1
  5.4 0.1 fusion
  5.6 0.6 copy.63
  6.2 0.7 copy.53
  7.0 0.8 copy.54
  7.7 1.7 concatenate.13.pack
  9.4 117.7 %front.1 = (bf16[2,4,4,32,3200]{4,3,2,1,0:T(8,128)(2,1)}, bf16[8,256,1024]{2,1,0:T(8,128)(2,1)}, f32[8,32,256]{2,1,0:T(8,128)}, bf16[4,1024,512]{2,1,0:T(8,128)(...) custom-call(bf16[256,1024]{1,0:T(8,128)(2,1)} %bitcast.57, ...), custom_call_target="tpu_custom_call" | custom-call | tf_op jit(solution)/shard_map/front/pallas_call | solution.py:526
  127.1 0.9 dynamic-slice_bitcast_fusion.1
  128.0 0.6 reshape.141.pos
  128.6 0.8 dynamic-slice_bitcast_fusion
  129.4 0.6 reshape.142.gates
  130.1 70.1 %experts.1 = (bf16[16,128,1024]{2,1,0:T(8,128)(2,1)}, bf16[16,128,1024]{2,1,0:T(8,128)(2,1)}, f32[4,16,128]{2,1,0:T(8,128)}, bf16[4,1024,512]{2,1,0:T(8,128)(2,1...) custom-call(bf16[16,128,1024]{2,1,0:T(8,128)(2,1)} %bitcast.48, bf16[16,128,1024]{2,1,0:T(8,128)(2,1)} %bitcast.47, ...), custom_call_target="tpu_custom_call" | custom-call | tf_op jit(solution)/shard_map/experts/pallas_call | solution.py:949
  200.2 0.8 reshape.144
  201.0 0.0 copy-start.2
  201.0 0.7 copy-done.2
  201.7 39.7 %send_back.1 = (f32[256,1024]{1,0:T(8,128)}, f32[32,256]{1,0:T(8,128)}) custom-call(bf16[8,256,1024]{2,1,0:T(8,128)(2,1)} %bitcast.49, f32[8,32,256]{2,1,0:T(8,128)} %copy-done.2), custom_call_target="tpu_custom_call" | custom-call | tf_op jit(solution)/shard_map/send_back/pallas_call | solution.py:576
  241.4 74.1 %retreat.1 = (bf16[1024,3200]{1,0:T(8,128)(2,1)}, f32[256,1024]{1,0:T(8,128)}, bf16[256,1024]{1,0:T(8,128)(2,1)}, bf16[2,4,64,512]{3,2,1,0:T(8,128)(2,1)}, bf16[...) custom-call(bf16[256,1024]{1,0:T(8,128)(2,1)} %bitcast.58, f32[256,128]{1,0:T(8,128)} %get-tuple-element.135.cos, ...), custom_call_target="tpu_custom_call" | custom-call | tf_op jit(solution)/shard_map/retreat/pallas_call | solution.py:715
  315.5 0.0 copy-start.4
  315.5 0.0 copy-start.3
  315.5 53.0 %settle.1 = (f32[32,3200]{1,0:T(8,128)}, f32[2,2,4,64,512]{4,3,2,1,0:T(8,128)}, f32[2,2,4,64,512]{4,3,2,1,0:T(8,128)}, f32[2,2,4,32,1024]{4,3,2,1,0:T(8,128)}) custom-call(bf16[2,4,4,32,3200]{4,3,2,1,0:T(8,128)(2,1)} %bitcast.45, bf16[2,4,64,512]{3,2,1,0:T(8,128)(2,1)} %get-tuple-element.71.tg, bf16[2,4,64,512]{3,2,1,0:T(8,128)(2,1)} %get-tuple-element.72.tu, ...), custom_call_target="tpu_custom_call" | custom-call | tf_op jit(solution)/shard_map/settle/pallas_call | solution.py:841
  368.5 0.0 copy-start.1
  368.5 1.6 slice_reduce_fusion
  370.1 1.7 fusion.6
  371.8 1.5 fusion.7
  373.3 1.3 slice.27
  374.6 0.0 copy-done.4
  374.6 0.8 copy.70
  375.4 0.0 copy-done.3
  375.4 1.0 copy.71
  376.4 0.0 copy-start
  376.4 3.2 copy.72
  379.6 0.0 copy-done.1
  379.6 1.3 copy.73
  381.0 0.0 copy-done
  381.0 1.3 copy.74
  (8 shorter events, 0.1 us)
Async XLA Ops:
  201.0 0.7 copy-start.2
  315.5 59.2 %copy-start.4 = (bf16[256,1024]{1,0:T(8,128)(2,1)S(1)}, bf16[256,1024]{1,0:T(8,128)(2,1)}, u32[]{:S(2)}) copy-start(bf16[256,1024]{1,0:T(8,128)(2,1)} %get-tuple-element.68) | copy-start | bytes 1572868
  315.5 60.0 %copy-start.3 = (f32[256,1024]{1,0:T(8,128)S(1)}, f32[256,1024]{1,0:T(8,128)}, u32[]{:S(2)}) copy-start(f32[256,1024]{1,0:T(8,128)} %get-tuple-element.69) | copy-start | bytes 3145732
  368.5 11.1 %copy-start.1 = (f32[2,2,4,64,512]{4,3,2,1,0:T(8,128)S(1)}, f32[2,2,4,64,512]{4,3,2,1,0:T(8,128)}, u32[]{:S(2)}) copy-start(f32[2,2,4,64,512]{4,3,2,1,0:T(8,128)} %get-tuple-element.76) | copy-start | bytes 6291460
  376.4 4.6 %copy-start = (f32[2,2,4,32,1024]{4,3,2,1,0:T(8,128)S(1)}, f32[2,2,4,32,1024]{4,3,2,1,0:T(8,128)}, u32[]{:S(2)}) copy-start(f32[2,2,4,32,1024]{4,3,2,1,0:T(8,128)} %get-tuple-element.77) | copy-start | bytes 6291460

commit v3 on v2

--- a/solution.py
+++ b/solution.py
@@ -136,30 +136,33 @@
     spread(far)
 
 
-def group_gather(lines, me, source, buf):
-    rows = buf.shape[1]
+def group_gather(lines, me, source, buf, start=0, rows=None):
+    rows = rows or buf.shape[1]
     ahead, behind, far = lax.rem(me.x + 1, 4), lax.rem(me.x + 3, 4), lax.rem(me.x + 2, 4)
     right, left, cross = me.right(), me.left(), me.cross()
     base, other = me.high * 4, (1 - me.high) * 4
 
+    def slot(k):
+        return buf.at[k, pl.ds(start, rows)]
+
     def half(k, h):
-        return buf.at[k, pl.ds(h * rows // 2, rows // 2)]
-
-    a = lines.send(source, buf.at[base + me.x], right)
-    b = lines.send(source, buf.at[base + me.x], left)
-    e = lines.send(source, buf.at[base + me.x], cross)
+        return buf.at[k, pl.ds(start + h * rows // 2, rows // 2)]
+
+    e = lines.send(source, slot(base + me.x), cross)
+    a = lines.send(source, slot(base + me.x), right)
+    b = lines.send(source, slot(base + me.x), left)
     yield
     a.wait_recv()
     c = lines.send(half(base + behind, 0), half(base + behind, 0), right)
     b.wait_recv()
     d = lines.send(half(base + ahead, 1), half(base + ahead, 1), left)
     e.wait_recv()
-    f = lines.send(buf.at[other + me.x], buf.at[other + me.x], right)
-    g = lines.send(buf.at[other + me.x], buf.at[other + me.x], left)
+    f = lines.send(slot(other + me.x), slot(other + me.x), right)
+    g = lines.send(slot(other + me.x), slot(other + me.x), left)
     yield
     c.wait_recv()
     d.wait_recv()
-    h = lines.send(buf.at[base + far], buf.at[base + far], cross)
+    h = lines.send(slot(base + far), slot(base + far), cross)
     yield
     f.wait_recv()
     g.wait_recv()
@@ -172,66 +175,79 @@
         body(pl.ds(pl.multiple_of(i * step, step), step))
 
 
-def group_scatter(lines, me, q, out, by, sf, tl, tr, t, hl, hr, nl, nr, fl, fr, fy):
-    rows = q.shape[1]
+def group_scatter(lines, me, q, out, start, rows, by, sf, tl, tr, t, hl, hr, nl, nr, fl, fr, fy):
     mid = rows // 2
-    step = min(32, mid)
+    step_rows = min(32, mid)
     ahead, behind, far = lax.rem(me.x + 1, 4), lax.rem(me.x + 3, 4), lax.rem(me.x + 2, 4)
     right, left, cross = me.right(), me.left(), me.cross()
     base, other = me.high * 4, (1 - me.high) * 4
     first, second = pl.ds(0, mid), pl.ds(mid, mid)
 
-    def wide(ref, sl):
-        return ref[sl].astype(F32)
-
-    e = lines.send(q.at[other + far], by, cross)
-    g1 = lines.send(q.at[other + ahead], tl, right)
-    g2 = lines.send(q.at[other + behind], tr, left)
-    i1 = lines.send(q.at[base + ahead, second], fl.at[second], right)
-    i2 = lines.send(q.at[base + behind, first], fr.at[first], left)
+    def whole(k):
+        return q.at[k, pl.ds(start, rows)]
+
+    def part(k, h):
+        return q.at[k, pl.ds(start + h * mid, mid)]
+
+    def each(count, offset, body):
+        @pl.loop(0, count // step_rows)
+        def _(i):
+            here = pl.multiple_of(i * step_rows, step_rows)
+            there = pl.multiple_of(start + offset + i * step_rows, step_rows)
+            body(pl.ds(here, step_rows), pl.ds(there, step_rows))
+
+    e = lines.send(whole(other + far), by, cross)
+    g1 = lines.send(whole(other + ahead), tl, right)
+    g2 = lines.send(whole(other + behind), tr, left)
+    i1 = lines.send(part(base + ahead, 1), fl.at[second], right)
+    i2 = lines.send(part(base + behind, 0), fr.at[first], left)
     yield
     e.wait_recv()
 
-    def far_sum(sl):
-        sf[sl] = (q[base + far, sl].astype(F32) + wide(by, sl)).astype(sf.dtype)
-
-    tiles(rows, step, far_sum)
+    def far_sum(here, there):
+        sf[here] = q[base + far, there] + by[here]
+
+    each(rows, 0, far_sum)
     j1 = lines.send(sf.at[first], hl, right)
     j2 = lines.send(sf.at[second], hr, left)
     yield
     g1.wait_recv()
     g2.wait_recv()
 
-    def partner_sum(sl):
-        t[sl] = (q[other + me.x, sl].astype(F32) + wide(tl, sl) + wide(tr, sl)).astype(t.dtype)
-
-    tiles(rows, step, partner_sum)
+    def partner_sum(here, there):
+        total = q[other + me.x, there].astype(F32) + tl[here].astype(F32) + tr[here].astype(F32)
+        t[here] = total.astype(t.dtype)
+
+    each(rows, 0, partner_sum)
     k = lines.send(t, fy, cross)
     yield
     j1.wait_recv()
 
-    def right_sum(sl):
-        nl[sl] = (q[base + ahead, sl].astype(F32) + wide(hl, sl)).astype(nl.dtype)
-
-    tiles(mid, step, right_sum)
+    def right_sum(here, there):
+        nl[here] = q[base + ahead, there] + hl[here]
+
+    each(mid, 0, right_sum)
     l1 = lines.send(nl, fl.at[first], right)
     j2.wait_recv()
 
-    @pl.loop(0, mid // step)
-    def _(i):
-        here = pl.ds(pl.multiple_of(i * step, step), step)
-        there = pl.ds(pl.multiple_of(mid + i * step, step), step)
-        nr[here] = (q[base + behind, there].astype(F32) + wide(hr, here)).astype(nr.dtype)
-
+    def left_sum(here, there):
+        nr[here] = q[base + behind, there] + hr[here]
+
+    each(mid, mid, left_sum)
     l2 = lines.send(nr, fr.at[second], left)
     yield
     for copy in (i1, i2, l1, l2, k):
         copy.wait_recv()
 
-    def total(sl):
-        out[sl] = q[base + me.x, sl].astype(F32) + wide(fl, sl) + wide(fr, sl) + wide(fy, sl)
-
-    tiles(rows, step, total)
+    def total(here, there):
+        out[there] = (
+            q[base + me.x, there].astype(F32)
+            + fl[here].astype(F32)
+            + fr[here].astype(F32)
+            + fy[here].astype(F32)
+        )
+
+    each(rows, 0, total)
 
 
 def ring_scatter(lines, arr, pos, right, left, hl, hr, fl, fr, store):
@@ -307,6 +323,48 @@
     return jnp.where(lanes() < 64, even, odd)
 
 
+def side(table):
+    return jnp.concatenate([table[:EXPERTS], table[EXPERTS:]], axis=1)
+
+
+def phases(segment):
+    across = jnp.broadcast_to(segment.astype(F32), (LENGTH, LENGTH))
+    down = jnp.transpose(across)
+    t = lax.broadcasted_iota(jnp.int32, (LENGTH, LENGTH), 0)
+    u = lax.broadcasted_iota(jnp.int32, (LENGTH, LENGTH), 1)
+    keep = jnp.where((u <= t) & (across == down), 1.0, 0.0)
+    offset = jnp.sum(keep, axis=1, keepdims=True) - 1.0
+    step_of = lax.rem(lanes(), 32).astype(F32)
+    frequency = jnp.exp(-math.log(ROPE_BASE) * 2.0 * step_of / HEAD_DIM)
+    angles = offset * frequency
+    sign = jnp.where(lax.rem(lanes(), 64) < 32, -1.0, 1.0)
+    return jnp.cos(angles), sign * jnp.sin(angles), keep
+
+
+def slot_table(route_ids):
+    wide = jnp.concatenate([route_ids.astype(F32), jnp.zeros((LENGTH, 128 - TOPK), F32)], axis=1)
+    by_choice = jnp.transpose(wide)
+    ids = lax.broadcasted_iota(jnp.int32, (EXPERTS, LENGTH), 0).astype(F32)
+    named = jnp.zeros((EXPERTS, LENGTH), F32)
+    for j in range(TOPK):
+        named = jnp.where(by_choice[j : j + 1] == ids, 1.0, named)
+    t = lax.broadcasted_iota(jnp.int32, (LENGTH, LENGTH), 0)
+    u = lax.broadcasted_iota(jnp.int32, (LENGTH, LENGTH), 1)
+    before = jnp.where(t < u, 1.0, 0.0).astype(BF16)
+    return jnp.where(named > 0.0, dot(named.astype(BF16), before), -1.0)
+
+
+def small_shard(router, gains):
+    wide = jnp.concatenate([router.astype(F32), jnp.zeros((32, 128 - EXPERTS), F32)], axis=1)
+    row = lax.broadcasted_iota(jnp.int32, (32, 32), 0)
+    lane = lax.broadcasted_iota(jnp.int32, (32, 32), 1)
+    for i in range(2):
+        across = jnp.broadcast_to(gains[i : i + 1].astype(F32), (32, 32))
+        column = jnp.sum(jnp.where(row == lane, across, 0.0), axis=1, keepdims=True)
+        wide = jnp.where(lanes() == EXPERTS + i, column, wide)
+    return wide.astype(BF16)
+
+
 def norm_scale(values):
     return lax.rsqrt(jnp.mean(values * values, axis=1, keepdims=True) + EPS)
 
@@ -348,9 +406,9 @@
 
 
 def front_kernel(
-    tokens, cos, sin, keep, slots, pack, g, wg, wu, wd,
-    dense, gbuf, sbuf, wgb, wub, wdb, hbuf, gatebuf, q, k, v, p, o, y1, gates,
-    dn, h, send_sems, recv_sems, local_sems,
+    tokens, segments, routes, wq_own, wk_own, wv_own, wo_own, wr_own, gains, g, wg, wu, wd,
+    dense, gbuf, sbuf, wgb, wub, wdb, hbuf, gatebuf, q, k, v, p, o, y1, gates, cos, sin,
+    dn, h, keep, slots, send_sems, recv_sems, local_sems,
 ):
     me = Place()
     right, left, above, below = me.right(), me.left(), me.above(), me.below()
@@ -358,43 +416,71 @@
     rows = pl.ds(pl.multiple_of(me.core * 16, 16), 16)
     own = me.high * 4 + me.x
     local = [
-        pltpu.make_async_copy(pack.at[rows], dn.at[me.high, me.x, me.z, rows], local_sems.at[0]),
         pltpu.make_async_copy(g, gbuf.at[own], local_sems.at[1]),
-        pltpu.make_async_copy(slots, sbuf.at[own], local_sems.at[2]),
         pltpu.make_async_copy(wg, wgb.at[me.z], local_sems.at[3]),
         pltpu.make_async_copy(wu, wub.at[me.z], local_sems.at[4]),
         pltpu.make_async_copy(wd, wdb.at[me.z], local_sems.at[5]),
     ]
     for copy in local:
         copy.start()
+    shard = dn.at[me.high, me.x, me.z]
+    shard[:, 0:1024] = wq_own[...]
+    shard[:, 1024:1536] = wk_own[...]
+    shard[:, 1536:2048] = wv_own[...]
+    shard[:, 2048:3072] = wo_own[...]
+    shard[:, 3072:3200] = small_shard(wr_own[...], gains[...])
     greet((right, left, above, below, cross, sibling))
     lines = Lines(send_sems, recv_sems)
     shared = []
 
     def dense_chain(columns, x_first):
-        def on_z(p, k=None):
-            if x_first:
-                return dn.at[slice(None) if k is None else k, :, p, rows, columns]
-            return dn.at[slice(None) if k is None else k, me.x, p, rows, columns]
-
-        def on_x(p, k=None):
-            if x_first:
-                return dn.at[slice(None) if k is None else k, p, me.z, rows, columns]
-            return dn.at[slice(None) if k is None else k, p, :, rows, columns]
-
-        if x_first:
-            first = (on_x(me.x), on_x, on_x, me.x, right, left)
-            last = (on_z(me.z), on_z, on_z, me.z, above, below)
-        else:
-            first = (on_z(me.z), on_z, on_z, me.z, above, below)
-            last = (on_x(me.x), on_x, on_x, me.x, right, left)
-        yield from ring_gather(lines, *first)
-
-        def spread(p):
-            shared.append(lines.send(last[1](p), last[1](p), sibling))
-
-        spread(last[3])
-        yield from ring_gather(lines, *last, spread=spread)
+        on_x, on_z = (me.x, right, left), (me.z, above, below)
+        (pos, up, down), (pos2, up2, down2) = (on_x, on_z) if x_first else (on_z, on_x)
+        ahead, behind, far = lax.rem(pos + 1, 4), lax.rem(pos + 3, 4), lax.rem(pos + 2, 4)
+
+        def piece(one, two, k=None):
+            x, z = (one, two) if x_first else (two, one)
+            return dn.at[slice(None) if k is None else k, x, z, rows, columns]
+
+        def unit(one):
+            def spread(two):
+                shared.append(lines.send(piece(one, two), piece(one, two), sibling))
+
+            def slot(two):
+                return piece(one, two)
+
+            def half(two, k):
+                return piece(one, two, k)
+
+            chain = ring_gather(lines, slot(pos2), slot, half, pos2, up2, down2, spread=spread)
+            next(chain)
+            spread(pos2)
+            return chain
+
+        mine = piece(pos, pos2)
+        a = lines.send(mine, mine, up)
+        b = lines.send(mine, mine, down)
+        units = [unit(pos)]
+        yield
+        a.wait_recv()
+        c = lines.send(piece(behind, pos2, 0), piece(behind, pos2, 0), up)
+        units.append(unit(behind))
+        b.wait_recv()
+        d = lines.send(piece(ahead, pos2, 1), piece(ahead, pos2, 1), down)
+        units.append(unit(ahead))
+        yield
+        step(units[0])
+        yield
+        c.wait_recv()
+        d.wait_recv()
+        units.append(unit(far))
+        yield
+        step(units[1], units[2])
+        yield
+        step(units[0], units[3])
+        yield
+        step(*units[1:])
+        step(*units)
 
     def weight_chain(source, buf):
         half_rows = source.shape[0] // 2
@@ -421,17 +507,26 @@
             spread=spread,
         )
 
-    swap = lines.send(pack.at[rows], dn.at[me.high, me.x, me.z, rows], cross)
-    local[0].wait()
+    swap = lines.send(shard.at[rows], shard.at[rows], cross)
+    for part in range(2):
+        here = slice(part * LENGTH, (part + 1) * LENGTH)
+        cos[here], sin[here], keep[part] = phases(segments[part : part + 1, :])
+        slots[part * EXPERTS : (part + 1) * EXPERTS] = slot_table(routes[here, :])
+    local.append(pltpu.make_async_copy(slots, sbuf.at[own], local_sems.at[2]))
+    local[-1].start()
     swap.wait_recv()
     gs = group_gather(lines, me, g, gbuf)
     ss = group_gather(lines, me, slots, sbuf)
     w1, w2, w3 = weight_chain(wg, wgb), weight_chain(wu, wub), weight_chain(wd, wdb)
-    drive(dense_chain(pl.ds(0, CUT), False), dense_chain(pl.ds(CUT, WIDE - CUT), True))
+    dense_a, dense_b = dense_chain(pl.ds(0, CUT), False), dense_chain(pl.ds(CUT, WIDE - CUT), True)
+    for _ in range(4):
+        step(dense_a, dense_b)
+    step(gs, ss, w1)
+    drive(dense_a, dense_b)
     for copy in shared:
         copy.wait_recv()
     del shared[:]
-    step(gs, ss, w1)
+    step(gs, ss)
     keeping = pltpu.make_async_copy(dn, dense, local_sems.at[6])
     keeping.start()
 
@@ -457,7 +552,7 @@
                 u * cos[...] + swap_halves(u) * sin[...]
             ).astype(BF16)
     v[...] = dot(h[...], weight(1536, 512)).astype(BF16)
-    step(w2)
+    step(w1, w2)
 
     def attend(i):
         s, m = lax.div(i, 4), lax.rem(i, 4)
@@ -476,53 +571,49 @@
             both = dot(probs.astype(BF16), doubled(v_tile, odd))
             o[here, q_column] = side_by_side(both).astype(BF16)
 
-    for part in range(4):
-
-        @pl.loop(part * 2, part * 2 + 2)
+    late = []
+    routed = []
+    for part in range(2):
+
+        @pl.loop(part * 4, part * 4 + 4)
         def _(i):
             attend(i)
 
-        if part == 1:
-            step(w1)
-        if part == 2:
-            step(gs, ss)
-        if part == 3:
-            step(w3)
-
-    middle = tokens[...].astype(F32) + RESIDUAL * dot(o[...], weight(2048, 1024))
-    y1[...] = middle
-    h[...] = (middle * norm_scale(middle) * gain_two).astype(BF16)
-    logits = dot(small, h[...], ((0,), (1,)))[:EXPERTS]
-    named = slots[...] >= 0.0
-    top = jnp.max(jnp.where(named, logits, -jnp.inf), axis=0, keepdims=True)
-    raised = jnp.where(named, jnp.exp(jnp.where(named, logits - top, 0.0)), 0.0)
-    gates[...] = raised / jnp.sum(raised, axis=0, keepdims=True)
-
-    late = [
-        pltpu.make_async_copy(h, hbuf.at[own], local_sems.at[7]),
-        pltpu.make_async_copy(gates, gatebuf.at[own], local_sems.at[8]),
-    ]
-    for copy in late:
-        copy.start()
-    drive(
-        group_gather(lines, me, h, hbuf),
-        group_gather(lines, me, gates, gatebuf),
-        gs,
-        ss,
-        w1,
-        w2,
-        w3,
-    )
+        here = slice(part * LENGTH, (part + 1) * LENGTH)
+        middle = tokens[here].astype(F32) + RESIDUAL * dot(o[here], weight(2048, 1024))
+        y1[here] = middle
+        h[here] = (middle * norm_scale(middle) * gain_two).astype(BF16)
+        routed.append(group_gather(lines, me, h.at[here], hbuf, part * LENGTH, LENGTH))
+        step(routed[part])
+        late.append(pltpu.make_async_copy(h.at[here], hbuf.at[own, here], local_sems.at[7 + part]))
+        late[part].start()
+        logits = dot(small, h[here], ((0,), (1,)))[:EXPERTS]
+        table = slice(part * EXPERTS, (part + 1) * EXPERTS)
+        named = slots[table] >= 0.0
+        top = jnp.max(jnp.where(named, logits, -jnp.inf), axis=0, keepdims=True)
+        raised = jnp.where(named, jnp.exp(jnp.where(named, logits - top, 0.0)), 0.0)
+        gates[table] = raised / jnp.sum(raised, axis=0, keepdims=True)
+
+    weighed = group_gather(lines, me, gates, gatebuf)
+    late.append(pltpu.make_async_copy(gates, gatebuf.at[own], local_sems.at[9]))
+    late[2].start()
+    step(weighed, w3, gs, ss)
+    step(routed[0], w2)
+    step(routed[1], weighed, w1, w3)
+    step(routed[0], w2)
+    step(routed[1], weighed)
+    drive(routed[0], routed[1], weighed, gs, ss, w1, w2, w3)
     for copy in shared:
         copy.wait_recv()
-    for copy in local[1:] + [keeping] + late:
+    for copy in local + [keeping] + late:
         copy.wait()
     lines.drain()
 
 
-def front(tokens, cos, sin, keep, slots, pack, g, wg, wu, wd):
+def front(tokens, segments, routes, wq, wk, wv, wo, wr, gains, g, wg, wu, wd):
     shape = jax.ShapeDtypeStruct
     rows = tokens.shape[0]
+    slots = shape((2 * EXPERTS, LENGTH), F32)
     return pl.pallas_call(
         front_kernel,
         name="front",
@@ -534,56 +625,35 @@
             shape((4,) + wu.shape, BF16),
             shape((4,) + wd.shape, BF16),
             shape((8, rows, D), BF16),
-            shape((8, EXPERTS, rows), F32),
+            shape((8,) + slots.shape, F32),
             shape((rows, 1024), BF16),
             shape((rows, 512), BF16),
             shape((rows, 512), BF16),
             shape((8, 2, 256, 128), F32),
             shape((rows, 1024), BF16),
             shape((rows, D), F32),
-            shape((EXPERTS, rows), F32),
+            shape(slots.shape, F32),
+            shape((rows, 128), F32),
+            shape((rows, 128), F32),
         ),
-        in_specs=vmem(6) + anywhere(4),
-        out_specs=anywhere(8) + vmem(7),
-        scratch_shapes=[pltpu.VMEM((2, 4, 4, 32, WIDE), BF16), pltpu.VMEM((rows, D), BF16)]
-        + sems(88)
-        + [pltpu.SemaphoreType.DMA((9,))],
+        in_specs=vmem(13),
+        out_specs=anywhere(8) + vmem(9),
+        scratch_shapes=[
+            pltpu.VMEM((2, 4, 4, 32, WIDE), BF16),
+            pltpu.VMEM((rows, D), BF16),
+            pltpu.VMEM((2, LENGTH, LENGTH), F32),
+            pltpu.VMEM(slots.shape, F32),
+        ]
+        + sems(140)
+        + [pltpu.SemaphoreType.DMA((10,))],
         compiler_params=params(0),
-    )(tokens, cos, sin, keep, slots, pack, g, wg, wu, wd)
+    )(tokens, segments, routes, wq, wk, wv, wo, wr, gains, g, wg, wu, wd)
 
 
 def scatter_scratch(rows, columns, dtype):
     full = pltpu.VMEM((rows, columns), dtype)
     half = pltpu.VMEM((rows // 2, columns), dtype)
     return [full] * 5 + [half] * 4 + [full] * 3
-
-
-def back_kernel(qh, qg, dh, dg, *scratch):
-    me = Place()
-    send_sems, recv_sems = scratch[:2]
-    greet((me.right(), me.left(), me.cross()))
-    lines = Lines(send_sems, recv_sems)
-    drive(
-        group_scatter(lines, me, qg, dg, *scratch[2:14]),
-        group_scatter(lines, me, qh, dh, *scratch[14:26]),
-    )
-    lines.drain()
-
-
-def send_back(qh, qg):
-    shape = jax.ShapeDtypeStruct
-    rows = qh.shape[1]
-    return pl.pallas_call(
-        back_kernel,
-        name="send_back",
-        out_shape=(shape((rows, D), F32), shape(qg.shape[1:], F32)),
-        in_specs=vmem(2),
-        out_specs=vmem(2),
-        scratch_shapes=sems(36)
-        + scatter_scratch(qg.shape[1], qg.shape[2], F32)
-        + scatter_scratch(rows, D, BF16),
-        compiler_params=params(1),
-    )(qh, qg)
 
 
 def retreat_kernel(
@@ -620,7 +690,7 @@
     e1 = chain(gg, tg, local[0], *scratch[3:9])
     e2 = chain(gu, tu, local[1], *scratch[9:15])
     e3 = chain(gd, td, local[2], *scratch[15:21])
-    ys = group_scatter(lines, me, qy, mixture, *scratch[21:33])
+    ys = group_scatter(lines, me, qy, mixture, 0, 2 * LENGTH, *scratch[21:33])
     step(e1, e2, e3, ys)
 
     small = dense[:, 3072:3200]
@@ -631,8 +701,8 @@
     scale = norm_scale(middle)
     normed = middle * scale
     routed = (normed * gain_two).astype(BF16)
-    inner = jnp.sum(gates[...] * dg[...], axis=0, keepdims=True)
-    choice = gates[...] * (dg[...] - inner)
+    weights, grad = side(gates), side(dg)
+    choice = weights * (grad - jnp.sum(weights * grad, axis=0, keepdims=True))
     by_token = jnp.transpose(
         jnp.concatenate([choice, jnp.zeros((128 - EXPERTS, choice.shape[1]), F32)])
     ).astype(BF16)
@@ -747,7 +817,7 @@
     )
 
 
-def settle_kernel(grads, tg, tu, td, out, og, ou, od, rc, *scratch):
+def settle_kernel(grads, tg, tu, td, oq, ok, ov, oo, osmall, og, ou, od, rc, out, *scratch):
     me = Place()
     send_sems, recv_sems = scratch[:2]
     right, left, above, below = me.right(), me.left(), me.above(), me.below()
@@ -756,17 +826,23 @@
     lines = Lines(send_sems, recv_sems)
     mine = pl.ds(pl.multiple_of(me.core * 16, 16), 16)
     theirs = pl.ds(pl.multiple_of((1 - me.core) * 16, 16), 16)
-    swap = lines.send(grads.at[:, :, :, theirs], rc, sibling)
-
-    def chain(columns, x_first, acc, second, hl, hr, fl, fr, hl2, hr2, fl2, fr2, r2, ry, r3, yb):
+
+    def swap(columns):
+        return lines.send(grads.at[:, :, :, theirs, columns], rc.at[:, :, :, :, columns], sibling)
+
+    swaps = [swap(pl.ds(0, CUT)), swap(pl.ds(CUT, WIDE - CUT))]
+
+    def chain(swap, columns, x_first, acc, second, hl, hr, fl, fr, hl2, hr2, fl2, fr2, r2, ry, r3, yb):
+        swap.wait_recv()
+
         @pl.loop(0, 32)
         def _(i):
             k, x, z = lax.div(i, 16), lax.rem(lax.div(i, 4), 4), lax.rem(i, 4)
-            value = grads[k, x, z, mine, columns].astype(F32) + rc[k, x, z, :, columns].astype(F32)
+            value = grads[k, x, z, mine, columns] + rc[k, x, z, :, columns]
             if x_first:
-                acc[x, k, z] = value.astype(BF16)
+                acc[x, k, z] = value
             else:
-                acc[z, k, x] = value.astype(BF16)
+                acc[z, k, x] = value
 
         yield
 
@@ -808,12 +884,16 @@
 
     others = [swapped(t, w, s) for t, w, s in zip((tg, tu, td), (og, ou, od), scratch[30:33])]
     step(*others)
-    swap.wait_recv()
-    drive(
-        chain(pl.ds(0, CUT), True, *scratch[2:16]),
-        chain(pl.ds(CUT, WIDE - CUT), False, *scratch[16:30]),
-    )
+    one = chain(swaps[0], pl.ds(0, CUT), True, *scratch[2:16])
+    two = chain(swaps[1], pl.ds(CUT, WIDE - CUT), False, *scratch[16:30])
+    step(one)
+    step(one, two)
+    drive(one, two)
     drive(*others)
+    start = 0
+    for part in (oq, ok, ov, oo, osmall):
+        part[...] = out[:, start : start + part.shape[1]]
+        start += part.shape[1]
     lines.drain()
 
 
@@ -842,14 +922,18 @@
         settle_kernel,
         name="settle",
         out_shape=(
-            shape((32, WIDE), F32),
+            shape((32, 1024), F32),
+            shape((32, 512), F32),
+            shape((32, 512), F32),
+            shape((32, 1024), F32),
+            shape((32, 128), F32),
             shape((2, 2, 4, 64, 512), F32),
             shape((2, 2, 4, 64, 512), F32),
             shape((2, 2, 4, 32, 1024), F32),
         ),
         in_specs=vmem(4),
-        out_specs=vmem(4),
-        scratch_shapes=[pltpu.VMEM((2, 4, 4, 16, WIDE), BF16)]
+        out_specs=vmem(8),
+        scratch_shapes=[pltpu.VMEM((2, 4, 4, 16, WIDE), BF16), pltpu.VMEM((32, WIDE), F32)]
         + sems(48)
         + scratch(CUT)
         + scratch(WIDE - CUT)
@@ -858,33 +942,98 @@
     )(grads.reshape(2, 4, 4, 32, WIDE), tg, tu, td)
 
 
+def finish_kernel(*refs):
+    n = len(refs) // 3
+    sources, targets, stages, arrived = refs[:n], refs[n : 2 * n], refs[2 * n : 3 * n], refs[3 * n]
+    fetches, writes = [], []
+    for i in range(n):
+        fetches.append(pltpu.make_async_copy(sources[i], stages[i], arrived.at[i]))
+        writes.append(pltpu.make_async_copy(stages[i], targets[i], arrived.at[n + i]))
+        fetches[i].start()
+    for i in range(n):
+        fetches[i].wait()
+        writes[i].start()
+    for write in writes:
+        write.wait()
+
+
+def finish(*arrays):
+    n = len(arrays)
+    return pl.pallas_call(
+        finish_kernel,
+        name="finish",
+        out_shape=tuple(jax.ShapeDtypeStruct(a.shape, a.dtype) for a in arrays),
+        in_specs=anywhere(n),
+        out_specs=tuple(anywhere(n)),
+        scratch_shapes=[pltpu.VMEM(a.shape, a.dtype) for a in arrays]
+        + [pltpu.SemaphoreType.DMA((2 * n,))],
+        compiler_params=params(limit=60),
+    )(*arrays)
+
+
 def experts_kernel(
-    h, g, pos, gates, wg, wu, wd, qy, qh, dg, gg, gu, gd, xs, gs, dys, gys, dhs, ms, das, dbs, gcol, dcol
+    h_all, g_all, pos, gates, wg, wu, wd,
+    qy, dh, dg, gg, gu, gd,
+    hg, xs, gs, dys, dhs, ms, das, dbs, gcol, dcol, qg, gg_part, gu_part, local_sems, send_sems, recv_sems, *scratch,
 ):
     e = pl.program_id(0)
-    n_seqs = h.shape[0]
+    me = Place()
+    partners = (me.right(), me.left(), me.cross())
+    first = me.high * 16 + me.x * 4
+    n_seqs = 16
     rows = n_seqs * CAP
     places = lax.broadcasted_iota(jnp.int32, (CAP, LENGTH), 0).astype(F32)
 
-    def slots_of(s, k):
-        return pl.ds(pl.multiple_of(s * CAP, CAP), CAP)
-
-    @pl.loop(0, n_seqs)
-    def _(s):
-        here = slots_of(s, e)
-        chosen = places == pos[e, pl.ds(s, 1), :]
-        pick = chosen.astype(F32).astype(BF16)
-        xs[here] = dot(pick, h[s]).astype(BF16)
-        got = dot(pick, g[s])
-        weight = jnp.sum(jnp.where(chosen, gates[e, pl.ds(s, 1), :], 0.0), axis=1, keepdims=True)
-        gs[here] = got.astype(BF16)
-        dys[here] = (weight * (RESIDUAL * got)).astype(BF16)
-        gcol[here] = jnp.broadcast_to(weight, (CAP, LENGTH))
+    def row_of(table, member, part, k):
+        return table[member, pl.ds(part * EXPERTS + first + k, 1), :]
+
+    def slots_of(member, part):
+        return pl.ds(pl.multiple_of((member * 2 + part) * CAP, CAP), CAP)
+
+    def picks(member, part):
+        chosen = [places == row_of(pos, member, part, k) for k in range(HERE)]
+        return chosen, jnp.concatenate([c.astype(F32).astype(BF16) for c in chosen])
+
+    @pl.when(e == 0)
+    def _():
+        loads = [
+            pltpu.make_async_copy(h_all, hg.at[0], local_sems.at[0]),
+            pltpu.make_async_copy(g_all, hg.at[1], local_sems.at[1]),
+        ]
+        for load in loads:
+            load.start()
+        greet(partners)
+        qg[...] = jnp.zeros_like(qg)
+        for load in loads:
+            load.wait()
+
+        @pl.loop(0, 8)
+        def _(member):
+            for part in range(2):
+                chosen, pick = picks(member, part)
+                here = slots_of(member, part)
+                tokens = slice(part * LENGTH, (part + 1) * LENGTH)
+                got = dot(pick, hg[0, member, tokens]).astype(BF16)
+                for k in range(HERE):
+                    xs[k, here] = got[k * CAP : (k + 1) * CAP]
+                got = dot(pick, hg[1, member, tokens]).astype(BF16)
+                for k in range(HERE):
+                    gs[k, here] = got[k * CAP : (k + 1) * CAP]
+                    weight = jnp.sum(
+                        jnp.where(chosen[k], row_of(gates, member, part, k), 0.0),
+                        axis=1,
+                        keepdims=True,
+                    )
+                    gcol[k, here] = jnp.broadcast_to(weight, (CAP, LENGTH))
 
     @pl.loop(0, rows // 256)
     def _(r):
         here = pl.ds(pl.multiple_of(r * 256, 256), 256)
-        x = xs[here]
+        x = xs[e, here]
+        g_slot = gs[e, here].astype(F32)
+        weight = gcol[e, here][:, :1]
+        dy = (weight * (RESIDUAL * g_slot)).astype(BF16)
+        dys[here] = dy
         a = dot(x, wg[0])
         b = dot(x, wu[0])
         sig = jax.nn.sigmoid(a)
@@ -892,29 +1041,25 @@
         m = (swish * b).astype(BF16)
         ms[here] = m
         y = dot(m, wd[0]).astype(BF16).astype(F32)
-        inner = RESIDUAL * jnp.sum(gs[here].astype(F32) * y, axis=1, keepdims=True)
+        inner = RESIDUAL * jnp.sum(g_slot * y, axis=1, keepdims=True)
         dcol[here] = jnp.broadcast_to(inner, (256, LENGTH))
-        gys[e, here] = (gcol[here][:, :1] * y).astype(BF16)
-        dm = dot(dys[here], wd[0], ((1,), (1,)))
+        gs[e, here] = (weight * y).astype(BF16)
+        dm = dot(dy, wd[0], ((1,), (1,)))
         da = (dm * b * sig * (1.0 + a * (1.0 - sig))).astype(BF16)
         db = (dm * swish).astype(BF16)
-        das[here] = da
-        dbs[here] = db
-        dh = dot(da, wg[0], ((1,), (1,))) + dot(db, wu[0], ((1,), (1,)))
-        dhs[e, here] = dh.astype(BF16)
-
-    @pl.loop(0, n_seqs)
-    def _(s):
-        chosen = places == pos[e, pl.ds(s, 1), :]
-        part = jnp.sum(jnp.where(chosen, dcol[slots_of(s, e)], 0.0), axis=0, keepdims=True)
-        dg[e, pl.ds(s, 1), :] = part
-
-    @pl.loop(0, D // 256)
-    def _(r):
-        here = pl.ds(pl.multiple_of(r * 256, 256), 256)
-        x = xs[:, here]
-        gg[0, here] = dot(x, das[...], ((0,), (0,))).astype(BF16)
-        gu[0, here] = dot(x, dbs[...], ((0,), (0,))).astype(BF16)
+        das[e, here] = da
+        dbs[e, here] = db
+        dh_slot = dot(da, wg[0], ((1,), (1,))) + dot(db, wu[0], ((1,), (1,)))
+        dhs[e, here] = dh_slot.astype(BF16)
+
+    @pl.loop(0, 8)
+    def _(member):
+        for part in range(2):
+            chosen = places == row_of(pos, member, part, e)
+            total = jnp.sum(
+                jnp.where(chosen, dcol[slots_of(member, part)], 0.0), axis=0, keepdims=True
+            )
+            qg[member, pl.ds(part * EXPERTS + first + e, 1), :] = total
 
     @pl.loop(0, FE // 256)
     def _(r):
@@ -923,23 +1068,60 @@
 
     @pl.when(e == HERE - 1)
     def _():
-        @pl.loop(0, n_seqs)
-        def _(s):
-            here = slots_of(s, e)
-            pick = jnp.concatenate(
-                [(places == pos[k, pl.ds(s, 1), :]).astype(F32).astype(BF16) for k in range(HERE)]
+        def combine(source, where, part):
+            @pl.loop(0, 8)
+            def _(member):
+                _, pick = picks(member, part)
+                here = slots_of(member, part)
+                stack = jnp.concatenate([source[k, here] for k in range(HERE)])
+                hg[where, member, part * LENGTH : (part + 1) * LENGTH] = dot(
+                    pick, stack, ((0,), (0,))
+                ).astype(BF16)
+
+        lines = Lines(send_sems, recv_sems)
+        sums = [
+            group_scatter(lines, me, hg.at[0], dh, 0, LENGTH, *scratch[12:24]),
+            group_scatter(lines, me, hg.at[0], dh, LENGTH, LENGTH, *scratch[24:36]),
+            group_scatter(lines, me, qg, dg, 0, 2 * EXPERTS, *scratch[0:12]),
+        ]
+        for part in range(2):
+            combine(dhs, 0, part)
+            step(sums[part])
+        step(sums[2])
+        for part in range(2):
+            combine(gs, 1, part)
+        keep = pltpu.make_async_copy(hg.at[1], qy, local_sems.at[0])
+        keep.start()
+        for k in range(HERE):
+            slot = k % 2
+            copies = (
+                pltpu.make_async_copy(gg_part.at[slot], gg.at[k], local_sems.at[1 + slot]),
+                pltpu.make_async_copy(gu_part.at[slot], gu.at[k], local_sems.at[3 + slot]),
             )
-            qy[s] = dot(
-                pick, jnp.concatenate([gys[k, here] for k in range(HERE)]), ((0,), (0,))
-            ).astype(BF16)
-            qh[s] = dot(
-                pick, jnp.concatenate([dhs[k, here] for k in range(HERE)]), ((0,), (0,))
-            ).astype(BF16)
+            if k >= 2:
+                for copy in copies:
+                    copy.wait()
+
+            @pl.loop(0, D // 256)
+            def _(r, k=k, slot=slot):
+                here = pl.ds(pl.multiple_of(r * 256, 256), 256)
+                x = xs[k, :, here]
+                gg_part[slot, here] = dot(x, das[k], ((0,), (0,))).astype(BF16)
+                gu_part[slot, here] = dot(x, dbs[k], ((0,), (0,))).astype(BF16)
+
+            for copy in copies:
+                copy.start()
+            step(*((), sums, sums[:1], sums[1:])[k])
+        drive(*sums)
+        for slot in range(2):
+            pltpu.make_async_copy(gg_part.at[slot], gg.at[2 + slot], local_sems.at[1 + slot]).wait()
+            pltpu.make_async_copy(gu_part.at[slot], gu.at[2 + slot], local_sems.at[3 + slot]).wait()
+        keep.wait()
+        lines.drain()
 
 
 def experts(h, g, pos, gates, wg, wu, wd):
-    n_seqs = h.shape[0]
-    rows = n_seqs * CAP
+    rows = 16 * CAP
     shape = jax.ShapeDtypeStruct
     whole = pl.BlockSpec(memory_space=pltpu.VMEM)
 
@@ -951,47 +1133,39 @@
         name="experts",
         grid=(HERE,),
         out_shape=(
-            shape((n_seqs, LENGTH, D), BF16),
-            shape((n_seqs, LENGTH, D), BF16),
-            shape((HERE, n_seqs, LENGTH), F32),
+            shape(h.shape, BF16),
+            shape(h.shape[1:], F32),
+            shape(gates.shape[1:], F32),
             shape((HERE, D, FE), BF16),
             shape((HERE, D, FE), BF16),
             shape((HERE, FE, D), BF16),
         ),
-        in_specs=[whole] * 4 + [per_expert(D, FE), per_expert(D, FE), per_expert(FE, D)],
-        out_specs=(whole, whole, whole, per_expert(D, FE), per_expert(D, FE), per_expert(FE, D)),
-        scratch_shapes=[pltpu.VMEM((rows, D), BF16)] * 3
-        + [pltpu.VMEM((HERE, rows, D), BF16)] * 2
-        + [pltpu.VMEM((rows, FE), BF16)] * 3
-        + [pltpu.VMEM((rows, LENGTH), F32)] * 2,
-        compiler_params=params(limit=60),
+        in_specs=anywhere(2)
+        + [whole] * 2
+        + [per_expert(D, FE), per_expert(D, FE), per_expert(FE, D)],
+        out_specs=anywhere(1) + [whole] * 2 + anywhere(2) + [per_expert(FE, D)],
+        scratch_shapes=[
+            pltpu.VMEM((2,) + h.shape, BF16),
+            pltpu.VMEM((HERE, rows, D), BF16),
+            pltpu.VMEM((HERE, rows, D), BF16),
+            pltpu.VMEM((rows, D), BF16),
+            pltpu.VMEM((HERE, rows, D), BF16),
+            pltpu.VMEM((rows, FE), BF16),
+            pltpu.VMEM((HERE, rows, FE), BF16),
+            pltpu.VMEM((HERE, rows, FE), BF16),
+            pltpu.VMEM((HERE, rows, LENGTH), F32),
+            pltpu.VMEM((rows, LENGTH), F32),
+            pltpu.VMEM(gates.shape, F32),
+            pltpu.VMEM((2, D, FE), BF16),
+            pltpu.VMEM((2, D, FE), BF16),
+            pltpu.SemaphoreType.DMA((5,)),
+        ]
+        + sems(36)
+        + scatter_scratch(gates.shape[1], gates.shape[2], F32)
+        + scatter_scratch(LENGTH, D, BF16)
+        + scatter_scratch(LENGTH, D, BF16),
+        compiler_params=params(1, 60),
     )(h, g, pos, gates, wg, wu, wd)
-
-
-def phases(segment):
-    length = segment.shape[0]
-    places = jnp.arange(length, dtype=jnp.int32)
-    same = segment[:, None] == segment[None, :]
-    visible = (places[None, :] <= places[:, None]) & same
-    offset = jnp.sum(visible.astype(F32), axis=1) - 1.0
-    halves = HEAD_DIM // 2
-    frequency = jnp.exp(-math.log(ROPE_BASE) * 2.0 * jnp.arange(halves).astype(F32) / HEAD_DIM)
-    angles = offset[:, None] * frequency[None, :]
-    cos, sin = jnp.cos(angles), jnp.sin(angles)
-    return (
-        jnp.concatenate([cos] * 4, axis=1),
-        jnp.concatenate([-sin, sin] * 2, axis=1),
-        visible.astype(F32),
-    )
-
-
-def slot_table(route_ids):
-    length = route_ids.shape[0]
-    ids = jnp.arange(EXPERTS, dtype=jnp.int32)
-    named = jnp.any(route_ids[None, :, :] == ids[:, None, None], axis=2)
-    before = jnp.arange(length)[:, None] < jnp.arange(length)[None, :]
-    count = jnp.dot(named.astype(BF16), before.astype(BF16), preferred_element_type=F32)
-    return jnp.where(named, count, -1.0)
 
 
 def on_device(
@@ -1012,55 +1186,42 @@
 ):
     micro = tokens.shape[0]
     rows = micro * LENGTH
-    first_expert = (lax.axis_index("fsdp") // 4) * 4
-    cos, sin, keep = jax.vmap(phases)(segments[:, 0])
-    cos, sin = cos.reshape(rows, 128), sin.reshape(rows, 128)
-    slots = jnp.swapaxes(jax.vmap(slot_table)(routes[:, 0]), 0, 1).reshape(EXPERTS, rows)
-    small = jnp.concatenate(
-        [w_router, attn_gain[:, None], moe_gain[:, None], jnp.zeros((32, 94), BF16)], axis=1
-    )
-    pack = jnp.concatenate([w_query, w_key, w_value, w_output, small], axis=1)
     inputs = tokens.reshape(rows, D)
     upstream = cotangent.reshape(rows, D)
-    dense, gbuf, sbuf, wgb, wub, wdb, hbuf, gatebuf, q, k, v, p, o, y1, gates = front(
-        inputs, cos, sin, keep, slots, pack, upstream, w_gate[0], w_up[0], w_down[0]
+    dense, gbuf, sbuf, wgb, wub, wdb, hbuf, gatebuf, q, k, v, p, o, y1, gates, cos, sin = front(
+        inputs,
+        segments[:, 0],
+        routes.reshape(rows, TOPK),
+        w_query,
+        w_key,
+        w_value,
+        w_output,
+        w_router,
+        jnp.stack([attn_gain, moe_gain]).astype(F32),
+        upstream,
+        w_gate[0],
+        w_up[0],
+        w_down[0],
     )
 
-    def mine(buf):
-        part = lax.dynamic_slice_in_dim(buf, first_expert, HERE, axis=1)
-        return jnp.swapaxes(part, 0, 1).reshape(HERE, 8 * micro, LENGTH)
-
-    qy, qh, dg, gg, gu, gd = experts(
-        hbuf.reshape(8 * micro, LENGTH, D),
-        gbuf.reshape(8 * micro, LENGTH, D),
-        mine(sbuf),
-        mine(gatebuf),
-        wgb,
-        wub,
-        wdb,
-    )
-    qg = lax.dynamic_update_slice_in_dim(
-        jnp.zeros((8, EXPERTS, rows), F32),
-        jnp.swapaxes(dg.reshape(HERE, 8, rows), 0, 1),
-        first_expert,
-        axis=1,
-    )
-    dh, gate_grad = send_back(qh.reshape(8, rows, D), qg)
+    qy, dh, gate_grad, gg, gu, gd = experts(hbuf, gbuf, sbuf, gatebuf, wgb, wub, wdb)
     grads, grad_tokens, result, tg, tu, td = retreat(
         inputs, cos, sin, gates, dense.reshape(D, WIDE), upstream, y1, q, k, v, p, o, dh, gate_grad,
-        qy.reshape(8, rows, D), gg, gu, gd,
+        qy, gg, gu, gd,
     )
-    summed, grad_gate, grad_up, grad_down = settle(grads, tg, tu, td)
+    gq, gk, gv, go, gsmall, grad_gate, grad_up, grad_down, grad_tokens, result = finish(
+        *settle(grads, tg, tu, td), grad_tokens, result
+    )
     return (
         result.reshape(micro, 1, LENGTH, D),
         grad_tokens.reshape(micro, 1, LENGTH, D),
-        summed[:, 3104],
-        summed[:, 3105],
-        summed[:, :1024],
-        summed[:, 1024:1536],
-        summed[:, 1536:2048],
-        summed[:, 2048:3072],
-        summed[:, 3072:3104],
+        gsmall[:, 32],
+        gsmall[:, 33],
+        gq,
+        gk,
+        gv,
+        go,
+        gsmall[:, :32],
         grad_gate.reshape(1, D, FE),
         grad_up.reshape(1, D, FE),
         grad_down.reshape(1, FE, D),

time: 383 us -> 324 us (0.85)
  Pallas kernels: 355 us -> 318 us
  local copies, waits for them, and re-layouts: 22 us -> 2.98 us
    pallas_call x2, Pallas kernels: 92.7 us -> 62.3 us  [the longest x1 56 us: settle(): pl.pallas_call(settle_kernel, name='settle', out_shape=(shape((32, 1024),...]
    pallas_call x1, Pallas kernels: 118 us -> 105 us  [front(): pl.pallas_call(front_kernel, name='front', out_shape=(shape((2, 4, 4, 32,...]
    pallas_call x1, Pallas kernels: 70.1 us -> 79.8 us  [experts(): pl.pallas_call(experts_kernel, name='experts', grid=(HERE,), out_shape=(s...]
    unnamed x15 -> x1, local copies, waits for them, and re-layouts: 8.34 us -> 1.48 us
    slice x4 -> x1, local copies, waits for them, and re-layouts: 6.12 us -> 1.5 us  [on_device(): gsmall[:, 33]]
where the time goes in v3:
time: 324 us; the launch traced here: 322 us
  Pallas kernels  318 us (98%)
    pallas_call x1, Pallas kernels, front(): pl.pallas_call(front_kernel, name='front', out_shape=(shape((2, 4, 4, 32,...  105 us
    pallas_call x1, Pallas kernels, experts(): pl.pallas_call(experts_kernel, name='experts', grid=(HERE,), out_shape=(s...  79.8 us
    pallas_call x1, Pallas kernels, retreat(): pl.pallas_call(retreat_kernel, name='retreat', out_shape=(shape((D, WIDE)...  70.8 us
    pallas_call x1, Pallas kernels, settle(): pl.pallas_call(settle_kernel, name='settle', out_shape=(shape((32, 1024),...  56 us

profile of v3, /device:TPU:1, one launch (start us, length us, event | category | flops | bytes accessed | tf_op | source)
XLA Modules:
  0.0 322.5 jit_solution(5897630075671270830)
XLA Ops:
  0.6 1.2 maximum_convert_fusion.gains
  1.9 1.5 copy.29
  3.4 104.7 %front.1 = (bf16[2,4,4,32,3200]{4,3,2,1,0:T(8,128)(2,1)}, bf16[8,256,1024]{2,1,0:T(8,128)(2,1)}, f32[8,64,128]{2,1,0:T(8,128)}, bf16[4,1024,512]{2,1,0:T(8,128)(...) custom-call(bf16[256,1024]{1,0:T(8,128)(2,1)} %bitcast.29, ...), custom_call_target="tpu_custom_call" | custom-call | tf_op jit(solution)/shard_map/front/pallas_call | solution.py:617
  108.1 79.8 %experts.1 = (bf16[8,256,1024]{2,1,0:T(8,128)(2,1)}, f32[256,1024]{1,0:T(8,128)}, f32[64,128]{1,0:T(8,128)}, bf16[4,1024,512]{2,1,0:T(8,128)(2,1)}, bf16[4,1024,...) custom-call(bf16[8,256,1024]{2,1,0:T(8,128)(2,1)} %get-tuple-element.69.h_all, ...), custom_call_target="tpu_custom_call" | custom-call | tf_op jit(solution)/shard_map/experts/pallas_call | solution.py:1131
  187.9 70.8 %retreat.1 = (bf16[1024,3200]{1,0:T(8,128)(2,1)}, f32[256,1024]{1,0:T(8,128)}, bf16[256,1024]{1,0:T(8,128)(2,1)}, bf16[2,4,64,512]{3,2,1,0:T(8,128)(2,1)}, bf16[...) custom-call(bf16[256,1024]{1,0:T(8,128)(2,1)} %bitcast.30, f32[256,128]{1,0:T(8,128)} %get-tuple-element.59.cos, ...), custom_call_target="tpu_custom_call" | custom-call | tf_op jit(solution)/shard_map/retreat/pallas_call | solution.py:785
  258.7 56.0 %settle.1 = (f32[32,1024]{1,0:T(8,128)}, f32[32,512]{1,0:T(8,128)}, f32[32,512]{1,0:T(8,128)}, f32[32,1024]{1,0:T(8,128)}, f32[32,128]{1,0:T(8,128)}, /*index=5*...) custom-call(bf16[2,4,4,32,3200]{4,3,2,1,0:T(8,128)(2,1)} %bitcast.24, ...), custom_call_target="tpu_custom_call" | custom-call | tf_op jit(solution)/shard_map/settle/pallas_call | solution.py:921
  314.6 6.3 %finish.1 = (f32[32,1024]{1,0:T(8,128)}, f32[32,512]{1,0:T(8,128)}, f32[32,512]{1,0:T(8,128)}, f32[32,1024]{1,0:T(8,128)}, f32[32,128]{1,0:T(8,128)}, /*index=5*...) custom-call(f32[32,1024]{1,0:T(8,128)} %get-tuple-element.86.refs_0_, ...), custom_call_target="tpu_custom_call" | custom-call | tf_op jit(solution)/shard_map/finish/pallas_call | solution.py:962
  321.0 1.5 slice_reduce_fusion

commit v4 on v3

--- a/solution.py
+++ b/solution.py
@@ -74,7 +74,7 @@
 
 class Lines:
     def __init__(self, send_sems, recv_sems):
-        self.send_sems, self.recv_sems, self.copies = send_sems, recv_sems, []
+        self.send_sems, self.recv_sems, self.copies, self.left = send_sems, recv_sems, [], 0
 
     def send(self, src, dst, device):
         i = len(self.copies)
@@ -92,8 +92,9 @@
         return copy
 
     def drain(self):
-        for copy in self.copies:
+        for copy in self.copies[self.left :]:
             copy.wait_send()
+        self.left = len(self.copies)
 
 
 def step(*chains):
@@ -136,7 +137,7 @@
     spread(far)
 
 
-def group_gather(lines, me, source, buf, start=0, rows=None):
+def group_gather(lines, me, source, buf, start=0, rows=None, last=True):
     rows = rows or buf.shape[1]
     ahead, behind, far = lax.rem(me.x + 1, 4), lax.rem(me.x + 3, 4), lax.rem(me.x + 2, 4)
     right, left, cross = me.right(), me.left(), me.cross()
@@ -162,20 +163,35 @@
     yield
     c.wait_recv()
     d.wait_recv()
-    h = lines.send(slot(base + far), slot(base + far), cross)
-    yield
+    if last:
+        h = lines.send(slot(base + far), slot(base + far), cross)
+        yield
+        h.wait_recv()
     f.wait_recv()
     g.wait_recv()
-    h.wait_recv()
-
-
-def tiles(rows, step, body):
-    @pl.loop(0, rows // step)
-    def _(i):
-        body(pl.ds(pl.multiple_of(i * step, step), step))
-
-
-def group_scatter(lines, me, q, out, start, rows, by, sf, tl, tr, t, hl, hr, nl, nr, fl, fr, fy):
+
+
+def weight_chain(lines, me, shared, source, buf):
+    half_rows = source.shape[0] // 2
+    quarter = half_rows // 2
+    start = me.core * half_rows
+    mine = pl.ds(pl.multiple_of(start, half_rows), half_rows)
+
+    def slot(p):
+        return buf.at[p, mine]
+
+    def half(p, k):
+        return buf.at[p, pl.ds(pl.multiple_of(start + k * quarter, quarter), quarter)]
+
+    def spread(p):
+        shared.append(lines.send(slot(p), slot(p), me.sibling()))
+
+    yield from ring_gather(
+        lines, source.at[mine], slot, half, me.z, me.above(), me.below(), spread=spread
+    )
+
+
+def group_scatter(lines, me, q, out, start, rows, by, tl, tr, hl, hr, fl, fr, fy):
     mid = rows // 2
     step_rows = min(32, mid)
     ahead, behind, far = lax.rem(me.x + 1, 4), lax.rem(me.x + 3, 4), lax.rem(me.x + 2, 4)
@@ -205,36 +221,36 @@
     e.wait_recv()
 
     def far_sum(here, there):
-        sf[here] = q[base + far, there] + by[here]
+        by[here] = q[base + far, there] + by[here]
 
     each(rows, 0, far_sum)
-    j1 = lines.send(sf.at[first], hl, right)
-    j2 = lines.send(sf.at[second], hr, left)
+    j1 = lines.send(by.at[first], hl, right)
+    j2 = lines.send(by.at[second], hr, left)
     yield
     g1.wait_recv()
     g2.wait_recv()
 
     def partner_sum(here, there):
         total = q[other + me.x, there].astype(F32) + tl[here].astype(F32) + tr[here].astype(F32)
-        t[here] = total.astype(t.dtype)
+        tl[here] = total.astype(tl.dtype)
 
     each(rows, 0, partner_sum)
-    k = lines.send(t, fy, cross)
+    k = lines.send(tl, fy, cross)
     yield
     j1.wait_recv()
 
     def right_sum(here, there):
-        nl[here] = q[base + ahead, there] + hl[here]
+        hl[here] = q[base + ahead, there] + hl[here]
 
     each(mid, 0, right_sum)
-    l1 = lines.send(nl, fl.at[first], right)
+    l1 = lines.send(hl, fl.at[first], right)
     j2.wait_recv()
 
     def left_sum(here, there):
-        nr[here] = q[base + behind, there] + hr[here]
+        hr[here] = q[base + behind, there] + hr[here]
 
     each(mid, mid, left_sum)
-    l2 = lines.send(nr, fr.at[second], left)
+    l2 = lines.send(hr, fr.at[second], left)
     yield
     for copy in (i1, i2, l1, l2, k):
         copy.wait_recv()
@@ -406,8 +422,8 @@
 
 
 def front_kernel(
-    tokens, segments, routes, wq_own, wk_own, wv_own, wo_own, wr_own, gains, g, wg, wu, wd,
-    dense, gbuf, sbuf, wgb, wub, wdb, hbuf, gatebuf, q, k, v, p, o, y1, gates, cos, sin,
+    tokens, segments, routes, wq_own, wk_own, wv_own, wo_own, wr_own, gains, g, wg, wu,
+    dense, gbuf, sbuf, wgb, wub, h2, q, k, v, p, o, y1, gates, cos, sin,
     dn, h, keep, slots, send_sems, recv_sems, local_sems,
 ):
     me = Place()
@@ -419,7 +435,6 @@
         pltpu.make_async_copy(g, gbuf.at[own], local_sems.at[1]),
         pltpu.make_async_copy(wg, wgb.at[me.z], local_sems.at[3]),
         pltpu.make_async_copy(wu, wub.at[me.z], local_sems.at[4]),
-        pltpu.make_async_copy(wd, wdb.at[me.z], local_sems.at[5]),
     ]
     for copy in local:
         copy.start()
@@ -482,31 +497,6 @@
         step(*units[1:])
         step(*units)
 
-    def weight_chain(source, buf):
-        half_rows = source.shape[0] // 2
-        quarter = half_rows // 2
-        start = me.core * half_rows
-
-        def slot(p):
-            return buf.at[p, pl.ds(pl.multiple_of(start, half_rows), half_rows)]
-
-        def half(p, k):
-            return buf.at[p, pl.ds(pl.multiple_of(start + k * quarter, quarter), quarter)]
-
-        def spread(p):
-            shared.append(lines.send(slot(p), slot(p), sibling))
-
-        yield from ring_gather(
-            lines,
-            source.at[pl.ds(pl.multiple_of(start, half_rows), half_rows)],
-            slot,
-            half,
-            me.z,
-            above,
-            below,
-            spread=spread,
-        )
-
     swap = lines.send(shard.at[rows], shard.at[rows], cross)
     for part in range(2):
         here = slice(part * LENGTH, (part + 1) * LENGTH)
@@ -515,18 +505,18 @@
     local.append(pltpu.make_async_copy(slots, sbuf.at[own], local_sems.at[2]))
     local[-1].start()
     swap.wait_recv()
-    gs = group_gather(lines, me, g, gbuf)
+    gs = group_gather(lines, me, g, gbuf, last=False)
     ss = group_gather(lines, me, slots, sbuf)
-    w1, w2, w3 = weight_chain(wg, wgb), weight_chain(wu, wub), weight_chain(wd, wdb)
+    w1 = weight_chain(lines, me, shared, wg, wgb)
+    w2 = weight_chain(lines, me, shared, wu, wub)
     dense_a, dense_b = dense_chain(pl.ds(0, CUT), False), dense_chain(pl.ds(CUT, WIDE - CUT), True)
-    for _ in range(4):
-        step(dense_a, dense_b)
+    step(dense_a, dense_b)
     step(gs, ss, w1)
     drive(dense_a, dense_b)
     for copy in shared:
         copy.wait_recv()
     del shared[:]
-    step(gs, ss)
+    step(gs, ss, w2)
     keeping = pltpu.make_async_copy(dn, dense, local_sems.at[6])
     keeping.start()
 
@@ -552,7 +542,7 @@
                 u * cos[...] + swap_halves(u) * sin[...]
             ).astype(BF16)
     v[...] = dot(h[...], weight(1536, 512)).astype(BF16)
-    step(w1, w2)
+    step(w1)
 
     def attend(i):
         s, m = lax.div(i, 4), lax.rem(i, 4)
@@ -571,46 +561,34 @@
             both = dot(probs.astype(BF16), doubled(v_tile, odd))
             o[here, q_column] = side_by_side(both).astype(BF16)
 
-    late = []
-    routed = []
     for part in range(2):
 
         @pl.loop(part * 4, part * 4 + 4)
         def _(i):
             attend(i)
 
-        here = slice(part * LENGTH, (part + 1) * LENGTH)
-        middle = tokens[here].astype(F32) + RESIDUAL * dot(o[here], weight(2048, 1024))
-        y1[here] = middle
-        h[here] = (middle * norm_scale(middle) * gain_two).astype(BF16)
-        routed.append(group_gather(lines, me, h.at[here], hbuf, part * LENGTH, LENGTH))
-        step(routed[part])
-        late.append(pltpu.make_async_copy(h.at[here], hbuf.at[own, here], local_sems.at[7 + part]))
-        late[part].start()
-        logits = dot(small, h[here], ((0,), (1,)))[:EXPERTS]
-        table = slice(part * EXPERTS, (part + 1) * EXPERTS)
-        named = slots[table] >= 0.0
-        top = jnp.max(jnp.where(named, logits, -jnp.inf), axis=0, keepdims=True)
-        raised = jnp.where(named, jnp.exp(jnp.where(named, logits - top, 0.0)), 0.0)
-        gates[table] = raised / jnp.sum(raised, axis=0, keepdims=True)
-
-    weighed = group_gather(lines, me, gates, gatebuf)
-    late.append(pltpu.make_async_copy(gates, gatebuf.at[own], local_sems.at[9]))
-    late[2].start()
-    step(weighed, w3, gs, ss)
-    step(routed[0], w2)
-    step(routed[1], weighed, w1, w3)
-    step(routed[0], w2)
-    step(routed[1], weighed)
-    drive(routed[0], routed[1], weighed, gs, ss, w1, w2, w3)
+        if part == 0:
+            step(w2, ss)
+
+    middle = tokens[...].astype(F32) + RESIDUAL * dot(o[...], weight(2048, 1024))
+    y1[...] = middle
+    h2[...] = (middle * norm_scale(middle) * gain_two).astype(BF16)
+    logits = dot(small, h2[...], ((0,), (1,)))[:EXPERTS]
+    named = side(slots) >= 0.0
+    top = jnp.max(jnp.where(named, logits, -jnp.inf), axis=0, keepdims=True)
+    raised = jnp.where(named, jnp.exp(jnp.where(named, logits - top, 0.0)), 0.0)
+    raised = raised / jnp.sum(raised, axis=0, keepdims=True)
+    gates[:EXPERTS] = raised[:, :LENGTH]
+    gates[EXPERTS:] = raised[:, LENGTH:]
+    drive(ss, w1, w2, gs)
     for copy in shared:
         copy.wait_recv()
-    for copy in local + [keeping] + late:
+    for copy in local + [keeping]:
         copy.wait()
     lines.drain()
 
 
-def front(tokens, segments, routes, wq, wk, wv, wo, wr, gains, g, wg, wu, wd):
+def front(tokens, segments, routes, wq, wk, wv, wo, wr, gains, g, wg, wu):
     shape = jax.ShapeDtypeStruct
     rows = tokens.shape[0]
     slots = shape((2 * EXPERTS, LENGTH), F32)
@@ -623,9 +601,7 @@
             shape((8,) + slots.shape, F32),
             shape((4,) + wg.shape, BF16),
             shape((4,) + wu.shape, BF16),
-            shape((4,) + wd.shape, BF16),
-            shape((8, rows, D), BF16),
-            shape((8,) + slots.shape, F32),
+            shape((rows, D), BF16),
             shape((rows, 1024), BF16),
             shape((rows, 512), BF16),
             shape((rows, 512), BF16),
@@ -636,8 +612,8 @@
             shape((rows, 128), F32),
             shape((rows, 128), F32),
         ),
-        in_specs=vmem(13),
-        out_specs=anywhere(8) + vmem(9),
+        in_specs=vmem(12),
+        out_specs=anywhere(5) + vmem(10),
         scratch_shapes=[
             pltpu.VMEM((2, 4, 4, 32, WIDE), BF16),
             pltpu.VMEM((rows, D), BF16),
@@ -645,37 +621,52 @@
             pltpu.VMEM(slots.shape, F32),
         ]
         + sems(140)
-        + [pltpu.SemaphoreType.DMA((10,))],
+        + [pltpu.SemaphoreType.DMA((7,))],
         compiler_params=params(0),
-    )(tokens, segments, routes, wq, wk, wv, wo, wr, gains, g, wg, wu, wd)
+    )(tokens, segments, routes, wq, wk, wv, wo, wr, gains, g, wg, wu)
 
 
 def scatter_scratch(rows, columns, dtype):
     full = pltpu.VMEM((rows, columns), dtype)
     half = pltpu.VMEM((rows // 2, columns), dtype)
-    return [full] * 5 + [half] * 4 + [full] * 3
+    return [full] * 3 + [half] * 2 + [full] * 3
 
 
 def retreat_kernel(
     tokens, cos, sin, gates, dense, g, y1, q, k, v, p, o, dh, dg, qy, gg, gu, gd,
-    grads, grad_tokens, result, tg, tu, td,
+    grads, got, grad_tokens, result, tg, tu, td,
     h, do, dq, dk, dv, small_grad, mixture, *scratch,
 ):
     me = Place()
     send_sems, recv_sems, local_sems = scratch[:3]
-    above, below, sibling = me.above(), me.below(), me.sibling()
+    above, below = me.above(), me.below()
     local = []
     for i, (grad, acc) in enumerate(((gg, scratch[4]), (gu, scratch[10]), (gd, scratch[16]))):
-        local.append(pltpu.make_async_copy(grad.at[:, me.core], acc, local_sems.at[i]))
+        local.append(pltpu.make_async_copy(grad.at[0], acc, local_sems.at[i]))
         local[-1].start()
-    greet((me.right(), me.left(), me.cross(), above, below, sibling))
+    for i, (grad, rc) in enumerate(((gg, scratch[3]), (gu, scratch[9]), (gd, scratch[15]))):
+        local.append(pltpu.make_async_copy(grad.at[1], rc, local_sems.at[3 + i]))
+        local[-1].start()
+    greet((me.right(), me.left(), me.cross(), above, below, me.sibling()))
     lines = Lines(send_sems, recv_sems)
 
-    def chain(grad, tot, mine, rc, acc, hl, hr, fl, fr):
-        first = lines.send(grad.at[:, 1 - me.core], rc, sibling)
-        yield
+    theirs = pl.ds(pl.multiple_of((1 - me.core) * 16, 16), 16)
+    handed = []
+
+    def keep_rows(t, columns, value):
+        shards = value.astype(BF16).reshape(2, 4, 32, value.shape[1])
+        grads[t // 2, (t % 2) * 2 : (t % 2) * 2 + 2, :, :, columns] = shards
+
+    def hand(columns):
+        handed.append(
+            lines.send(
+                grads.at[:, :, :, theirs, columns], got.at[:, :, :, :, columns], me.sibling()
+            )
+        )
+
+    def chain(tot, mine, theirs_in, rc, acc, hl, hr, fl, fr):
         mine.wait()
-        first.wait_recv()
+        theirs_in.wait()
 
         @pl.loop(0, 32)
         def _(i):
@@ -687,11 +678,11 @@
 
         yield from ring_scatter(lines, acc, me.z, above, below, hl, hr, fl, fr, store)
 
-    e1 = chain(gg, tg, local[0], *scratch[3:9])
-    e2 = chain(gu, tu, local[1], *scratch[9:15])
-    e3 = chain(gd, td, local[2], *scratch[15:21])
-    ys = group_scatter(lines, me, qy, mixture, 0, 2 * LENGTH, *scratch[21:33])
-    step(e1, e2, e3, ys)
+    e1 = chain(tg, local[0], local[3], *scratch[3:9])
+    e2 = chain(tu, local[1], local[4], *scratch[9:15])
+    e3 = chain(td, local[2], local[5], *scratch[15:21])
+    ys = group_scatter(lines, me, qy, mixture, 0, 2 * LENGTH, *scratch[21:29])
+    step(e1, ys)
 
     small = dense[:, 3072:3200]
     gain_one, gain_two = gain_rows(small)
@@ -712,12 +703,13 @@
     dy = g[...].astype(F32) + scale * (dn - normed * jnp.mean(dn * normed, axis=1, keepdims=True))
     grad_tokens[...] = dy
     dz = (RESIDUAL * dy).astype(BF16)
-    step(e1)
+    step(e2)
     for t in range(4):
         here = slice(t * 256, t * 256 + 256)
-        grads[here, 2048:3072] = dot(o[:, here], dz, ((0,), (0,))).astype(BF16)
+        keep_rows(t, pl.ds(2048, 1024), dot(o[:, here], dz, ((0,), (0,))))
+    hand(pl.ds(2048, 1024))
     do[...] = dot(dz, dense[:, 2048:3072], ((1,), (1,))).astype(BF16)
-    step(e2)
+    step(e1, ys)
 
     def attend_back(i):
         s, m = lax.div(i, 4), lax.rem(i, 4)
@@ -747,32 +739,38 @@
         def _(i):
             attend_back(i)
 
-        step((e3, ys, e1, e2)[part])
+        step(*((e3,), (ys, e2), (e1,), (ys, e3))[part])
 
     for t in range(4):
         here = slice(t * 256, t * 256 + 256)
-        grads[here, 0:1024] = dot(h[:, here], dq[...], ((0,), (0,))).astype(BF16)
-        grads[here, 1024:1536] = dot(h[:, here], dk[...], ((0,), (0,))).astype(BF16)
-        grads[here, 1536:2048] = dot(h[:, here], dv[...], ((0,), (0,))).astype(BF16)
+        keep_rows(t, pl.ds(0, 1024), dot(h[:, here], dq[...], ((0,), (0,))))
+        keep_rows(t, pl.ds(1024, 512), dot(h[:, here], dk[...], ((0,), (0,))))
+        keep_rows(t, pl.ds(1536, 512), dot(h[:, here], dv[...], ((0,), (0,))))
+    hand(pl.ds(0, 2048))
     dh1 = (
         dot(dq[...], dense[:, 0:1024], ((1,), (1,)))
         + dot(dk[...], dense[:, 1024:1536], ((1,), (1,)))
         + dot(dv[...], dense[:, 1536:2048], ((1,), (1,)))
     )
-    step(e3, ys)
+    step(e2, ys)
     x = tokens[...].astype(F32)
     scale = norm_scale(x)
     normed = x * scale
-    grads[:, 3072:3200] = (small_grad[...] + column_sums(dh1 * normed, EXPERTS)).astype(BF16)
+    small_sum = small_grad[...] + column_sums(dh1 * normed, EXPERTS)
+    for t in range(4):
+        keep_rows(t, pl.ds(3072, 128), small_sum[t * 256 : t * 256 + 256])
+    hand(pl.ds(3072, 128))
     dn = dh1 * gain_one
     grad_tokens[...] += scale * (dn - normed * jnp.mean(dn * normed, axis=1, keepdims=True))
     drive(ys, e1, e2, e3)
     result[...] = (y1[...] + RESIDUAL * mixture[...]).astype(BF16)
+    for copy in handed:
+        copy.wait_recv()
     lines.drain()
 
 
 def halves(r, w):
-    return (4, 2, 2, 4, r, w)
+    return (2, 4, 2, 4, r, w)
 
 
 def retreat(tokens, cos, sin, gates, dense, g, y1, q, k, v, p, o, dh, dg, qy, gg, gu, gd):
@@ -786,7 +784,8 @@
         retreat_kernel,
         name="retreat",
         out_shape=(
-            shape((D, WIDE), BF16),
+            shape((2, 4, 4, 32, WIDE), BF16),
+            shape((2, 4, 4, 16, WIDE), BF16),
             shape((rows, D), F32),
             shape((rows, D), BF16),
             shape((2, 4, 64, 512), BF16),
@@ -794,7 +793,7 @@
             shape((2, 4, 32, 1024), BF16),
         ),
         in_specs=vmem(15) + anywhere(3),
-        out_specs=vmem(6),
+        out_specs=vmem(1) + anywhere(1) + vmem(5),
         scratch_shapes=[
             pltpu.VMEM((rows, D), BF16),
             pltpu.VMEM((rows, 1024), BF16),
@@ -805,7 +804,7 @@
             pltpu.VMEM((rows, D), F32),
         ]
         + sems(40)
-        + [pltpu.SemaphoreType.DMA((3,))]
+        + [pltpu.SemaphoreType.DMA((6,))]
         + scratch(64, 512)
         + scratch(64, 512)
         + scratch(32, 1024)
@@ -817,7 +816,7 @@
     )
 
 
-def settle_kernel(grads, tg, tu, td, oq, ok, ov, oo, osmall, og, ou, od, rc, out, *scratch):
+def settle_kernel(grads, rc, tg, tu, td, oq, ok, ov, oo, osmall, og, ou, od, out, *scratch):
     me = Place()
     send_sems, recv_sems = scratch[:2]
     right, left, above, below = me.right(), me.left(), me.above(), me.below()
@@ -827,14 +826,7 @@
     mine = pl.ds(pl.multiple_of(me.core * 16, 16), 16)
     theirs = pl.ds(pl.multiple_of((1 - me.core) * 16, 16), 16)
 
-    def swap(columns):
-        return lines.send(grads.at[:, :, :, theirs, columns], rc.at[:, :, :, :, columns], sibling)
-
-    swaps = [swap(pl.ds(0, CUT)), swap(pl.ds(CUT, WIDE - CUT))]
-
-    def chain(swap, columns, x_first, acc, second, hl, hr, fl, fr, hl2, hr2, fl2, fr2, r2, ry, r3, yb):
-        swap.wait_recv()
-
+    def chain(columns, x_first, acc, second, hl, hr, fl, fr, hl2, hr2, fl2, fr2, r2, ry, r3, yb):
         @pl.loop(0, 32)
         def _(i):
             k, x, z = lax.div(i, 16), lax.rem(lax.div(i, 4), 4), lax.rem(i, 4)
@@ -884,10 +876,12 @@
 
     others = [swapped(t, w, s) for t, w, s in zip((tg, tu, td), (og, ou, od), scratch[30:33])]
     step(*others)
-    one = chain(swaps[0], pl.ds(0, CUT), True, *scratch[2:16])
-    two = chain(swaps[1], pl.ds(CUT, WIDE - CUT), False, *scratch[16:30])
+    one = chain(pl.ds(0, CUT), True, *scratch[2:16])
+    two = chain(pl.ds(CUT, WIDE - CUT), False, *scratch[16:30])
     step(one)
-    step(one, two)
+    step(one)
+    step(two)
+    step(two)
     drive(one, two)
     drive(*others)
     start = 0
@@ -897,7 +891,7 @@
     lines.drain()
 
 
-def settle(grads, tg, tu, td):
+def settle(grads, got, tg, tu, td):
     def scratch(w):
         shapes = [
             (4, 2, 4, 16, w),
@@ -931,15 +925,15 @@
             shape((2, 2, 4, 64, 512), F32),
             shape((2, 2, 4, 32, 1024), F32),
         ),
-        in_specs=vmem(4),
+        in_specs=vmem(5),
         out_specs=vmem(8),
-        scratch_shapes=[pltpu.VMEM((2, 4, 4, 16, WIDE), BF16), pltpu.VMEM((32, WIDE), F32)]
+        scratch_shapes=[pltpu.VMEM((32, WIDE), F32)]
         + sems(48)
         + scratch(CUT)
         + scratch(WIDE - CUT)
         + [pltpu.VMEM(t.shape, BF16) for t in (tg, tu, td)],
         compiler_params=params(3),
-    )(grads.reshape(2, 4, 4, 32, WIDE), tg, tu, td)
+    )(grads, got, tg, tu, td)
 
 
 def finish_kernel(*refs):
@@ -971,201 +965,282 @@
     )(*arrays)
 
 
+HALF = 8 * CAP
+TILE = 384
+
+
 def experts_kernel(
-    h_all, g_all, pos, gates, wg, wu, wd,
+    h2, own_gates, g_all, pos, wg_all, wu_all, wd,
     qy, dh, dg, gg, gu, gd,
-    hg, xs, gs, dys, dhs, ms, das, dbs, gcol, dcol, qg, gg_part, gu_part, local_sems, send_sems, recv_sems, *scratch,
+    hb, gb, gates, wdb, wg, wu, xs, gs, ms, das, dbs, gys, dhs, gcol, dcol, qg, gg_part, gu_part, gd_part,
+    local_sems, send_sems, recv_sems, hand_send, hand_recv, *scratch,
 ):
-    e = pl.program_id(0)
     me = Place()
-    partners = (me.right(), me.left(), me.cross())
+    own = me.high * 4 + me.x
     first = me.high * 16 + me.x * 4
-    n_seqs = 16
-    rows = n_seqs * CAP
+    rows = 2 * HALF
     places = lax.broadcasted_iota(jnp.int32, (CAP, LENGTH), 0).astype(F32)
+
+    def fetch(e):
+        slot = lax.rem(e, 2)
+        return (
+            pltpu.make_async_copy(wg_all.at[e], wg.at[slot], local_sems.at[slot]),
+            pltpu.make_async_copy(wu_all.at[e], wu.at[slot], local_sems.at[2 + slot]),
+        )
+
+    base, other = me.high * 4, (1 - me.high) * 4
+    ahead, behind, far = lax.rem(me.x + 1, 4), lax.rem(me.x + 3, 4), lax.rem(me.x + 2, 4)
+    local = [
+        pltpu.make_async_copy(h2, hb.at[own], local_sems.at[4]),
+        pltpu.make_async_copy(own_gates, gates.at[own], local_sems.at[5]),
+        pltpu.make_async_copy(wd, wdb.at[me.z], local_sems.at[6]),
+        pltpu.make_async_copy(g_all.at[pl.ds(base, 4)], gb.at[pl.ds(base, 4)], local_sems.at[7]),
+    ] + [
+        pltpu.make_async_copy(g_all.at[other + p], gb.at[other + p], local_sems.at[8 + i])
+        for i, p in enumerate((me.x, ahead, behind))
+    ]
+    for copy in (*local, *fetch(0), *fetch(1)):
+        copy.start()
+    greet((me.right(), me.left(), me.cross(), me.above(), me.below(), me.sibling()))
+    lines = Lines(send_sems, recv_sems)
+    shared = []
+    weighed = group_gather(lines, me, own_gates, gates)
+    h0 = group_gather(lines, me, h2.at[pl.ds(0, LENGTH)], hb, 0, LENGTH)
+    h1 = group_gather(lines, me, h2.at[pl.ds(LENGTH, LENGTH)], hb, LENGTH, LENGTH)
+    w3 = weight_chain(lines, me, shared, wd, wdb)
+    step(weighed, h0, w3)
+    last_g = lines.send(g_all.at[base + far], gb.at[base + far], me.cross())
+    qg[...] = jnp.zeros_like(qg)
+    step(weighed, h0)
+    step(h1)
+    step(w3)
+    step(weighed, h0)
+    step(h1)
+    step(weighed)
+    last_g.wait_recv()
+    for copy in local:
+        copy.wait()
 
     def row_of(table, member, part, k):
         return table[member, pl.ds(part * EXPERTS + first + k, 1), :]
 
-    def slots_of(member, part):
-        return pl.ds(pl.multiple_of((member * 2 + part) * CAP, CAP), CAP)
+    def slots_of(member):
+        return pl.ds(pl.multiple_of(member * CAP, CAP), CAP)
+
+    def all_slots_of(member, part):
+        return pl.ds(pl.multiple_of(part * HALF + member * CAP, CAP), CAP)
 
     def picks(member, part):
         chosen = [places == row_of(pos, member, part, k) for k in range(HERE)]
         return chosen, jnp.concatenate([c.astype(F32).astype(BF16) for c in chosen])
 
-    @pl.when(e == 0)
-    def _():
-        loads = [
-            pltpu.make_async_copy(h_all, hg.at[0], local_sems.at[0]),
-            pltpu.make_async_copy(g_all, hg.at[1], local_sems.at[1]),
-        ]
-        for load in loads:
-            load.start()
-        greet(partners)
-        qg[...] = jnp.zeros_like(qg)
-        for load in loads:
-            load.wait()
-
+    def gather_g(part):
         @pl.loop(0, 8)
         def _(member):
-            for part in range(2):
-                chosen, pick = picks(member, part)
-                here = slots_of(member, part)
-                tokens = slice(part * LENGTH, (part + 1) * LENGTH)
-                got = dot(pick, hg[0, member, tokens]).astype(BF16)
-                for k in range(HERE):
-                    xs[k, here] = got[k * CAP : (k + 1) * CAP]
-                got = dot(pick, hg[1, member, tokens]).astype(BF16)
-                for k in range(HERE):
-                    gs[k, here] = got[k * CAP : (k + 1) * CAP]
-                    weight = jnp.sum(
-                        jnp.where(chosen[k], row_of(gates, member, part, k), 0.0),
-                        axis=1,
-                        keepdims=True,
-                    )
-                    gcol[k, here] = jnp.broadcast_to(weight, (CAP, LENGTH))
-
-    @pl.loop(0, rows // 256)
-    def _(r):
-        here = pl.ds(pl.multiple_of(r * 256, 256), 256)
-        x = xs[e, here]
-        g_slot = gs[e, here].astype(F32)
-        weight = gcol[e, here][:, :1]
-        dy = (weight * (RESIDUAL * g_slot)).astype(BF16)
-        dys[here] = dy
-        a = dot(x, wg[0])
-        b = dot(x, wu[0])
-        sig = jax.nn.sigmoid(a)
-        swish = a * sig
-        m = (swish * b).astype(BF16)
-        ms[here] = m
-        y = dot(m, wd[0]).astype(BF16).astype(F32)
-        inner = RESIDUAL * jnp.sum(g_slot * y, axis=1, keepdims=True)
-        dcol[here] = jnp.broadcast_to(inner, (256, LENGTH))
-        gs[e, here] = (weight * y).astype(BF16)
-        dm = dot(dy, wd[0], ((1,), (1,)))
-        da = (dm * b * sig * (1.0 + a * (1.0 - sig))).astype(BF16)
-        db = (dm * swish).astype(BF16)
-        das[e, here] = da
-        dbs[e, here] = db
-        dh_slot = dot(da, wg[0], ((1,), (1,))) + dot(db, wu[0], ((1,), (1,)))
-        dhs[e, here] = dh_slot.astype(BF16)
-
-    @pl.loop(0, 8)
-    def _(member):
-        for part in range(2):
+            chosen, pick = picks(member, part)
+            here = all_slots_of(member, part)
+            got = dot(pick, gb[member, part * LENGTH : (part + 1) * LENGTH]).astype(BF16)
+            for k in range(HERE):
+                gs[k, here] = got[k * CAP : (k + 1) * CAP]
+                weight = jnp.sum(
+                    jnp.where(chosen[k], row_of(gates, member, part, k), 0.0),
+                    axis=1,
+                    keepdims=True,
+                )
+                gcol[k, here] = jnp.broadcast_to(weight, (CAP, LENGTH))
+
+    def gather_h(part):
+        @pl.loop(0, 8)
+        def _(member):
+            _, pick = picks(member, part)
+            here = all_slots_of(member, part)
+            got = dot(pick, hb[member, part * LENGTH : (part + 1) * LENGTH]).astype(BF16)
+            for k in range(HERE):
+                xs[k, here] = got[k * CAP : (k + 1) * CAP]
+
+    def work(part, e):
+        slot = lax.rem(e, 2)
+        for copy in fetch(e):
+            copy.wait()
+
+        @pl.loop(0, HALF // TILE)
+        def _(r):
+            near = pl.ds(pl.multiple_of(r * TILE, TILE), TILE)
+            here = pl.ds(pl.multiple_of(part * HALF + r * TILE, TILE), TILE)
+            x = xs[e, here]
+            g_slot = gs[e, here].astype(F32)
+            weight = gcol[e, here][:, :1]
+            dy = (weight * (RESIDUAL * g_slot)).astype(BF16)
+            gs[e, here] = dy
+            a = dot(x, wg[slot])
+            b = dot(x, wu[slot])
+            sig = jax.nn.sigmoid(a)
+            swish = a * sig
+            m = (swish * b).astype(BF16)
+            ms[e, here] = m
+            y = dot(m, wdb[e]).astype(BF16).astype(F32)
+            inner = RESIDUAL * jnp.sum(g_slot * y, axis=1, keepdims=True)
+            dcol[near] = jnp.broadcast_to(inner, (TILE, LENGTH))
+            gys[e, near] = (weight * y).astype(BF16)
+            dm = dot(dy, wdb[e], ((1,), (1,)))
+            da = (dm * b * sig * (1.0 + a * (1.0 - sig))).astype(BF16)
+            db = (dm * swish).astype(BF16)
+            das[e, here] = da
+            dbs[e, here] = db
+            dh_slot = dot(da, wg[slot], ((1,), (1,))) + dot(db, wu[slot], ((1,), (1,)))
+            dhs[e, near] = dh_slot.astype(BF16)
+
+        @pl.loop(0, 8)
+        def _(member):
             chosen = places == row_of(pos, member, part, e)
-            total = jnp.sum(
-                jnp.where(chosen, dcol[slots_of(member, part)], 0.0), axis=0, keepdims=True
+            qg[member, pl.ds(part * EXPERTS + first + e, 1), :] = jnp.sum(
+                jnp.where(chosen, dcol[slots_of(member)], 0.0), axis=0, keepdims=True
             )
-            qg[member, pl.ds(part * EXPERTS + first + e, 1), :] = total
-
-    @pl.loop(0, FE // 256)
-    def _(r):
-        here = pl.ds(pl.multiple_of(r * 256, 256), 256)
-        gd[0, here] = dot(ms[:, here], dys[...], ((0,), (0,))).astype(BF16)
-
-    @pl.when(e == HERE - 1)
-    def _():
-        def combine(source, where, part):
-            @pl.loop(0, 8)
-            def _(member):
-                _, pick = picks(member, part)
-                here = slots_of(member, part)
-                stack = jnp.concatenate([source[k, here] for k in range(HERE)])
-                hg[where, member, part * LENGTH : (part + 1) * LENGTH] = dot(
-                    pick, stack, ((0,), (0,))
-                ).astype(BF16)
-
-        lines = Lines(send_sems, recv_sems)
-        sums = [
-            group_scatter(lines, me, hg.at[0], dh, 0, LENGTH, *scratch[12:24]),
-            group_scatter(lines, me, hg.at[0], dh, LENGTH, LENGTH, *scratch[24:36]),
-            group_scatter(lines, me, qg, dg, 0, 2 * EXPERTS, *scratch[0:12]),
-        ]
-        for part in range(2):
-            combine(dhs, 0, part)
-            step(sums[part])
-        step(sums[2])
-        for part in range(2):
-            combine(gs, 1, part)
-        keep = pltpu.make_async_copy(hg.at[1], qy, local_sems.at[0])
-        keep.start()
-        for k in range(HERE):
-            slot = k % 2
-            copies = (
-                pltpu.make_async_copy(gg_part.at[slot], gg.at[k], local_sems.at[1 + slot]),
-                pltpu.make_async_copy(gu_part.at[slot], gu.at[k], local_sems.at[3 + slot]),
-            )
-            if k >= 2:
-                for copy in copies:
-                    copy.wait()
-
-            @pl.loop(0, D // 256)
-            def _(r, k=k, slot=slot):
-                here = pl.ds(pl.multiple_of(r * 256, 256), 256)
-                x = xs[k, :, here]
-                gg_part[slot, here] = dot(x, das[k], ((0,), (0,))).astype(BF16)
-                gu_part[slot, here] = dot(x, dbs[k], ((0,), (0,))).astype(BF16)
-
-            for copy in copies:
+
+        def refill():
+            for copy in fetch(lax.rem(e + 2, HERE)):
                 copy.start()
-            step(*((), sums, sums[:1], sums[1:])[k])
-        drive(*sums)
-        for slot in range(2):
-            pltpu.make_async_copy(gg_part.at[slot], gg.at[2 + slot], local_sems.at[1 + slot]).wait()
-            pltpu.make_async_copy(gu_part.at[slot], gu.at[2 + slot], local_sems.at[3 + slot]).wait()
-        keep.wait()
-        lines.drain()
-
-
-def experts(h, g, pos, gates, wg, wu, wd):
-    rows = 16 * CAP
+
+        if part == 0:
+            refill()
+        else:
+            pl.when(e < 2)(refill)
+
+    def combine(source, target, part):
+        @pl.loop(0, 8)
+        def _(member):
+            _, pick = picks(member, part)
+            here = slots_of(member)
+            stack = jnp.concatenate([source[k, here] for k in range(HERE)])
+            target[member, part * LENGTH : (part + 1) * LENGTH] = dot(
+                pick, stack, ((0,), (0,))
+            ).astype(BF16)
+
+    gather_g(0)
+    gather_g(1)
+    step(h1)
+    step(w3)
+    drive(h0)
+    gather_h(0)
+    drive(w3)
+    for copy in shared:
+        copy.wait_recv()
+
+    @pl.loop(0, HERE)
+    def _(e):
+        work(0, e)
+
+    drive(h1, weighed)
+    lines.drain()
+    gather_h(1)
+    sums = [
+        group_scatter(lines, me, gb, dh, part * LENGTH, LENGTH, *scratch[8 * part : 8 * part + 8])
+        for part in range(2)
+    ]
+    grad = group_scatter(lines, me, qg, dg, 0, 2 * EXPERTS, *scratch[16:24])
+    combine(dhs, gb, 0)
+    step(sums[0])
+    combine(gys, hb, 0)
+
+    @pl.loop(0, 2)
+    def _(e):
+        work(1, e)
+
+    step(sums[0])
+
+    @pl.loop(2, HERE)
+    def _(e):
+        work(1, e)
+
+    combine(dhs, gb, 1)
+    step(sums[1], grad)
+    step(sums[0])
+    combine(gys, hb, 1)
+    keep = pltpu.make_async_copy(hb, qy, local_sems.at[4])
+    keep.start()
+    handed = Lines(hand_send, hand_recv)
+    copies = []
+    for e in range(HERE):
+        for copy in copies:
+            copy.wait()
+        handed.drain()
+
+        @pl.loop(0, D // 256)
+        def _(r, e=e):
+            here = pl.ds(pl.multiple_of(r * 256, 256), 256)
+            x = xs[e, :, here]
+            gg_part[here] = dot(x, das[e], ((0,), (0,))).astype(BF16)
+            gu_part[here] = dot(x, dbs[e], ((0,), (0,))).astype(BF16)
+
+        @pl.loop(0, FE // 256)
+        def _(r, e=e):
+            here = pl.ds(pl.multiple_of(r * 256, 256), 256)
+            gd_part[here] = dot(ms[e, :, here], gs[e], ((0,), (0,))).astype(BF16)
+
+        copies = []
+        for i, (part, target) in enumerate(((gg_part, gg), (gu_part, gu), (gd_part, gd))):
+            size = part.shape[0] // 2
+            mine = pl.ds(pl.multiple_of(me.core * size, size), size)
+            theirs = pl.ds(pl.multiple_of((1 - me.core) * size, size), size)
+            copies.append(pltpu.make_async_copy(part.at[mine], target.at[0, e], local_sems.at[i]))
+            copies[i].start()
+            handed.send(part.at[theirs], target.at[1, e], me.sibling())
+        step(*(sums[:1], [sums[1], grad], [sums[1], grad], [*sums, grad])[e])
+    drive(sums[1], grad, sums[0])
+    for copy in copies:
+        copy.wait()
+    handed.drain()
+    for copy in handed.copies:
+        copy.wait_recv()
+    keep.wait()
+    lines.drain()
+
+
+def experts(h2, gates, g, pos, wg, wu, wd):
+    rows = 2 * HALF
     shape = jax.ShapeDtypeStruct
-    whole = pl.BlockSpec(memory_space=pltpu.VMEM)
-
-    def per_expert(a, b):
-        return pl.BlockSpec((1, a, b), lambda e: (e, 0, 0))
-
     return pl.pallas_call(
         experts_kernel,
         name="experts",
-        grid=(HERE,),
         out_shape=(
-            shape(h.shape, BF16),
-            shape(h.shape[1:], F32),
-            shape(gates.shape[1:], F32),
-            shape((HERE, D, FE), BF16),
-            shape((HERE, D, FE), BF16),
-            shape((HERE, FE, D), BF16),
+            shape(g.shape, BF16),
+            shape(h2.shape, F32),
+            shape(gates.shape, F32),
+            shape((2, HERE, D // 2, FE), BF16),
+            shape((2, HERE, D // 2, FE), BF16),
+            shape((2, HERE, FE // 2, D), BF16),
         ),
-        in_specs=anywhere(2)
-        + [whole] * 2
-        + [per_expert(D, FE), per_expert(D, FE), per_expert(FE, D)],
-        out_specs=anywhere(1) + [whole] * 2 + anywhere(2) + [per_expert(FE, D)],
+        in_specs=anywhere(3) + vmem(1) + anywhere(3),
+        out_specs=anywhere(1) + vmem(2) + anywhere(3),
         scratch_shapes=[
-            pltpu.VMEM((2,) + h.shape, BF16),
+            pltpu.VMEM(g.shape, BF16),
+            pltpu.VMEM(g.shape, BF16),
+            pltpu.VMEM(pos.shape, F32),
+            pltpu.VMEM((HERE, FE, D), BF16),
+            pltpu.VMEM((2, D, FE), BF16),
+            pltpu.VMEM((2, D, FE), BF16),
             pltpu.VMEM((HERE, rows, D), BF16),
             pltpu.VMEM((HERE, rows, D), BF16),
-            pltpu.VMEM((rows, D), BF16),
-            pltpu.VMEM((HERE, rows, D), BF16),
-            pltpu.VMEM((rows, FE), BF16),
             pltpu.VMEM((HERE, rows, FE), BF16),
             pltpu.VMEM((HERE, rows, FE), BF16),
+            pltpu.VMEM((HERE, rows, FE), BF16),
+            pltpu.VMEM((HERE, HALF, D), BF16),
+            pltpu.VMEM((HERE, HALF, D), BF16),
             pltpu.VMEM((HERE, rows, LENGTH), F32),
-            pltpu.VMEM((rows, LENGTH), F32),
-            pltpu.VMEM(gates.shape, F32),
-            pltpu.VMEM((2, D, FE), BF16),
-            pltpu.VMEM((2, D, FE), BF16),
-            pltpu.SemaphoreType.DMA((5,)),
+            pltpu.VMEM((HALF, LENGTH), F32),
+            pltpu.VMEM(pos.shape, F32),
+            pltpu.VMEM((D, FE), BF16),
+            pltpu.VMEM((D, FE), BF16),
+            pltpu.VMEM((FE, D), BF16),
+            pltpu.SemaphoreType.DMA((11,)),
         ]
-        + sems(36)
-        + scatter_scratch(gates.shape[1], gates.shape[2], F32)
+        + sems(64)
+        + sems(12)
         + scatter_scratch(LENGTH, D, BF16)
-        + scatter_scratch(LENGTH, D, BF16),
+        + scatter_scratch(LENGTH, D, BF16)
+        + scatter_scratch(gates.shape[0], gates.shape[1], F32),
         compiler_params=params(1, 60),
-    )(h, g, pos, gates, wg, wu, wd)
+    )(h2, gates, g, pos, wg, wu, wd)
 
 
 def on_device(
@@ -1188,7 +1263,7 @@
     rows = micro * LENGTH
     inputs = tokens.reshape(rows, D)
     upstream = cotangent.reshape(rows, D)
-    dense, gbuf, sbuf, wgb, wub, wdb, hbuf, gatebuf, q, k, v, p, o, y1, gates, cos, sin = front(
+    dense, gbuf, sbuf, wgb, wub, h2, q, k, v, p, o, y1, gates, cos, sin = front(
         inputs,
         segments[:, 0],
         routes.reshape(rows, TOPK),
@@ -1201,16 +1276,17 @@
         upstream,
         w_gate[0],
         w_up[0],
-        w_down[0],
     )
 
-    qy, dh, gate_grad, gg, gu, gd = experts(hbuf, gbuf, sbuf, gatebuf, wgb, wub, wdb)
-    grads, grad_tokens, result, tg, tu, td = retreat(
+    qy, dh, gate_grad, gg, gu, gd = experts(
+        h2, gates, gbuf, sbuf, wgb, wub, w_down[0]
+    )
+    grads, got, grad_tokens, result, tg, tu, td = retreat(
         inputs, cos, sin, gates, dense.reshape(D, WIDE), upstream, y1, q, k, v, p, o, dh, gate_grad,
         qy, gg, gu, gd,
     )
     gq, gk, gv, go, gsmall, grad_gate, grad_up, grad_down, grad_tokens, result = finish(
-        *settle(grads, tg, tu, td), grad_tokens, result
+        *settle(grads, got, tg, tu, td), grad_tokens, result
     )
     return (
         result.reshape(micro, 1, LENGTH, D),

time: 324 us -> 315 us (0.972)
  Pallas kernels: 318 us -> 310 us
    pallas_call x1, Pallas kernels: 105 us -> 79.4 us  [front(): pl.pallas_call(front_kernel, name='front', out_shape=(shape((2, 4, 4, 32,...]
    pallas_call x2, Pallas kernels: 151 us -> 171 us  [the longest x1 104 us: experts(): pl.pallas_call(experts_kernel, name='experts', out_shape=(shape(g.shape,...]
where the time goes in v4:
time: 315 us
  Pallas kernels  310 us (98%)
    pallas_call x1, Pallas kernels, experts(): pl.pallas_call(experts_kernel, name='experts', out_shape=(shape(g.shape,...  104 us
    pallas_call x1, Pallas kernels, front(): pl.pallas_call(front_kernel, name='front', out_shape=(shape((2, 4, 4, 32,...  79.4 us
    pallas_call x1, Pallas kernels, retreat(): pl.pallas_call(retreat_kernel, name='retreat', out_shape=(shape((2, 4, 4,...  67.2 us
    pallas_call x1, Pallas kernels, settle(): pl.pallas_call(settle_kernel, name='settle', out_shape=(shape((32, 1024),...  53.3 us
    pallas_call x1, Pallas kernels, finish(): pl.pallas_call(finish_kernel, name='finish', out_shape=tuple((jax.ShapeDt...  6.31 us

profile of v4, /device:TPU:1, one launch (start us, length us, event | category | flops | bytes accessed | tf_op | source)
XLA Modules:
  0.0 315.1 jit_solution(854011640094414221)
XLA Ops:
  0.6 1.2 maximum_convert_fusion.gains
  1.9 1.5 copy.29
  3.4 79.4 %front.1 = (bf16[2,4,4,32,3200]{4,3,2,1,0:T(8,128)(2,1)}, bf16[8,256,1024]{2,1,0:T(8,128)(2,1)}, f32[8,64,128]{2,1,0:T(8,128)}, bf16[4,1024,512]{2,1,0:T(8,128)(...) custom-call(bf16[256,1024]{1,0:T(8,128)(2,1)} %bitcast.27, ...), custom_call_target="tpu_custom_call" | custom-call | tf_op jit(solution)/shard_map/front/pallas_call | solution.py:595
  82.8 104.0 %experts.1 = (bf16[8,256,1024]{2,1,0:T(8,128)(2,1)}, f32[256,1024]{1,0:T(8,128)}, f32[64,128]{1,0:T(8,128)}, bf16[2,4,512,512]{3,2,1,0:T(8,128)(2,1)}, bf16[2,4,...) custom-call(bf16[256,1024]{1,0:T(8,128)(2,1)} %get-tuple-element.68.h2, ...), custom_call_target="tpu_custom_call" | custom-call | tf_op jit(solution)/shard_map/experts/pallas_call | solution.py:1202
  186.8 67.2 %retreat.1 = (bf16[2,4,4,32,3200]{4,3,2,1,0:T(8,128)(2,1)}, bf16[2,4,4,16,3200]{4,3,2,1,0:T(8,128)(2,1)}, f32[256,1024]{1,0:T(8,128)}, bf16[256,1024]{1,0:T(8,12...) custom-call(bf16[256,1024]{1,0:T(8,128)(2,1)} %bitcast.28, ...), custom_call_target="tpu_custom_call" | custom-call | tf_op jit(solution)/shard_map/retreat/pallas_call | solution.py:783
  254.0 53.3 %settle.1 = (f32[32,1024]{1,0:T(8,128)}, f32[32,512]{1,0:T(8,128)}, f32[32,512]{1,0:T(8,128)}, f32[32,1024]{1,0:T(8,128)}, f32[32,128]{1,0:T(8,128)}, /*index=5*...) custom-call(bf16[2,4,4,32,3200]{4,3,2,1,0:T(8,128)(2,1)} %get-tuple-element.79.grads, ...), custom_call_target="tpu_custom_call" | custom-call | tf_op jit(solution)/shard_map/settle/pallas_call | solution.py:915
  307.3 6.3 %finish.1 = (f32[32,1024]{1,0:T(8,128)}, f32[32,512]{1,0:T(8,128)}, f32[32,512]{1,0:T(8,128)}, f32[32,1024]{1,0:T(8,128)}, f32[32,128]{1,0:T(8,128)}, /*index=5*...) custom-call(f32[32,1024]{1,0:T(8,128)} %get-tuple-element.84.refs_0_, ...), custom_call_target="tpu_custom_call" | custom-call | tf_op jit(solution)/shard_map/finish/pallas_call | solution.py:956
  313.6 1.5 slice_reduce_fusion

commit v5 on v4

--- a/solution.py
+++ b/solution.py
@@ -682,7 +682,7 @@
     e2 = chain(tu, local[1], local[4], *scratch[9:15])
     e3 = chain(td, local[2], local[5], *scratch[15:21])
     ys = group_scatter(lines, me, qy, mixture, 0, 2 * LENGTH, *scratch[21:29])
-    step(e1, ys)
+    step(e1, e2, ys)
 
     small = dense[:, 3072:3200]
     gain_one, gain_two = gain_rows(small)
@@ -703,7 +703,7 @@
     dy = g[...].astype(F32) + scale * (dn - normed * jnp.mean(dn * normed, axis=1, keepdims=True))
     grad_tokens[...] = dy
     dz = (RESIDUAL * dy).astype(BF16)
-    step(e2)
+    step(e3)
     for t in range(4):
         here = slice(t * 256, t * 256 + 256)
         keep_rows(t, pl.ds(2048, 1024), dot(o[:, here], dz, ((0,), (0,))))
@@ -739,7 +739,7 @@
         def _(i):
             attend_back(i)
 
-        step(*((e3,), (ys, e2), (e1,), (ys, e3))[part])
+        step(*((), (ys, e2), (e1,), (ys, e3))[part])
 
     for t in range(4):
         here = slice(t * 256, t * 256 + 256)

time: 315 us -> 318 us (level)
    pallas_call x1, Pallas kernels: 67.2 us -> 70.4 us  [retreat(): pl.pallas_call(retreat_kernel, name='retreat', out_shape=(shape((2, 4, 4,...]
where the time goes in v5:
time: 318 us
  Pallas kernels  313 us (98%)
    pallas_call x1, Pallas kernels, experts(): pl.pallas_call(experts_kernel, name='experts', out_shape=(shape(g.shape,...  104 us
    pallas_call x1, Pallas kernels, front(): pl.pallas_call(front_kernel, name='front', out_shape=(shape((2, 4, 4, 32,...  79.4 us
    pallas_call x1, Pallas kernels, retreat(): pl.pallas_call(retreat_kernel, name='retreat', out_shape=(shape((2, 4, 4,...  70.4 us
    pallas_call x1, Pallas kernels, settle(): pl.pallas_call(settle_kernel, name='settle', out_shape=(shape((32, 1024),...  53.1 us

profile of v5, /device:TPU:1, one launch (start us, length us, event | category | flops | bytes accessed | tf_op | source)
XLA Modules:
  0.0 318.1 jit_solution(5391578794669494946)
XLA Ops:
  0.6 1.2 maximum_convert_fusion.gains
  1.9 1.5 copy.29
  3.4 79.4 %front.1 = (bf16[2,4,4,32,3200]{4,3,2,1,0:T(8,128)(2,1)}, bf16[8,256,1024]{2,1,0:T(8,128)(2,1)}, f32[8,64,128]{2,1,0:T(8,128)}, bf16[4,1024,512]{2,1,0:T(8,128)(...) custom-call(bf16[256,1024]{1,0:T(8,128)(2,1)} %bitcast.27, ...), custom_call_target="tpu_custom_call" | custom-call | tf_op jit(solution)/shard_map/front/pallas_call | solution.py:595
  82.8 104.0 %experts.1 = (bf16[8,256,1024]{2,1,0:T(8,128)(2,1)}, f32[256,1024]{1,0:T(8,128)}, f32[64,128]{1,0:T(8,128)}, bf16[2,4,512,512]{3,2,1,0:T(8,128)(2,1)}, bf16[2,4,...) custom-call(bf16[256,1024]{1,0:T(8,128)(2,1)} %get-tuple-element.68.h2, ...), custom_call_target="tpu_custom_call" | custom-call | tf_op jit(solution)/shard_map/experts/pallas_call | solution.py:1202
  186.8 70.4 %retreat.1 = (bf16[2,4,4,32,3200]{4,3,2,1,0:T(8,128)(2,1)}, bf16[2,4,4,16,3200]{4,3,2,1,0:T(8,128)(2,1)}, f32[256,1024]{1,0:T(8,128)}, bf16[256,1024]{1,0:T(8,12...) custom-call(bf16[256,1024]{1,0:T(8,128)(2,1)} %bitcast.28, ...), custom_call_target="tpu_custom_call" | custom-call | tf_op jit(solution)/shard_map/retreat/pallas_call | solution.py:783
  257.2 53.1 %settle.1 = (f32[32,1024]{1,0:T(8,128)}, f32[32,512]{1,0:T(8,128)}, f32[32,512]{1,0:T(8,128)}, f32[32,1024]{1,0:T(8,128)}, f32[32,128]{1,0:T(8,128)}, /*index=5*...) custom-call(bf16[2,4,4,32,3200]{4,3,2,1,0:T(8,128)(2,1)} %get-tuple-element.79.grads, ...), custom_call_target="tpu_custom_call" | custom-call | tf_op jit(solution)/shard_map/settle/pallas_call | solution.py:915
  310.3 6.3 %finish.1 = (f32[32,1024]{1,0:T(8,128)}, f32[32,512]{1,0:T(8,128)}, f32[32,512]{1,0:T(8,128)}, f32[32,1024]{1,0:T(8,128)}, f32[32,128]{1,0:T(8,128)}, /*index=5*...) custom-call(f32[32,1024]{1,0:T(8,128)} %get-tuple-element.84.refs_0_, ...), custom_call_target="tpu_custom_call" | custom-call | tf_op jit(solution)/shard_map/finish/pallas_call | solution.py:956
  316.6 1.5 slice_reduce_fusion
